TPU v7x, 32 devices: a whole 2x2x4 slice. The times are simulated.
32 devices in a mesh: dp: 8 (over y, x, core), blk: 4 (over z).
Axes of the slice: x: 2, y: 2, z: 4, core: 2. Of those that a mesh axis runs over, the one named last changes fastest.
Arguments:
- fields: float32 [8, 2048, 192], P('dp', 'blk'), may hold values from -6 to 6
- targets: float32 [8, 2048, 192], P('dp', 'blk'), may hold values from -6 to 6
- lead_time: float32 [8], P('dp'), may hold values from 0.25 to 3
- pixel_mask: int32 [8, 2048, 192], P('dp', 'blk'), may hold values from 0 to 1
- group_id: int32 [8], P('dp'), may hold values from 0 to 4, as said below
- slot_of: int32 [16], replicated, may hold values from 0 to 15, each once
- tiles: float32 [16, 1024, 1024], P('dp', 'blk'), may hold values from -0.1875 to 0.1875
- tiles_m: float32 [16, 1024, 1024], P('dp', 'blk'), may hold values from -7.6293945e-06 to 7.6293945e-06
- tiles_v: float32 [16, 1024, 1024], P('dp', 'blk'), may hold values from 1.214702e-12 to 4.858808e-12
- vectors: float32 [499, 1024], replicated
- vec_m: float32 [499, 1024], replicated, may hold values from -3.0517578e-05 to 3.0517578e-05
- vec_v: float32 [499, 1024], replicated, may hold values from 1.9666602e-11 to 7.7509554e-11
Outputs:
- loss: float32 [], replicated
- grad_norm: float32 [], replicated
- tiles_new: float32 [16, 1024, 1024], P('dp', 'blk')
- tiles_m_new: float32 [16, 1024, 1024], P('dp', 'blk')
- tiles_v_new: float32 [16, 1024, 1024], P('dp', 'blk')
- vectors_new: float32 [499, 1024], replicated
- vec_m_new: float32 [499, 1024], replicated
- vec_v_new: float32 [499, 1024], replicated
Inputs may be any that keep to these rules, and one draw needn't show every extreme that they name: `group_id`: every one of the 5 sources has at least one sample. `slot_of`: each slot number once.
All inputs are finite; a program needn't handle non-finite values.
Results may differ from a plain program's by a relative error of at most 0.0055.
Values may be sent and summed in bfloat16 or wider, within the bound.
No kernel may reach another device: no remote copies, remote signals or barrier semaphores. Data moves between devices by JAX's collectives and lax.ppermute only.
A program may use at most 832 MiB of HBM per device.

v0:
```python
import math

import jax
import jax.numpy as jnp
from jax import lax
from jax.sharding import PartitionSpec as P

D = 1024
HEADS = 16
HD = 64
FF = 4096
VARS = 48
PIX = 4
PROWS = 32
PCOLS = 64
GROUPS = 5
STEP = 10


HIGHEST = lax.Precision.HIGHEST
beta_one = 0.9
beta_two = 0.95
clip_norm = 0.02
rate_tiles = 0.01
rate_vectors = 0.1
decay_weight = 1e-05
adam_eps = 1e-08
norm_eps = 1e-05


def position_table(start, count):
    index = start + jnp.arange(count)
    patch_row = (index // PCOLS).astype(jnp.float32)
    patch_col = (index % PCOLS).astype(jnp.float32)
    quarter = D // 4
    omega = jnp.exp(-math.log(10000.0) * jnp.arange(quarter).astype(jnp.float32) / quarter)
    angle_row = patch_row[:, None] * omega[None, :]
    angle_col = patch_col[:, None] * omega[None, :]
    return jnp.concatenate(
        [jnp.sin(angle_row), jnp.cos(angle_row), jnp.sin(angle_col), jnp.cos(angle_col)], axis=1
    )


def latitude_table(start, count):
    index = start + jnp.arange(count)
    inner = jnp.arange(PIX) // 2
    lat_rows = 2 * (index // PCOLS)[:, None] + inner[None, :]
    total_rows = 2 * PROWS
    angle = (lat_rows.astype(jnp.float32) + 0.5) * (math.pi / total_rows) - math.pi / 2
    every = (jnp.arange(total_rows).astype(jnp.float32) + 0.5) * (
        math.pi / total_rows
    ) - math.pi / 2
    weight = jnp.cos(angle) / jnp.mean(jnp.cos(every))
    return jnp.tile(weight, (1, VARS))


def product(left, right):
    return jnp.dot(left, right, preferred_element_type=jnp.float32)


def product_left(left, right):
    return lax.dot_general(
        left, right, (((0,), (0,)), ((), ())), preferred_element_type=jnp.float32
    )


def product_right(left, right):
    return lax.dot_general(
        left, right, (((1,), (1,)), ((), ())), preferred_element_type=jnp.float32
    )


def layer_norm(values, gain, shift):
    center = values - jnp.mean(values, axis=-1, keepdims=True)
    inverse = lax.rsqrt(jnp.mean(center * center, axis=-1, keepdims=True) + norm_eps)
    normed = center * inverse
    return (normed * gain + shift, normed, inverse)


def norm_back(grad_out, normed, inverse, gain):
    scaled = grad_out * gain
    grad_in = inverse * (
        scaled
        - jnp.mean(scaled, axis=-1, keepdims=True)
        - normed * jnp.mean(scaled * normed, axis=-1, keepdims=True)
    )
    return (grad_in, jnp.sum(grad_out * normed, axis=0), jnp.sum(grad_out, axis=0))


def softmax_back(probs, grad_probs):
    return probs * (grad_probs - jnp.sum(probs * grad_probs, axis=-1, keepdims=True))


def gelu_slope(pre_act):
    return (
        0.5 * (1.0 + lax.erf(pre_act * 0.7071067811865476))
        + pre_act * jnp.exp(-0.5 * pre_act * pre_act) * 0.3989422804014327
    )


def attend_sample(items):
    queries, keys_seq, values_seq = items
    count = queries.shape[0]
    total = keys_seq.shape[0]
    score = jnp.einsum(
        "qhe,khe->hqk",
        queries.reshape(count, HEADS, HD),
        keys_seq.reshape(total, HEADS, HD),
        preferred_element_type=jnp.float32,
    ) * HD ** (-0.5)
    largest = jnp.max(score, axis=-1, keepdims=True)
    expo = jnp.exp(score - largest)
    summed = jnp.sum(expo, axis=-1, keepdims=True)
    probs_low = (expo / summed).astype(jnp.bfloat16)
    mixed = jnp.einsum(
        "hqk,khe->qhe",
        probs_low,
        values_seq.reshape(total, HEADS, HD),
        preferred_element_type=jnp.float32,
    )
    return (mixed.reshape(count, D), largest[..., 0] + jnp.log(summed[..., 0]))


def attend_back(items):
    queries, keys_seq, values_seq, grad_out, log_total = items
    count = queries.shape[0]
    total = keys_seq.shape[0]
    scale = HD ** (-0.5)
    query_heads = queries.reshape(count, HEADS, HD)
    key_heads = keys_seq.reshape(total, HEADS, HD)
    value_heads = values_seq.reshape(total, HEADS, HD)
    grad_heads = grad_out.reshape(count, HEADS, HD)
    score = (
        jnp.einsum("qhe,khe->hqk", query_heads, key_heads, preferred_element_type=jnp.float32)
        * scale
    )
    probs = jnp.exp(score - log_total[..., None])
    grad_probs = jnp.einsum(
        "qhe,khe->hqk", grad_heads, value_heads, preferred_element_type=jnp.float32
    )
    grad_score = softmax_back(probs, grad_probs).astype(jnp.bfloat16)
    grad_query = (
        jnp.einsum("hqk,khe->qhe", grad_score, key_heads, preferred_element_type=jnp.float32)
        * scale
    )
    grad_key = (
        jnp.einsum("hqk,qhe->khe", grad_score, query_heads, preferred_element_type=jnp.float32)
        * scale
    )
    grad_value = jnp.einsum(
        "hqk,qhe->khe", probs.astype(jnp.bfloat16), grad_heads, preferred_element_type=jnp.float32
    )
    return (grad_query.reshape(count, D), grad_key.reshape(total, D), grad_value.reshape(total, D))


def adam_update(weight, grad, first, second, rate):
    first = beta_one * first + (1.0 - beta_one) * grad
    second = beta_two * second + (1.0 - beta_two) * grad * grad
    first_hat = first / (1.0 - beta_one**STEP)
    second_hat = second / (1.0 - beta_two**STEP)
    weight = weight - rate * (first_hat / (jnp.sqrt(second_hat) + adam_eps) + decay_weight * weight)
    return (weight, first, second)


def shards(
    fields,
    targets,
    lead_time,
    pixel_mask,
    group_id,
    slot_of,
    tiles,
    tiles_m,
    tiles_v,
    vectors,
    vec_m,
    vec_v,
):
    sample_count, patch_count, pixel_width = fields.shape
    row_count = sample_count * patch_count
    folds = FF // D
    scale = HD ** (-0.5)
    low_type = jnp.bfloat16
    patch_start = lax.axis_index("blk") * patch_count
    slots_low = lax.all_gather(tiles.astype(low_type), "dp", axis=0, tiled=True)
    weights = jnp.take(lax.all_gather(slots_low, "blk", axis=1, tiled=True), slot_of, axis=0)
    mask_float = pixel_mask.astype(jnp.float32)
    var_local = jnp.sum(mask_float.reshape(sample_count, patch_count, VARS, PIX), axis=(0, 1, 3))
    group_hot = (group_id[:, None] == jnp.arange(GROUPS)[None, :]).astype(jnp.float32)
    var_total, group_total = lax.psum((var_local, jnp.sum(group_hot, axis=0)), ("dp", "blk"))
    group_total = group_total / lax.axis_size("blk")
    sample_weight = jnp.sum(group_total) / (
        GROUPS * jnp.sum(group_hot * group_total[None, :], axis=1)
    )
    count_pixels = VARS * jnp.repeat(var_total, PIX)
    offset = VARS * PIX
    embed_weight = vectors[:offset].reshape(VARS, PIX, D)
    embed_bias = vectors[offset : offset + VARS] + vectors[offset + VARS : offset + 2 * VARS]
    head_low = vectors[offset + 2 * VARS : 2 * offset + 2 * VARS].astype(low_type)
    extras = vectors[2 * offset + 2 * VARS :]
    field_four = fields.reshape(row_count, VARS, PIX)
    tokens_low = (
        jnp.einsum("rvk,vkd->rvd", field_four, embed_weight, precision=HIGHEST) + embed_bias[None]
    ).astype(low_type)
    flat_tokens = tokens_low.reshape(row_count * VARS, D)
    var_query_low = extras[0].astype(low_type)
    query_low = (
        (product(var_query_low[None, :], weights[0])[0] + extras[3])
        .astype(low_type)
        .reshape(HEADS, HD)
    )
    keys_agg = product(flat_tokens, weights[1]).astype(low_type).reshape(row_count, VARS, HEADS, HD)
    vals_agg = (
        (product(flat_tokens, weights[2]) + extras[4])
        .astype(low_type)
        .reshape(row_count, VARS, HEADS, HD)
    )
    score_agg = (
        jnp.einsum("he,rvhe->rhv", query_low, keys_agg, preferred_element_type=jnp.float32) * scale
    )
    probs_agg = jax.nn.softmax(score_agg, axis=-1)
    probs_agg_low = probs_agg.astype(low_type)
    out_agg_low = (
        jnp.einsum("rhv,rvhe->rhe", probs_agg_low, vals_agg, preferred_element_type=jnp.float32)
        .reshape(row_count, D)
        .astype(low_type)
    )
    agg = product(out_agg_low, weights[3]) + extras[5]
    lead_term = lead_time[:, None, None] * extras[1] + extras[2]
    hidden0 = (
        agg.reshape(sample_count, patch_count, D)
        + position_table(patch_start, patch_count)[None]
        + lead_term
    ).reshape(row_count, D)
    normed1_out, normed1, inverse1 = layer_norm(hidden0, extras[6], extras[7])
    normed1_low = normed1_out.astype(low_type)
    query_blk = (product(normed1_low, weights[4]) + extras[8]).astype(low_type)
    key_blk = product(normed1_low, weights[5]).astype(low_type)
    value_blk = (product(normed1_low, weights[6]) + extras[9]).astype(low_type)
    query_seq = query_blk.reshape(sample_count, patch_count, D)
    keys_all, values_all = (
        lax.all_gather(key_blk.reshape(sample_count, patch_count, D), "blk", axis=1, tiled=True),
        lax.all_gather(value_blk.reshape(sample_count, patch_count, D), "blk", axis=1, tiled=True),
    )
    attended, log_total = lax.map(attend_sample, (query_seq, keys_all, values_all))
    attended_low = attended.reshape(row_count, D).astype(low_type)
    hidden1 = hidden0 + product(attended_low, weights[7])
    normed2_out, normed2, inverse2 = layer_norm(hidden1, extras[10], extras[11])
    normed2_low = normed2_out.astype(low_type)
    weight_one = weights[8 : 8 + folds]
    weight_two = weights[8 + folds :].reshape(FF, D)
    pre_act = jnp.einsum(
        "rd,fde->rfe", normed2_low, weight_one, preferred_element_type=jnp.float32
    ).reshape(row_count, FF) + extras[15 : 15 + folds].reshape(FF)
    activ_low = jax.nn.gelu(pre_act, approximate=False).astype(low_type)
    hidden2 = hidden1 + product(activ_low, weight_two) + extras[12]
    normed3_out, normed3, inverse3 = layer_norm(hidden2, extras[13], extras[14])
    normed3_low = normed3_out.astype(low_type)
    predict = product_right(normed3_low, head_low)
    error = predict.reshape(sample_count, patch_count, pixel_width) - targets
    factor = (
        sample_weight[:, None, None]
        * mask_float
        * latitude_table(patch_start, patch_count)[None]
        / count_pixels
    )
    loss_local = jnp.sum(factor * error * error)
    grad_pred_low = (2.0 * factor * error).reshape(row_count, pixel_width).astype(low_type)
    grad_head = product_left(grad_pred_low, normed3_low)
    grad_h2, gain3, shift3 = norm_back(
        product(grad_pred_low, head_low), normed3, inverse3, extras[13]
    )
    grad_h2_low = grad_h2.astype(low_type)
    grad_w_two = product_left(activ_low, grad_h2_low).reshape(folds, D, D)
    bias2 = jnp.sum(grad_h2, axis=0)
    grad_pre = product_right(grad_h2_low, weight_two) * gelu_slope(pre_act)
    bias1 = jnp.sum(grad_pre, axis=0).reshape(folds, D)
    grad_pre_low = grad_pre.astype(low_type).reshape(row_count, folds, D)
    grad_w_one = jnp.einsum(
        "rd,rfe->fde", normed2_low, grad_pre_low, preferred_element_type=jnp.float32
    )
    grad_n2 = jnp.einsum(
        "rfe,fde->rd", grad_pre_low, weight_one, preferred_element_type=jnp.float32
    )
    grad_h1_norm, gain2, shift2 = norm_back(grad_n2, normed2, inverse2, extras[10])
    grad_h1 = grad_h2 + grad_h1_norm
    grad_h1_low = grad_h1.astype(low_type)
    grad_wo = product_left(attended_low, grad_h1_low)
    grad_attended = (
        product_right(grad_h1_low, weights[7])
        .astype(low_type)
        .reshape(sample_count, patch_count, D)
    )
    grad_query, grad_keys_all, grad_values_all = lax.map(
        attend_back, (query_seq, keys_all, values_all, grad_attended, log_total)
    )
    grad_keys, grad_values = (
        lax.psum_scatter(
            grad_keys_all.astype(jnp.bfloat16), "blk", scatter_dimension=1, tiled=True
        ).astype(jnp.float32),
        lax.psum_scatter(
            grad_values_all.astype(jnp.bfloat16), "blk", scatter_dimension=1, tiled=True
        ).astype(jnp.float32),
    )
    grad_query = grad_query.reshape(row_count, D)
    grad_values = grad_values.reshape(row_count, D)
    bias_q = jnp.sum(grad_query, axis=0)
    bias_v = jnp.sum(grad_values, axis=0)
    grad_query_low = grad_query.astype(low_type)
    grad_keys_low = grad_keys.reshape(row_count, D).astype(low_type)
    grad_values_low = grad_values.astype(low_type)
    grad_wq = product_left(normed1_low, grad_query_low)
    grad_wk = product_left(normed1_low, grad_keys_low)
    grad_wv = product_left(normed1_low, grad_values_low)
    grad_n1 = (
        product_right(grad_query_low, weights[4])
        + product_right(grad_keys_low, weights[5])
        + product_right(grad_values_low, weights[6])
    )
    grad_h0_norm, gain1, shift1 = norm_back(grad_n1, normed1, inverse1, extras[6])
    grad_h0 = grad_h1 + grad_h0_norm
    lead_weight_grad = jnp.sum(
        grad_h0.reshape(sample_count, patch_count, D) * lead_time[:, None, None], axis=(0, 1)
    )
    bias_oa = jnp.sum(grad_h0, axis=0)
    grad_h0_low = grad_h0.astype(low_type)
    grad_woa = product_left(out_agg_low, grad_h0_low)
    grad_out_agg = (
        product_right(grad_h0_low, weights[3]).astype(low_type).reshape(row_count, HEADS, HD)
    )
    grad_probs_agg = jnp.einsum(
        "rhe,rvhe->rhv", grad_out_agg, vals_agg, preferred_element_type=jnp.float32
    )
    grad_score_agg = softmax_back(probs_agg, grad_probs_agg).astype(low_type)
    grad_query_agg = (
        jnp.einsum("rhv,rvhe->he", grad_score_agg, keys_agg, preferred_element_type=jnp.float32)
        * scale
    ).reshape(D)
    grad_keys_agg = (
        (
            jnp.einsum(
                "rhv,he->rvhe", grad_score_agg, query_low, preferred_element_type=jnp.float32
            )
            * scale
        )
        .astype(low_type)
        .reshape(row_count * VARS, D)
    )
    grad_vals_full = jnp.einsum(
        "rhv,rhe->rvhe", probs_agg_low, grad_out_agg, preferred_element_type=jnp.float32
    ).reshape(row_count * VARS, D)
    bias_va = jnp.sum(grad_vals_full, axis=0)
    grad_vals_agg = grad_vals_full.astype(low_type)
    grad_wka = product_left(flat_tokens, grad_keys_agg)
    grad_wva = product_left(flat_tokens, grad_vals_agg)
    grad_tokens = (
        product_right(grad_keys_agg, weights[1]) + product_right(grad_vals_agg, weights[2])
    ).reshape(row_count, VARS, D)
    grad_embed = jnp.einsum("rvk,rvd->vkd", field_four, grad_tokens, precision=HIGHEST).reshape(
        VARS * PIX, D
    )
    grad_embed_bias = jnp.sum(grad_tokens, axis=0)
    grad_wqa = var_query_low.astype(jnp.float32)[:, None] * grad_query_agg[None, :]
    grad_var_query = jnp.dot(weights[0].astype(jnp.float32), grad_query_agg, precision=HIGHEST)
    extra_grads = jnp.stack(
        [
            grad_var_query,
            lead_weight_grad,
            bias_oa,
            grad_query_agg,
            bias_va,
            bias_oa,
            gain1,
            shift1,
            bias_q,
            bias_v,
            gain2,
            shift2,
            bias2,
            gain3,
            shift3,
        ]
    )
    vector_local = jnp.concatenate(
        [grad_embed, grad_embed_bias, grad_embed_bias, grad_head, extra_grads, bias1], axis=0
    )
    tile_grads = jnp.concatenate(
        [
            jnp.stack([grad_wqa, grad_wka, grad_wva, grad_woa, grad_wq, grad_wk, grad_wv, grad_wo]),
            grad_w_one,
            grad_w_two,
        ],
        axis=0,
    )
    vector_grads, loss = lax.psum((vector_local, loss_local), ("dp", "blk"))
    slot_grads = jnp.take(tile_grads, jnp.argsort(slot_of), axis=0)
    row_part = lax.psum_scatter(
        slot_grads.astype(jnp.bfloat16), "blk", scatter_dimension=1, tiled=True
    ).astype(jnp.float32)
    shard_grads = lax.psum_scatter(row_part, "dp", scatter_dimension=0, tiled=True)
    square_sum = lax.psum(jnp.sum(shard_grads * shard_grads), ("dp", "blk")) + jnp.sum(
        vector_grads * vector_grads
    )
    grad_norm = jnp.sqrt(square_sum)
    clip = jnp.minimum(1.0, clip_norm / (grad_norm + 1e-06))
    tiles_new, tiles_m_new, tiles_v_new = adam_update(
        tiles, shard_grads * clip, tiles_m, tiles_v, rate_tiles
    )
    vectors_new, vec_m_new, vec_v_new = adam_update(
        vectors, vector_grads * clip, vec_m, vec_v, rate_vectors
    )
    return (loss, grad_norm, tiles_new, tiles_m_new, tiles_v_new, vectors_new, vec_m_new, vec_v_new)


def solution(mesh):
    placed = (
        P("dp", "blk", None),
        P("dp", "blk", None),
        P("dp"),
        P("dp", "blk", None),
        P("dp"),
        P(),
        P("dp", "blk", None),
        P("dp", "blk", None),
        P("dp", "blk", None),
        P(),
        P(),
        P(),
    )
    return jax.shard_map(
        shards,
        mesh=mesh,
        in_specs=placed,
        out_specs=(
            P(),
            P(),
            P("dp", "blk", None),
            P("dp", "blk", None),
            P("dp", "blk", None),
            P(),
            P(),
            P(),
        ),
        check_vma=False,
    )
```

profile of v0, /device:TPU:0, one launch (start us, length us, event | category | flops | bytes accessed | tf_op | source)
XLA Modules:
  0.0 3424.9 jit_solution(1723547407171848067)
XLA Ops:
  10.2 57.4 %all-gather.7.cloned.1.call-done = bf16[16,256,1024]{2,1,0:T(8,128)(2,1)} async-done(((bf16[2,256,1024]{2,1,0:T(8,128)(2,1)}), bf16[16,256,1024]{2,1,0:T(8,128)(2,1)}) %all-gather.7.cloned.1.call-update) | async-done | bytes 8388624 | tf_op jit(solution)/shard_map/all_gather | solution.py:185
  70.9 84.9 %fusion.8 = bf16[512,48,1024]{2,0,1:T(8,128)(2,1)} fusion(f32[48,1024]{1,0:T(8,128)S(1)} %slice_add_fusion, f32[48,4,1024]{2,1,0:T(4,128)} %reshape.640, f32[512,48,4]{0,2,1:T(4,128)S(1)} %reshape.641), kind=kOutput, calls=%fused_computation.29 | convolution fusion | flops 1258291200 | bytes 51707904 | tf_op jit(solution)/shard_map/rvk,vkd->rvd/dot_general | solution.py:203
  155.8 44.9 %copy.77 = bf16[512,48,1024]{2,1,0:T(8,128)(2,1)} copy(bf16[512,48,1024]{2,0,1:T(8,128)(2,1)} %fusion.8) | data formatting | bytes 100663296 | tf_op jit(solution)/shard_map/convert_element_type | solution.py:204
  201.4 16.6 multiply_sine_fusion.1
  218.0 412.6 %all-gather.9.cloned.1.call-done = bf16[16,1024,1024]{2,1,0:T(8,128)(2,1)} async-done(((bf16[16,256,1024]{2,1,0:T(8,128)(2,1)}), bf16[16,1024,1024]{2,1,0:T(8,128)(2,1)}) %all-gather.9.cloned.1.call-update) | async-done | bytes 33554448 | tf_op jit(solution)/shard_map/all_gather | solution.py:186
  630.6 23.1 fusion.162
  679.7 23.0 maximum_select_fusion.1
  710.4 60.7 %convolution_convert_fusion = bf16[24576,1024]{1,0:T(8,128)(2,1)} fusion(bf16[24576,1024]{1,0:T(8,128)(2,1)} %bitcast.290, bf16[16,1024,1024]{2,1,0:T(8,128)(2,1)} %maximum_select_fusion.1), kind=kOutput, calls=%fused_computation.30 | convolution fusion | flops 51564773376 | bytes 102760448 | tf_op jit(solution)/shard_map/dot_general | solution.py:58
  771.1 126.1 %reshape.643 = bf16[512,48,16,64]{3,2,1,0:T(8,128)(2,1)} reshape(bf16[24576,1024]{1,0:T(8,128)(2,1)} %convolution_convert_fusion) | data formatting | bytes 100663296 | tf_op jit(solution)/shard_map/reshape | solution.py:212
  897.2 63.3 %multiply_reduce_fusion.3 = f32[16,512,48]{0,2,1:T(8,128)} fusion(f32[16,64]{1,0:T(8,128)S(1)} %fusion.109, bf16[512,48,16,64]{3,2,1,0:T(8,128)(2,1)} %reshape.643), kind=kLoop, calls=%fused_computation.12 | loop fusion | flops 75104256 | bytes 51908608 | tf_op jit(solution)/shard_map/he,rvhe->rhv/dot_general | solution.py:219
  960.5 18.8 convert_convert_fusion
  979.3 60.7 %add_convert_fusion = bf16[24576,1024]{1,0:T(8,128)(2,1)} fusion(bf16[24576,1024]{1,0:T(8,128)(2,1)} %bitcast.291, f32[1024]{0:T(1024)S(1)} %bitcast.350, bf16[16,1024,1024]{2,1,0:T(8,128)(2,1)} %maximum_select_fusion.1), kind=kOutput, calls=%fused_computation.17 | convolution fusion | flops 51589939200 | bytes 102764544 | tf_op jit(solution)/shard_map/dot_general | solution.py:58
  1040.0 126.1 %reshape.645 = bf16[512,48,16,64]{3,2,1,0:T(8,128)(2,1)} reshape(bf16[24576,1024]{1,0:T(8,128)(2,1)} %add_convert_fusion) | data formatting | bytes 100663296 | tf_op jit(solution)/shard_map/reshape | solution.py:216
  1166.1 64.6 %multiply_reduce_fusion.2 = bf16[512,16,64]{2,1,0:T(8,128)(2,1)S(1)} fusion(f32[512,16,48]{1,2,0:T(8,128)} %get-tuple-element.143, bf16[512,48,16,64]{3,2,1,0:T(8,128)(2,1)} %reshape.645), kind=kLoop, calls=%fused_computation.11 | loop fusion | flops 74973184 | bytes 52953088
  1243.4 43.8 %all-reduce.1 = (f32[48]{0:T(128)S(1)}, f32[5]{0:T(128)S(1)}) all-reduce(f32[48]{0:T(128)S(1)} %reduce_sum.351, f32[5]{0:T(128)S(1)} %compare_convert_fusion), channel_id=1, replica_groups=mesh['dp'=8,'blk'=4] {'dp','blk'}, use_global_device_ids=true, to_apply=%region_6.7 | all-reduce | flops 53 | bytes 424 | tf_op jit(solution)/shard_map/psum | solution.py:190
  1329.0 26.1 multiply_reduce_fusion.5
  1355.0 21.5 fusion.7
  1377.2 26.5 all-gather.11.cloned.1.call-done
  1410.2 25.6 fusion.87
  1460.5 26.0 fusion.167
  1503.1 13.4 fusion.163
  1539.8 25.8 fusion.56
  1565.7 48.1 %multiply_reduce_fusion.4 = (f32[16,512]{1,0:T(8,128)S(1)}, f32[16,512,2048]{2,1,0:T(8,128)}) fusion(f32[16,512,2048]{2,1,0:T(8,128)} %get-tuple-element.148, f32[16,512]{1,0:T(8,128)S(1)} %copy-done.26, bf16[512,16,64]{0,2,1:T(8,128)(2,1)S(1)} %bitcast.304, bf16[2048,16,64]{0,2,1:T(8,128)(2,1)} %bitcast.298), kind=kOutput, calls=%fused_computation.22 | convolution fusion | flops 2214584320 | bytes 139526144 | tf_op jit(solution)/shard_map/while/body/eval_jaxpr/qhe,khe->hqk/dot_general | solution.py:138
  1613.7 53.4 %multiply_convert_fusion.1 = bf16[16,512,2048]{2,1,0:T(8,128)(2,1)} fusion(f32[16,512,2048]{2,1,0:T(8,128)} %get-tuple-element.158, f32[16,512,2048]{2,1,0:T(8,128)} %get-tuple-element.148, f32[16,512]{1,0:T(8,128)S(1)} %get-tuple-element.157, f32[16,512]{1,0:T(8,128)S(1)} %copy-done.26), kind=kLoop, calls=%fused_computation.21 | loop fusion | flops 83886080 | bytes 167837696 | tf_op jit(solution)/shard_map/while/body/eval_jaxpr/convert_element_type | solution.py:141
  1667.1 18.5 multiply_convert_fusion.3
  1689.4 21.4 fusion.53
  1717.3 18.6 bitcast_convert_fusion.2
  1745.0 15.9 reduce-scatter.5.cloned.1.call-done
  1776.7 117.9 %bitcast_convert_fusion = (bf16[512,48,16,64]{3,2,1,0:T(8,128)(2,1)}, f32[512,16,48]{1,2,0:T(8,128)}) fusion(f32[512,16,64]{2,1,0:T(8,128)} %copy.137, f32[512,16,48]{1,2,0:T(8,128)} %get-tuple-element.143, bf16[512,48,16,64]{3,2,1,0:T(8,128)(2,1)} %reshape.645), kind=kLoop, calls=%fused_computation.8 | loop fusion | flops 125435904 | bytes 105906176 | tf_op jit(solution)/shard_map/convert_element_type | solution.py:353
  1894.6 19.7 multiply_convert_fusion.2
  1914.2 14.8 convert_bitcast_fusion
  1929.1 63.8 %multiply_reduce_fusion = f32[16,64]{1,0:T(8,128)S(1)} fusion(f32[16,512,48]{0,2,1:T(8,128)} %get-tuple-element.117, bf16[512,48,16,64]{3,2,1,0:T(8,128)(2,1)} %reshape.643), kind=kLoop, calls=%fused_computation.9 | loop fusion | flops 75496448 | bytes 51908608 | tf_op jit(solution)/shard_map/rhv,rvhe->he/dot_general | solution.py:336
  1992.9 65.4 %fusion.3 = bf16[512,48,16,64]{3,2,1,0:T(8,128)(2,1)} fusion(f32[16,64]{1,0:T(8,128)S(1)} %copy-done.49, f32[16,512,48]{0,2,1:T(8,128)} %get-tuple-element.116), kind=kLoop, calls=%fused_computation.14 | loop fusion | flops 75497472 | bytes 51908608 | tf_op jit(solution)/shard_map/convert_element_type | solution.py:346
  2058.4 129.6 %reshape.657 = bf16[24576,1024]{1,0:T(8,128)(2,1)} reshape(bf16[512,48,16,64]{3,2,1,0:T(8,128)(2,1)} %fusion.3) | data formatting | bytes 100663296 | tf_op jit(solution)/shard_map/reshape | solution.py:347
  2188.0 129.6 %convert_element_type.298 = bf16[24576,1024]{1,0:T(8,128)(2,1)} reshape(bf16[512,48,16,64]{3,2,1,0:T(8,128)(2,1)} %get-tuple-element.118) | data formatting | bytes 100663296 | tf_op jit(solution)/shard_map/convert_element_type | solution.py:353
  2319.1 60.4 %bitcast_dynamic-update-slice_fusion.7 = bf16[16,1024,1024]{1,2,0:T(8,128)(2,1)} fusion(bf16[16,1024,1024]{1,2,0:T(8,128)(2,1)} %multiply_dynamic-update-slice_fusion, bf16[24576,1024]{1,0:T(8,128)(2,1)} %bitcast.292, bf16[24576,1024]{1,0:T(8,128)(2,1)} %reshape.657), kind=kOutput, calls=%fused_computation.110 | convolution fusion | flops 51539607552 | bytes 104857600 | tf_op jit(solution)/shard_map/dot_general | solution.py:62
  2379.5 60.7 %bitcast_dynamic-update-slice_fusion.6 = bf16[16,1024,1024]{1,2,0:T(8,128)(2,1)} fusion(bf16[16,1024,1024]{1,2,0:T(8,128)(2,1)} %bitcast_dynamic-update-slice_fusion.7, bf16[24576,1024]{1,0:T(8,128)(2,1)} %bitcast.293, bf16[24576,1024]{1,0:T(8,128)(2,1)} %convert_element_type.298), kind=kOutput, calls=%fused_computation.109 | convolution fusion | flops 51539607552 | bytes 104857600 | tf_op jit(solution)/shard_map/dot_general | solution.py:62
  2467.4 22.4 fusion.161
  2516.2 22.9 fusion.6
  2544.8 65.3 %fusion.69 = f32[24576,1024]{1,0:T(8,128)} fusion(bf16[24576,1024]{1,0:T(8,128)(2,1)} %reshape.657, bf16[16,1024,1024]{2,1,0:T(8,128)(2,1)} %maximum_select_fusion.1), kind=kOutput, calls=%fused_computation.169 | convolution fusion | flops 51539607552 | bytes 153092096 | tf_op jit(solution)/shard_map/dot_general | solution.py:68
  2610.1 93.8 %convolution_add_fusion = f32[24576,1024]{1,0:T(8,128)} fusion(f32[24576,1024]{1,0:T(8,128)} %fusion.69, bf16[24576,1024]{1,0:T(8,128)(2,1)} %convert_element_type.298, bf16[16,1024,1024]{2,1,0:T(8,128)(2,1)} %maximum_select_fusion.1), kind=kOutput, calls=%fused_computation.27 | convolution fusion | flops 51564773376 | bytes 253755392 | tf_op jit(solution)/shard_map/dot_general | solution.py:68
  2703.9 31.3 reduce_sum.370
  2735.2 121.9 %fusion.88 = f32[48,4,1024]{2,1,0:T(4,128)S(1)} fusion(f32[512,48,4]{0,2,1:T(4,128)S(1)} %copy-done.24, f32[512,48,1024]{2,1,0:T(8,128)} %bitcast.72), kind=kOutput, calls=%fused_computation.189 | convolution fusion | flops 1207959552 | bytes 101842944 | tf_op jit(solution)/shard_map/rvk,rvd->vkd/dot_general | solution.py:359
  2857.6 58.8 %bitcast_reduce_fusion = f32[16,64]{1,0:T(8,128)S(1)} fusion(f32[512,16,64]{2,1,0:T(8,128)} %copy.137, f32[512,16,48]{1,2,0:T(8,128)} %get-tuple-element.143), kind=kLoop, calls=%fused_computation.7 | loop fusion | flops 50330624 | bytes 3674112 | tf_op jit(solution)/shard_map/reduce_sum | solution.py:352
  2927.4 164.5 %reduce-scatter.9.cloned.1.call-done = bf16[16,256,1024]{1,2,0:T(8,128)(2,1)} async-done(((bf16[16,1024,1024]{1,2,0:T(8,128)(2,1)}), bf16[16,256,1024]{1,2,0:T(8,128)(2,1)}) %reduce-scatter.9.cloned.1.call-update) | async-done | bytes 8388624 | tf_op jit(solution)/shard_map/reduce_scatter | solution.py:397
  3112.1 120.7 %all-reduce.4.cloned.1.call-done = f32[499,1024]{1,0:T(8,128)} async-done(((f32[499,1024]{1,0:T(8,128)}), f32[499,1024]{1,0:T(8,128)}) %all-reduce.4.cloned.1.call-update) | async-done | bytes 2043920 | tf_op jit(solution)/shard_map/psum | solution.py:395
  3235.6 116.0 %reduce-scatter.11.cloned.1.call-done = f32[2,256,1024]{1,2,0:T(8,128)} async-done(((f32[16,256,1024]{1,2,0:T(8,128)}), f32[2,256,1024]{1,2,0:T(8,128)}) %reduce-scatter.11.cloned.1.call-update) | async-done | bytes 2097168 | tf_op jit(solution)/shard_map/reduce_scatter | solution.py:400
  3354.3 39.6 %all-reduce = (f32[]{:T(128)}, f32[]{:T(128)}) all-reduce(f32[]{:T(128)} %get-tuple-element.136, f32[]{:T(128)} %multiply_reduce_fusion.10), channel_id=1, replica_groups=mesh['dp'=8,'blk'=4] {'dp','blk'}, use_global_device_ids=true, to_apply=%region_18.19 | all-reduce | flops 2 | bytes 16 | tf_op jit(solution)/shard_map/psum | solution.py:395
  (339 shorter events, 317.6 us)
Async XLA Ops:
  7.2 61.2 %copy-start.17 = (f32[499,1024]{1,0:T(8,128)S(1)}, f32[499,1024]{1,0:T(8,128)}, u32[]{:S(2)}) copy-start(f32[499,1024]{1,0:T(8,128)} %param.21) | copy-start | bytes 6131716
  7.2 62.5 %slice-start = ((f32[499,1024]{1,0:T(8,128)}), f32[192,1024]{1,0:T(8,128)S(1)}, s32[]{:S(2)}) async-start(f32[499,1024]{1,0:T(8,128)} %param.21), calls=%async_computation.13 | async-start | bytes 1572864 | tf_op jit(solution)/shard_map/slice | solution.py:197
  7.2 63.6 %copy-start.40 = (f32[1,512,192]{1,2,0:T(8,128)S(1)}, f32[1,512,192]{1,2,0:T(8,128)}, u32[]{:S(2)}) copy-start(f32[1,512,192]{1,2,0:T(8,128)} %param.12) | copy-start | bytes 1179652
  7.2 60.4 %all-gather.7.cloned.1.call-start = ((), (), s32[]{:S(2)}) async-start(), calls=%async_computation.4 | async-start | bytes 9437184 | tf_op jit(solution)/shard_map/all_gather | solution.py:185
  10.1 620.5 %all-gather.9.cloned.1.call-start = ((), (), s32[]{:S(2)}) async-start(), calls=%async_computation.5 | async-start | bytes 41943040 | tf_op jit(solution)/shard_map/all_gather | solution.py:186
  67.6 1254.8 %all-gather.13.cloned.1.call-start = ((), (), s32[]{:S(2)}) async-start(), calls=%async_computation.12 | async-start | bytes 5242880 | tf_op jit(solution)/shard_map/all_gather | solution.py:242
  70.9 84.9 %copy-start.23 = (f32[512,48,4]{0,2,1:T(4,128)}, f32[512,48,4]{0,2,1:T(4,128)S(1)}, u32[]{:S(2)}) copy-start(f32[512,48,4]{0,2,1:T(4,128)S(1)} %reshape.641) | copy-start | bytes 1179652
  155.8 45.6 %copy-start.95 = (s32[16]{0:T(128)S(1)}, s32[16]{0:T(128)}, u32[]{:S(2)}) copy-start(s32[16]{0:T(128)} %param.17) | copy-start | bytes 196
  771.1 126.1 %copy-start.56 = (f32[16,64]{1,0:T(8,128)S(1)}, f32[16,64]{1,0:T(8,128)}, u32[]{:S(2)}) copy-start(f32[16,64]{1,0:T(8,128)} %squeeze.58) | copy-start | bytes 12292
  897.2 63.3 %copy-start.48 = (f32[16,64]{1,0:T(8,128)}, f32[16,64]{1,0:T(8,128)S(1)}, u32[]{:S(2)}) copy-start(f32[16,64]{1,0:T(8,128)S(1)} %fusion.109) | copy-start | bytes 12292
  1166.1 66.3 %copy-start.88 = (f32[1,1024]{1,0:T(1,128)S(1)}, f32[1,1024]{1,0:T(1,128)}, u32[]{:S(2)}) copy-start(f32[1,1024]{1,0:T(1,128)} %get-tuple-element.130) | copy-start | bytes 12292
  1166.1 66.3 %copy-start.89 = (f32[1,1024]{1,0:T(1,128)S(1)}, f32[1,1024]{1,0:T(1,128)}, u32[]{:S(2)}) copy-start(f32[1,1024]{1,0:T(1,128)} %get-tuple-element.131) | copy-start | bytes 12292
  1236.3 199.5 %copy-start.2 = (f32[512,1024]{1,0:T(8,128)}, f32[512,1024]{1,0:T(8,128)S(1)}, u32[]{:S(2)}) copy-start(f32[512,1024]{1,0:T(8,128)S(1)} %get-tuple-element.146) | copy-start | bytes 6291460
  1236.3 52.9 %copy-start.76 = (s32[512]{0:T(512)S(1)}, s32[512]{0:T(512)}, u32[]{:S(2)}) copy-start(s32[512]{0:T(512)} %get-tuple-element.163) | copy-start | bytes 6148
  1242.3 161.4 %all-gather.11.cloned.1.call-start = ((), (), s32[]{:S(2)}) async-start(), calls=%async_computation.11 | async-start | bytes 5242880 | tf_op jit(solution)/shard_map/all_gather | solution.py:243
  1305.3 435.2 %reduce-scatter.7.cloned.1.call-start = ((), (), s32[]{:S(2)}) async-start(), calls=%async_computation.7 | async-start | bytes 5242880 | tf_op jit(solution)/shard_map/reduce_scatter | solution.py:301
  1310.9 44.2 %copy-start.4 = (bf16[512,1024]{0,1:T(8,128)(2,1)}, bf16[512,1024]{0,1:T(8,128)(2,1)S(1)}, u32[]{:S(2)}) copy-start(bf16[512,1024]{0,1:T(8,128)(2,1)S(1)} %copy.80) | copy-start | bytes 3145732
  1439.1 93.8 %copy-start.61 = (f32[512]{0:T(512)}, f32[512]{0:T(512)S(1)}, u32[]{:S(2)}) copy-start(f32[512]{0:T(512)S(1)} %broadcast_multiply_fusion.8) | copy-start | bytes 6148
  1439.5 93.4 %copy-start.74 = (f32[512]{0:T(512)}, f32[512]{0:T(512)S(1)}, u32[]{:S(2)}) copy-start(f32[512]{0:T(512)S(1)} %add_rsqrt_fusion.1) | copy-start | bytes 6148
  1460.5 26.9 copy-start.18
  1533.7 233.8 %copy-start = (f32[512,1024]{1,0:T(8,128)}, f32[512,1024]{1,0:T(8,128)S(1)}, u32[]{:S(2)}) copy-start(f32[512,1024]{1,0:T(8,128)S(1)} %multiply_add_fusion.2) | copy-start | bytes 6291460
  1565.6 195.3 %reduce-scatter.5.cloned.1.call-start = ((), (), s32[]{:S(2)}) async-start(), calls=%async_computation.6 | async-start | bytes 5242880 | tf_op jit(solution)/shard_map/reduce_scatter | solution.py:298
  1613.7 53.4 %copy-start.5 = (bf16[512,1024]{0,1:T(8,128)(2,1)S(1)}, bf16[512,1024]{0,1:T(8,128)(2,1)}, u32[]{:S(2)}) copy-start(bf16[512,1024]{0,1:T(8,128)(2,1)} %copy-done.4) | copy-start | bytes 3145732
  1685.6 1406.3 %reduce-scatter.9.cloned.1.call-start = ((), (), s32[]{:S(2)}) async-start(), calls=%async_computation.8 | async-start | bytes 41943040 | tf_op jit(solution)/shard_map/reduce_scatter | solution.py:397
  1929.1 63.9 %copy-start.49 = (f32[16,64]{1,0:T(8,128)S(1)}, f32[16,64]{1,0:T(8,128)}, u32[]{:S(2)}) copy-start(f32[16,64]{1,0:T(8,128)} %copy-done.48) | copy-start | bytes 12292
  1992.9 65.5 %copy-start.46 = (f32[16,64]{1,0:T(8,128)}, f32[16,64]{1,0:T(8,128)S(1)}, u32[]{:S(2)}) copy-start(f32[16,64]{1,0:T(8,128)S(1)} %broadcast_multiply_fusion) | copy-start | bytes 12292
  2187.9 129.6 %copy-start.73 = (f32[1024]{0:T(1024)S(1)}, f32[1024]{0:T(1024)}, u32[]{:S(2)}) copy-start(f32[1024]{0:T(1024)} %convert_element_type.273) | copy-start | bytes 12292
  2379.5 60.7 %copy-start.28 = (bf16[512,16,64]{0,2,1:T(8,128)(2,1)S(1)}, bf16[512,16,64]{0,2,1:T(8,128)(2,1)}, u32[]{:S(2)}) copy-start(bf16[512,16,64]{0,2,1:T(8,128)(2,1)} %copy-done.27) | copy-start | bytes 3145732
  2379.5 60.7 %copy-start.34 = (bf16[512,1024]{1,0:T(8,128)(2,1)S(1)}, bf16[512,1024]{1,0:T(8,128)(2,1)}, u32[]{:S(2)}) copy-start(bf16[512,1024]{1,0:T(8,128)(2,1)} %copy-done.33) | copy-start | bytes 3145732
  2539.2 693.7 %all-reduce.4.cloned.1.call-start = ((), (), s32[]{:S(2)}) async-start(), calls=%async_computation.10 | async-start | bytes 4128768 | tf_op jit(solution)/shard_map/psum | solution.py:395
  2703.9 31.3 copy-start.24
  2857.4 59.0 %copy-start.39 = (bf16[1,512,1024]{1,2,0:T(8,128)(2,1)S(1)}, bf16[1,512,1024]{1,2,0:T(8,128)(2,1)}, u32[]{:S(2)}) copy-start(bf16[1,512,1024]{1,2,0:T(8,128)(2,1)} %reduce-scatter.7.cloned.1.call-done) | copy-start | bytes 3145732
  2857.4 59.3 %copy-start.71 = (f32[1024,1]{0,1:T(1,128)S(1)}, f32[1024,1]{0,1:T(1,128)}, u32[]{:S(2)}) copy-start(f32[1024,1]{0,1:T(1,128)} %reshape.715) | copy-start | bytes 12292
  2857.4 62.6 %copy-start.25 = (f32[192,1024]{1,0:T(8,128)S(1)}, f32[192,1024]{1,0:T(8,128)}, u32[]{:S(2)}) copy-start(f32[192,1024]{1,0:T(8,128)} %fusion.170) | copy-start | bytes 2359300
  2857.5 62.6 %copy-start.51 = (f32[4,1024]{1,0:T(4,128)S(1)}, f32[4,1024]{1,0:T(4,128)}, u32[]{:S(2)}) copy-start(f32[4,1024]{1,0:T(4,128)} %reshape.660) | copy-start | bytes 49156
  2857.5 62.6 %copy-start.52 = (f32[1024]{0:T(1024)S(1)}, f32[1024]{0:T(1024)}, u32[]{:S(2)}) copy-start(f32[1024]{0:T(1024)} %get-tuple-element.93) | copy-start | bytes 12292
  2857.5 62.6 %copy-start.63 = (f32[1024]{0:T(1024)S(1)}, f32[1024]{0:T(1024)}, u32[]{:S(2)}) copy-start(f32[1024]{0:T(1024)} %get-tuple-element.94) | copy-start | bytes 12292
  2857.5 62.6 %copy-start.64 = (f32[1024]{0:T(1024)S(1)}, f32[1024]{0:T(1024)}, u32[]{:S(2)}) copy-start(f32[1024]{0:T(1024)} %get-tuple-element.107) | copy-start | bytes 12292
  2857.5 62.6 %copy-start.69 = (f32[1,1024]{1,0:T(1,128)S(1)}, f32[1,1024]{1,0:T(1,128)}, u32[]{:S(2)}) copy-start(f32[1,1024]{1,0:T(1,128)} %stack.75) | copy-start | bytes 12292
  2857.5 62.6 %copy-start.70 = (f32[1,1024]{1,0:T(1,128)S(1)}, f32[1,1024]{1,0:T(1,128)}, u32[]{:S(2)}) copy-start(f32[1,1024]{1,0:T(1,128)} %broadcast_in_dim_reshape.4) | copy-start | bytes 12292
  2857.5 62.6 %copy-start.77 = (f32[1024]{0:T(1024)S(1)}, f32[1024]{0:T(1024)}, u32[]{:S(2)}) copy-start(f32[1024]{0:T(1024)} %get-tuple-element.81) | copy-start | bytes 12292
  2857.5 62.6 %copy-start.78 = (f32[1024]{0:T(1024)S(1)}, f32[1024]{0:T(1024)}, u32[]{:S(2)}) copy-start(f32[1024]{0:T(1024)} %get-tuple-element.90) | copy-start | bytes 12292
  2857.5 62.6 %copy-start.79 = (f32[1024]{0:T(1024)S(1)}, f32[1024]{0:T(1024)}, u32[]{:S(2)}) copy-start(f32[1024]{0:T(1024)} %get-tuple-element.83) | copy-start | bytes 12292
  2857.6 62.6 %copy-start.80 = (f32[1024]{0:T(1024)S(1)}, f32[1024]{0:T(1024)}, u32[]{:S(2)}) copy-start(f32[1024]{0:T(1024)} %get-tuple-element.91) | copy-start | bytes 12292
  2857.6 62.6 %copy-start.81 = (f32[1024]{0:T(1024)S(1)}, f32[1024]{0:T(1024)}, u32[]{:S(2)}) copy-start(f32[1024]{0:T(1024)} %get-tuple-element.85) | copy-start | bytes 12292
  2857.6 62.6 %copy-start.82 = (f32[1024]{0:T(1024)S(1)}, f32[1024]{0:T(1024)}, u32[]{:S(2)}) copy-start(f32[1024]{0:T(1024)} %get-tuple-element.92) | copy-start | bytes 12292
  2927.3 424.2 %reduce-scatter.11.cloned.1.call-start = ((), (), s32[]{:S(2)}) async-start(), calls=%async_computation.9 | async-start | bytes 18874368 | tf_op jit(solution)/shard_map/reduce_scatter | solution.py:400
  3106.2 289.0 %copy-start.15 = (f32[2,256,1024]{1,2,0:T(8,128)S(1)}, f32[2,256,1024]{1,2,0:T(8,128)}, u32[]{:S(2)}) copy-start(f32[2,256,1024]{1,2,0:T(8,128)} %copy.102) | copy-start | bytes 6291460
  (60 other events, 562.0 us)
Sparse Core Ops, SparseCore 0:
  10.5 57.0 all-gather.6
  69.2 561.3 all-gather.8
  1242.4 79.9 all-gather.12
  1324.4 79.2 all-gather.10
  1565.7 75.3 reduce-scatter.6
  1685.7 75.2 reduce-scatter.4
  2539.3 552.5 reduce-scatter.8
  3098.7 134.1 all-reduce.3
  3236.4 115.0 reduce-scatter.10
where the time goes:
time: 3450 us; the launch traced here: 3420 us
  waiting for transfers between devices  925 us (27%)
  matrix products  911 us (26%)
  local copies, waits for them, and re-layouts  758 us (22%)
  other arithmetic  726 us (21%)
  blocking collectives  83.4 us (2%)
    all_gather x1, waiting for transfers between devices, shards(): lax.all_gather(slots_low, 'blk', axis=1, tiled=True)  413 us
    dot_general x9, matrix products, product_right(): lax.dot_general(left, right, (((1,), (1,)), ((), ())), preferred_element_...  197 us
    dot_general x10, matrix products, product(): return jnp.dot(left, right, preferred_element_type=jnp.float32)  170 us
    reduce_scatter x1, waiting for transfers between devices, shards(): lax.psum_scatter(slot_grads.astype(jnp.bfloat16), 'blk', scatter_dimensio...  165 us
    dot_general x9, matrix products, product_left(): lax.dot_general(left, right, (((0,), (0,)), ((), ())), preferred_element_...  142 us
    reshape x1, local copies, waits for them, and re-layouts, shards(): grad_keys_agg = (jnp.einsum('rhv,he->rvhe', grad_score_agg, query_low, pr...  130 us
    convert_element_type x1, local copies, waits for them, and re-layouts, shards(): grad_vals_agg = grad_vals_full.astype(low_type)  130 us
    reshape x1, local copies, waits for them, and re-layouts, shards(): vals_agg = (product(flat_tokens, weights[2]) + extras[4]).astype(low_type...  126 us
  transfers between devices with their start and end apart: 9, of which 8 were waited for; matrix products, arithmetic and copies ran while one was open for 24% of the time, Pallas kernels for 0%

commit v1 on v0

v1 whole, which is shorter than its diff:
```python
import functools
import math

import jax
import jax.numpy as jnp
from jax import lax
from jax.experimental import pallas as pl
from jax.experimental.pallas import tpu as pltpu
from jax.sharding import PartitionSpec as P

D = 1024
HEADS = 16
HD = 64
FF = 4096
VARS = 48
PIX = 4
TABLE = (PIX + 1) * VARS
norm_eps = 1e-05
f32 = jnp.float32
bf16 = jnp.bfloat16
NT = (((1,), (1,)), ((), ()))
NN = (((1,), (0,)), ((), ()))


def nt(a, b):
    return lax.dot_general(a, b, NT, preferred_element_type=f32)


def nn(a, b):
    return lax.dot_general(a, b, NN, preferred_element_type=f32)


def once(shape):
    zeros = (0,) * len(shape)
    return pl.BlockSpec(shape, lambda *_: zeros, pipeline_mode=pl.Buffered(1))


def cost(flops, moved, exps=0):
    return pl.CostEstimate(flops=flops, bytes_accessed=moved, transcendentals=exps)


def limit(mib):
    return pltpu.CompilerParams(vmem_limit_bytes=mib << 20)


def tile_spec(every, m):
    return pl.BlockSpec(every.shape[:2] + (1,) + every.shape[3:], lambda *_: (0, 0, m, 0, 0), pipeline_mode=pl.Buffered(1))


def tile_of(ref):
    return ref[...].reshape(D, D)


def attend_kernel(qb, q_ref, k_ref, v_ref, o_ref, l_ref):
    rows = q_ref.shape[0]
    lane = lax.broadcasted_iota(jnp.int32, (qb, 128), 1)
    pair = pl.program_id(0)

    @pl.when(pair == 0)
    def _():
        l_ref[...] = jnp.zeros_like(l_ref)

    def step(i, carry):
        at = pl.ds(pl.multiple_of(i * qb, qb), qb)
        q = q_ref[at, :]
        outs = []
        low = l_ref[at, :]
        for h in range(2):
            own = (lane < HD) if h == 0 else (lane >= HD)
            s = nt(jnp.where(own, q, jnp.zeros_like(q)), k_ref[...])
            m = jnp.max(s, axis=1, keepdims=True)
            e = jnp.exp(s - m)
            t = jnp.sum(e, axis=1, keepdims=True)
            outs.append(nn(e.astype(bf16), v_ref[...]) * (1.0 / t))
            low = jnp.where(lane == 2 * pair + h, m + jnp.log(t), low)
        o_ref[at, :] = jnp.where(lane < HD, outs[0], outs[1]).astype(bf16)
        l_ref[at, :] = low
        return carry

    lax.fori_loop(0, rows // qb, step, 0)


def attend(q, k, v, qb=256):
    rows, total = q.shape[0], k.shape[0]
    qb = min(qb, rows)
    pair_q = pl.BlockSpec((rows, 128), lambda p: (0, p))
    pair_k = pl.BlockSpec((total, 128), lambda p: (0, p))
    return pl.pallas_call(
        functools.partial(attend_kernel, qb),
        grid=(HEADS // 2,),
        in_specs=[pair_q, pair_k, pair_k],
        out_specs=[pair_q, pl.BlockSpec((rows, 128), lambda p: (0, 0))],
        out_shape=[jax.ShapeDtypeStruct((rows, D), bf16), jax.ShapeDtypeStruct((rows, 128), f32)],
        compiler_params=limit(48),
        cost_estimate=cost(16 * rows * total * D, 8 * total * D, HEADS * rows * total),
        name="attend",
    )(q, k, v)


def attend_back_kernel(qb, q_ref, k_ref, v_ref, o_ref, g_ref, l_ref, dq_ref, dk_ref, dv_ref, dk_acc, dv_acc):
    rows = q_ref.shape[0]
    lane = lax.broadcasted_iota(jnp.int32, (qb, 128), 1)
    pair = pl.program_id(0)
    dk_acc[...] = jnp.zeros_like(dk_acc)
    dv_acc[...] = jnp.zeros_like(dv_acc)

    def step(i, carry):
        at = pl.ds(pl.multiple_of(i * qb, qb), qb)
        q = q_ref[at, :]
        g = g_ref[at, :]
        qt = q.astype(f32).T.astype(bf16)
        gt = g.astype(f32).T.astype(bf16)
        prod = o_ref[at, :].astype(f32) * g.astype(f32)
        low = l_ref[at, :]
        dqs = []
        for h in range(2):
            own = (lane < HD) if h == 0 else (lane >= HD)
            lse = jnp.sum(jnp.where(lane == 2 * pair + h, low, 0.0), axis=1, keepdims=True)
            delta = jnp.sum(jnp.where(own, prod, 0.0), axis=1, keepdims=True)
            s = nt(jnp.where(own, q, jnp.zeros_like(q)), k_ref[...])
            p = jnp.exp(s - lse)
            dp = nt(jnp.where(own, g, jnp.zeros_like(g)), v_ref[...])
            ds = (p * (dp - delta)).astype(bf16)
            part = pl.ds(h * HD, HD)
            dv_acc[part, :] += nn(gt[h * HD : (h + 1) * HD, :], p.astype(bf16))
            dk_acc[part, :] += nn(qt[h * HD : (h + 1) * HD, :], ds)
            dqs.append(nn(ds, k_ref[...]))
        dq_ref[at, :] = (jnp.where(lane < HD, dqs[0], dqs[1]) * (HD**-0.5)).astype(bf16)
        return carry

    lax.fori_loop(0, rows // qb, step, 0)
    dk_ref[...] = dk_acc[...].T.astype(bf16)
    dv_ref[...] = dv_acc[...].T.astype(bf16)


def attend_back(q, k, v, o, g, l, qb=512):
    rows, total = q.shape[0], k.shape[0]
    qb = min(qb, rows)
    pair_q = pl.BlockSpec((rows, 128), lambda p: (0, p))
    pair_k = pl.BlockSpec((total, 128), lambda p: (0, p))
    return pl.pallas_call(
        functools.partial(attend_back_kernel, qb),
        grid=(HEADS // 2,),
        in_specs=[pair_q, pair_k, pair_k, pair_q, pair_q, pl.BlockSpec((rows, 128), lambda p: (0, 0))],
        out_specs=[pair_q, pair_k, pair_k],
        out_shape=[
            jax.ShapeDtypeStruct((rows, D), bf16),
            jax.ShapeDtypeStruct((total, D), bf16),
            jax.ShapeDtypeStruct((total, D), bf16),
        ],
        scratch_shapes=[pltpu.VMEM((128, total), f32), pltpu.VMEM((128, total), f32)],
        compiler_params=limit(48),
        cost_estimate=cost(40 * rows * total * D, 16 * total * D, HEADS * rows * total),
        name="attend_back",
    )(q, k, v, o, g, l)


def fold_kernel(w0_ref, w1_ref, w2_ref, hi_ref, lo_ref, vec_ref, coef_ref, low_ref, lowt_ref, key_ref, query_ref):
    head = lax.broadcasted_iota(jnp.int32, (128, D), 0)
    column = lax.broadcasted_iota(jnp.int32, (128, D), 1)
    query = (nn(vec_ref[...].astype(bf16), tile_of(w0_ref))[0:1, :] + vec_ref[1:2, :]).astype(bf16)
    query_ref[...] = jnp.broadcast_to(query.astype(f32), query_ref.shape)
    spread = jnp.where(column // HD == head, query.astype(f32), 0.0).astype(bf16)
    key = nt(spread, tile_of(w1_ref)) * (HD**-0.5)
    key_ref[...] = key[:HEADS]
    key_hi = key.astype(bf16)
    key_lo = (key - key_hi.astype(f32)).astype(bf16)
    coef_ref[...] = nt(hi_ref[...], key_hi) + nt(lo_ref[...], key_hi) + nt(hi_ref[...], key_lo)
    value = tile_of(w2_ref)
    val = nn(hi_ref[...], value) + nn(lo_ref[...], value)
    row = lax.broadcasted_iota(jnp.int32, (TABLE, D), 0)
    val = jnp.where(row >= PIX * VARS, val + vec_ref[2:3, :], val)
    low_ref[...] = val.astype(bf16)
    lowt_ref[...] = val.T.astype(bf16)


def fold(every, hi, lo, vecs):
    return pl.pallas_call(
        fold_kernel,
        grid=(1,),
        in_specs=[*(tile_spec(every, m) for m in range(3)), once((TABLE, D)), once((TABLE, D)), once((8, D))],
        out_specs=[once(s) for s in ((TABLE, 128), (TABLE, D), (D, TABLE), (HEADS, D), (8, D))],
        out_shape=[
            jax.ShapeDtypeStruct((TABLE, 128), f32),
            jax.ShapeDtypeStruct((TABLE, D), bf16),
            jax.ShapeDtypeStruct((D, TABLE), bf16),
            jax.ShapeDtypeStruct((HEADS, D), f32),
            jax.ShapeDtypeStruct((8, D), f32),
        ],
        compiler_params=limit(40),
        cost_estimate=cost(6 * TABLE * D * D, 6 * D * D),
        name="fold",
    )(every, every, every, hi, lo, vecs)


def mix_probs(f, coef_ref, h):
    part = lambda k: coef_ref[k * VARS : (k + 1) * VARS, h : h + 1]
    s = part(PIX)
    for k in range(PIX):
        s = s + part(k) * f[k]
    e = jnp.exp(s - jnp.max(s, axis=0, keepdims=True))
    return e * (1.0 / jnp.sum(e, axis=0, keepdims=True))


def mix_kernel(f_ref, coef_ref, tt_ref, o_ref):
    f = [f_ref[0, k].astype(f32) for k in range(PIX)]

    def one(h):
        pa = mix_probs(f, coef_ref, h)
        pf = jnp.concatenate([pa * x for x in f] + [pa], axis=0).astype(bf16)
        return nn(tt_ref[h * HD : (h + 1) * HD, :], pf)

    for p in range(HEADS // 2):
        both = jnp.concatenate([one(2 * p), one(2 * p + 1)], axis=0)
        o_ref[:, p * 128 : (p + 1) * 128] = both.T.astype(bf16)


def mix(fields, coef, tt):
    nb, _, _, count = fields.shape
    return pl.pallas_call(
        mix_kernel,
        grid=(nb,),
        in_specs=[
            pl.BlockSpec((1, PIX, VARS, count), lambda b: (b, 0, 0, 0)),
            once((TABLE, 128)),
            once((D, TABLE)),
        ],
        out_specs=pl.BlockSpec((count, D), lambda b: (b, 0)),
        out_shape=jax.ShapeDtypeStruct((nb * count, D), bf16),
        compiler_params=limit(40),
        cost_estimate=cost(8 * nb * count * TABLE * D, 4 * nb * count * D, nb * count * VARS * HEADS),
        name="mix",
    )(fields, coef, tt)


def mix_back_kernel(side_ref, f_ref, coef_ref, t_ref, g_ref, rest_ref, mine_ref, other_ref, dt_ref, dc_ref):
    @pl.when(pl.program_id(0) == 0)
    def _():
        dc_ref[...] = jnp.zeros_like(dc_ref)
        dt_ref[...] = jnp.zeros_like(dt_ref)

    lane = lax.broadcasted_iota(jnp.int32, (VARS, 128), 1)
    f = [f_ref[0, k].astype(f32) for k in range(PIX)]
    for h in range(HEADS):
        pair = slice(h // 2 * 128, h // 2 * 128 + 128)
        own = (lane[:1] < HD) if h % 2 == 0 else (lane[:1] >= HD)
        pa = mix_probs(f, coef_ref, h)
        pf = jnp.concatenate([pa * x for x in f] + [pa], axis=0).astype(bf16)
        g = jnp.where(own, g_ref[:, pair], jnp.zeros((), bf16))
        dpf = nt(t_ref[:, pair], g)
        dpa = dpf[PIX * VARS :]
        for k in range(PIX):
            dpa = dpa + dpf[k * VARS : (k + 1) * VARS] * f[k]
        ds = pa * (dpa - jnp.sum(pa * dpa, axis=0, keepdims=True))
        for k in range(PIX + 1):
            w = ds * f[k] if k < PIX else ds
            dc_ref[k * VARS : (k + 1) * VARS, :] += jnp.where(lane == h, jnp.sum(w, axis=1, keepdims=True), 0.0)
        dt_ref[:, pair] += nn(pf, g)

    @pl.when(pl.program_id(0) == pl.num_programs(0) - 1)
    def _():
        dct = jnp.concatenate([dc_ref[...].T[:HEADS], jnp.zeros((HEADS, D // 2 - TABLE), f32)], axis=1)
        half = D // 2
        for at, left, right in (
            (0, dt_ref[:, :half], dt_ref[:, half:]),
            (TABLE, dct, jnp.zeros_like(dct)),
            (TABLE + HEADS, rest_ref[:, :half], rest_ref[:, half:]),
        ):
            rows = slice(at, at + left.shape[0])
            first = side_ref[0] == 0
            mine_ref[rows, :] = jnp.where(first, left, right)
            other_ref[rows, :] = jnp.where(first, right, left).astype(bf16)


def mix_back(side, fields, coef, t, g, rest):
    nb, _, _, count = fields.shape
    shape = (TABLE + HEADS + rest.shape[0], D // 2)
    whole = lambda s: pl.BlockSpec(s, lambda b: (0,) * len(s))
    return pl.pallas_call(
        mix_back_kernel,
        grid=(nb,),
        in_specs=[
            pl.BlockSpec(memory_space=pltpu.SMEM),
            pl.BlockSpec((1, PIX, VARS, count), lambda b: (b, 0, 0, 0)),
            once((TABLE, 128)),
            once((TABLE, D)),
            pl.BlockSpec((count, D), lambda b: (b, 0)),
            once(rest.shape),
        ],
        out_specs=[whole(shape), whole(shape)],
        out_shape=[jax.ShapeDtypeStruct(shape, f32), jax.ShapeDtypeStruct(shape, bf16)],
        scratch_shapes=[pltpu.VMEM((TABLE, D), f32), pltpu.VMEM((TABLE, 128), f32)],
        compiler_params=limit(40),
        cost_estimate=cost(16 * nb * count * TABLE * D, 4 * nb * count * D, nb * count * VARS * HEADS),
        name="mix_back",
    )(side, fields, coef, t, g, rest)


def front_kernel(m_ref, w3_ref, w4_ref, w5_ref, w6_ref, row_ref, col_ref, vec_ref, h_ref, a_ref, q_ref, k_ref, v_ref):
    per = row_ref.shape[1]
    h = nn(m_ref[...], tile_of(w3_ref))
    h = h + jnp.concatenate([col_ref[...] + row_ref[0, i : i + 1, :] for i in range(per)], axis=0)
    h_ref[...] = h
    center = h - jnp.mean(h, axis=-1, keepdims=True)
    inverse = lax.rsqrt(jnp.mean(center * center, axis=-1, keepdims=True) + norm_eps)
    a = (center * inverse * vec_ref[0:1, :] + vec_ref[1:2, :]).astype(bf16)
    a_ref[...] = a
    k_ref[...] = nn(a, tile_of(w5_ref)).astype(bf16)
    v_ref[...] = (nn(a, tile_of(w6_ref)) + vec_ref[3:4, :]).astype(bf16)

    @pl.when(pl.program_id(0) == 0)
    def _():
        q_ref[...] = ((nn(a, tile_of(w4_ref)) + vec_ref[2:3, :]) * (HD**-0.5)).astype(bf16)


def front(mixed, every, row, col, vecs, blocks):
    total = mixed.shape[0]
    count = total // blocks
    per = row.shape[0] // blocks
    block = pl.BlockSpec((count, D), lambda b: (b, 0))
    return pl.pallas_call(
        front_kernel,
        grid=(blocks,),
        in_specs=[
            block,
            *(tile_spec(every, m) for m in range(3, 7)),
            pl.BlockSpec((1, per, D), lambda b: (b, 0, 0)),
            once(col.shape),
            once(vecs.shape),
        ],
        out_specs=[block, block, pl.BlockSpec((count, D), lambda b: (0, 0)), block, block],
        out_shape=[
            jax.ShapeDtypeStruct((total, D), f32),
            jax.ShapeDtypeStruct((total, D), bf16),
            jax.ShapeDtypeStruct((count, D), bf16),
            jax.ShapeDtypeStruct((total, D), bf16),
            jax.ShapeDtypeStruct((total, D), bf16),
        ],
        compiler_params=limit(52),
        cost_estimate=cost(6 * total * D * D, 16 * total * D),
        name="front",
    )(mixed, *[every] * 4, row.reshape(blocks, per, D), col, vecs)


def back_kernel(dq_ref, dk_ref, dv_ref, h_ref, dh_ref, w3_ref, w4_ref, w5_ref, w6_ref, vec_ref, g_ref, gm_ref, sum_ref, acc):
    first = pl.program_id(0) == 0
    acc[...] = nt(dk_ref[...], tile_of(w5_ref)) + nt(dv_ref[...], tile_of(w6_ref))

    @pl.when(first)
    def _():
        sum_ref[...] = jnp.zeros_like(sum_ref)
        acc[...] += nt(dq_ref[...], tile_of(w4_ref))
        sum_ref[4:5, :] = jnp.sum(dq_ref[...].astype(f32), axis=0, keepdims=True)

    h = h_ref[...]
    center = h - jnp.mean(h, axis=-1, keepdims=True)
    inverse = lax.rsqrt(jnp.mean(center * center, axis=-1, keepdims=True) + norm_eps)
    normed = center * inverse
    grad = acc[...]
    sum_ref[1:2, :] += jnp.sum(grad * normed, axis=0, keepdims=True)
    sum_ref[2:3, :] += jnp.sum(grad, axis=0, keepdims=True)
    sum_ref[3:4, :] += jnp.sum(dv_ref[...].astype(f32), axis=0, keepdims=True)
    scaled = grad * vec_ref[0:1, :]
    out = inverse * (
        scaled
        - jnp.mean(scaled, axis=-1, keepdims=True)
        - normed * jnp.mean(scaled * normed, axis=-1, keepdims=True)
    )
    acc[...] = out

    @pl.when(first)
    def _():
        acc[...] += dh_ref[...]

    out = acc[...]
    sum_ref[0:1, :] += jnp.sum(out, axis=0, keepdims=True)
    low = out.astype(bf16)
    g_ref[...] = low
    gm_ref[...] = nt(low, tile_of(w3_ref)).astype(bf16)


def back(dq, dk, dv, h, dh, every, vecs, blocks):
    total = dk.shape[0]
    count = total // blocks
    block = pl.BlockSpec((count, D), lambda b: (b, 0))
    return pl.pallas_call(
        back_kernel,
        grid=(blocks,),
        in_specs=[
            once((count, D)),
            block,
            block,
            block,
            once((count, D)),
            *(tile_spec(every, m) for m in range(3, 7)),
            once(vecs.shape),
        ],
        out_specs=[block, block, pl.BlockSpec((8, D), lambda b: (0, 0))],
        out_shape=[
            jax.ShapeDtypeStruct((total, D), bf16),
            jax.ShapeDtypeStruct((total, D), bf16),
            jax.ShapeDtypeStruct((8, D), f32),
        ],
        scratch_shapes=[pltpu.VMEM((count, D), f32)],
        compiler_params=limit(52),
        cost_estimate=cost(7 * total * D * D, 16 * total * D),
        name="back",
    )(dq, dk, dv, h, dh, *[every] * 4, vecs)


def choose_kernel(first, slot_ref, p_ref, wait_ref, out_ref):
    for m in range(out_ref.shape[0]):
        out_ref[m] = p_ref[slot_ref[first + m]]


def choose(slot_of, pieces, first, count, wait):
    shape = (count,) + pieces.shape[1:]
    whole = lambda s: pl.BlockSpec(s, lambda i, at: (0, 0, 0))
    return pl.pallas_call(
        functools.partial(choose_kernel, first),
        grid_spec=pltpu.PrefetchScalarGridSpec(
            num_scalar_prefetch=1,
            grid=(1,),
            in_specs=[whole(pieces.shape), pl.BlockSpec(memory_space=pl.ANY)],
            out_specs=whole(shape),
        ),
        out_shape=jax.ShapeDtypeStruct(shape, pieces.dtype),
        compiler_params=limit(32),
        cost_estimate=cost(0, 4 * pieces.size),
        name="choose",
    )(slot_of, pieces, wait)


def finish_kernel(plan, slot_ref, *refs):
    ins, out, square = refs[:-2], refs[-2], refs[-1]
    half = out.shape[2]
    for m in range(3):
        out[slot_ref[m]] = jnp.zeros_like(out[0])
    total = jnp.zeros(out.shape[1:], f32)
    ins = list(ins)
    for per, tiles in plan:
        job, ins = ins[:per], ins[per:]
        for m, index, col in tiles:
            parts = [r[index, :, col * half : (col + 1) * half].astype(f32) for r in job]
            value = sum(parts[1:], parts[0])
            out[slot_ref[m]] = value.astype(out.dtype)
            total = total + value * value
    square[...] = jnp.sum(total.reshape(total.shape[0] // 8, 8, half), axis=0)


def finish(slot_of, plan, jobs):
    arrays = [a for job in jobs for a in job]
    plan = tuple((len(job), tiles) for job, tiles in zip(jobs, plan))
    rows, half = arrays[0].shape[1], D // 2
    whole = lambda s: pl.BlockSpec(s, lambda i, at: (0,) * len(s))
    n = slot_of.shape[0]
    return pl.pallas_call(
        functools.partial(finish_kernel, plan),
        grid_spec=pltpu.PrefetchScalarGridSpec(
            num_scalar_prefetch=1,
            grid=(1,),
            in_specs=[whole(a.shape) for a in arrays],
            out_specs=[whole((n, rows, half)), whole((8, half))],
        ),
        out_shape=[jax.ShapeDtypeStruct((n, rows, half), bf16), jax.ShapeDtypeStruct((8, half), f32)],
        compiler_params=limit(48),
        cost_estimate=cost(0, 3 * 4 * n * rows * half),
        name="finish",
    )(slot_of, *arrays)


beta_one = 0.9
beta_two = 0.95
rate_tiles = 0.01
rate_vectors = 0.1
decay_weight = 1e-05
adam_eps = 1e-08
STEP = 10
clip_norm = 0.02


def adam_update(weight, grad, first, second, rate):
    first = beta_one * first + (1.0 - beta_one) * grad
    second = beta_two * second + (1.0 - beta_two) * grad * grad
    first_hat = first / (1.0 - beta_one**STEP)
    second_hat = second / (1.0 - beta_two**STEP)
    weight = weight - rate * (first_hat / (jnp.sqrt(second_hat) + adam_eps) + decay_weight * weight)
    return (weight, first, second)


def tail_kernel(square_ref, w0_ref, w1_ref, w2_ref, hi_ref, lo_ref, gram_ref, key_ref, query_ref, vec_ref, late_ref,
                p_ref, m_ref, v_ref, clip_ref, gkey_ref, agg_ref, p_new, m_new, v_new, ge, extra):
    head = lax.broadcasted_iota(jnp.int32, (HEADS, D), 0)
    column = lax.broadcasted_iota(jnp.int32, (HEADS, D), 1)

    def parts(a):
        high = a.astype(bf16)
        return high, (a - high.astype(f32)).astype(bf16)

    def tn(a, b):
        return lax.dot_general(a, b, (((0,), (0,)), ((), ())), preferred_element_type=f32)

    offset = PIX * VARS
    fold_ref, head_ref = late_ref.at[0:TABLE, :], late_ref.at[TABLE + 40 : TABLE + 40 + offset, :]
    coef_hi, coef_lo = parts(late_ref[TABLE : TABLE + HEADS, 0:256][:, :TABLE])
    grad_key = (nn(coef_hi, hi_ref[...]) + nn(coef_hi, lo_ref[...]) + nn(coef_lo, hi_ref[...])) * (HD**-0.5)
    gkey_ref[...] = grad_key
    key_hi, key_lo = parts(grad_key)
    by_head = nn(key_hi, tile_of(w1_ref)) + nn(key_lo, tile_of(w1_ref))
    agg = jnp.sum(jnp.where(column // HD == head, by_head, 0.0), axis=0, keepdims=True)
    agg_ref[...] = jnp.broadcast_to(agg, agg_ref.shape)
    agg_hi, agg_lo = parts(jnp.broadcast_to(agg, (8, D)))
    by_query = (nt(agg_hi, tile_of(w0_ref)) + nt(agg_lo, tile_of(w0_ref)))[0:1]
    fold_hi, fold_lo = parts(fold_ref[...])
    fold_key_hi, fold_key_lo = parts(key_ref[...])
    ge[...] = (
        nt(fold_hi, tile_of(w2_ref)) + nt(fold_lo, tile_of(w2_ref))
        + tn(coef_hi, fold_key_hi) + tn(coef_hi, fold_key_lo) + tn(coef_lo, fold_key_hi)
    )
    rest = late_ref[TABLE + HEADS : TABLE + HEADS + 24, :]
    order = [
        by_query, rest[5:6], rest[0:1], agg, jnp.sum(fold_ref[offset:, :], axis=0, keepdims=True), rest[0:1],
        rest[1:2], rest[2:3], rest[4:5], rest[3:4], rest[11:12], rest[12:13], rest[8:9], rest[9:10], rest[10:11],
    ]
    for i, r in enumerate(order):
        extra[i : i + 1, :] = r
    extra[15:19, :] = rest[14:18]
    gram_hi, gram_lo = parts(gram_ref[...])
    through = nn(gram_hi, fold_hi) + nn(gram_hi, fold_lo) + nn(gram_lo, fold_hi)
    total = jnp.sum(through * fold_ref[...], axis=0, keepdims=True)
    total += jnp.sum(ge[...] * ge[...], axis=0, keepdims=True)
    bias = ge[offset:, :]
    total += jnp.sum(bias * bias, axis=0, keepdims=True)
    total += jnp.sum(head_ref[...] * head_ref[...], axis=0, keepdims=True)
    total += jnp.sum(extra[0:19, :] * extra[0:19, :], axis=0, keepdims=True)
    vq = vec_ref[0:1, :].astype(bf16).astype(f32)
    total = jnp.sum(total, axis=1, keepdims=True)
    total += jnp.sum(vq * vq, axis=1, keepdims=True) * jnp.sum(agg * agg, axis=1, keepdims=True)
    query = query_ref[0:1, :]
    per_head = jnp.sum(jnp.where(column // HD == head, query * query, 0.0), axis=1, keepdims=True)
    total += jnp.sum(jnp.sum(grad_key * grad_key, axis=1, keepdims=True) * per_head, axis=0, keepdims=True)
    norm = jnp.sqrt(total + square_ref[0])
    clip = jnp.minimum(1.0, clip_norm / (norm + 1e-06))
    lane = lax.broadcasted_iota(jnp.int32, (8, 128), 1)
    clip_ref[...] = jnp.where(lane == 0, clip, norm)

    def update(rows, grad):
        p_new[rows, :], m_new[rows, :], v_new[rows, :] = adam_update(
            p_ref[rows, :], grad * clip, m_ref[rows, :], v_ref[rows, :], rate_vectors
        )

    for k in range(PIX):
        for v in range(VARS):
            extra_row = 32 + v * PIX + k
            extra[extra_row : extra_row + 1, :] = ge[k * VARS + v : k * VARS + v + 1, :]
    update(pl.ds(0, offset), extra[32 : 32 + offset, :])
    update(pl.ds(offset, VARS), bias)
    update(pl.ds(offset + VARS, VARS), bias)
    update(pl.ds(offset + 2 * VARS, offset), head_ref[...])
    update(pl.ds(2 * offset + 2 * VARS, 19), extra[0:19, :])


def tail(square, every, hi, lo, gram, key, query, vecs, late, w, m, v):
    vmem = pl.BlockSpec(memory_space=pltpu.VMEM)
    arrays = (hi, lo, gram, key, query, vecs, late, w, m, v)
    return pl.pallas_call(
        tail_kernel,
        grid=(1,),
        in_specs=[pl.BlockSpec(memory_space=pltpu.SMEM), *(tile_spec(every, m) for m in range(3))]
        + [once(a.shape) for a in arrays],
        out_specs=[once(s) for s in ((8, 128), (HEADS, D), (8, D), w.shape, w.shape, w.shape)],
        out_shape=[
            jax.ShapeDtypeStruct(s, f32) for s in ((8, 128), (HEADS, D), (8, D), w.shape, w.shape, w.shape)
        ],
        scratch_shapes=[pltpu.VMEM((TABLE, D), f32), pltpu.VMEM((32 + PIX * VARS, D), f32)],
        compiler_params=limit(52),
        cost_estimate=cost(8 * TABLE * D * D, 28 * w.size),
        name="tail",
    )(square, every, every, every, *arrays)


PROWS = 32
PCOLS = 64
GROUPS = 5
HIGHEST = lax.Precision.HIGHEST
clip_norm = 0.02
SCALE = HD**-0.5


def position_parts():
    quarter = D // 4
    omega = jnp.exp(-math.log(10000.0) * jnp.arange(quarter).astype(f32) / quarter)
    row = jnp.arange(PROWS).astype(f32)[:, None] * omega[None, :]
    col = jnp.arange(PCOLS).astype(f32)[:, None] * omega[None, :]
    zero_row = jnp.zeros((PROWS, D // 2), f32)
    zero_col = jnp.zeros((PCOLS, D // 2), f32)
    row_part = jnp.concatenate([jnp.sin(row), jnp.cos(row), zero_row], axis=1)
    col_part = jnp.concatenate([zero_col, jnp.sin(col), jnp.cos(col)], axis=1)
    return row_part, col_part


def latitude_table(start, count):
    index = start + jnp.arange(count)
    inner = jnp.arange(PIX) // 2
    lat_rows = 2 * (index // PCOLS)[:, None] + inner[None, :]
    total_rows = 2 * PROWS
    angle = (lat_rows.astype(f32) + 0.5) * (math.pi / total_rows) - math.pi / 2
    every = (jnp.arange(total_rows).astype(f32) + 0.5) * (math.pi / total_rows) - math.pi / 2
    weight = jnp.cos(angle) / jnp.mean(jnp.cos(every))
    return jnp.tile(weight, (1, VARS))


def tn(left, right):
    return lax.dot_general(left, right, (((0,), (0,)), ((), ())), preferred_element_type=f32)


def layer_norm(values, gain, shift):
    center = values - jnp.mean(values, axis=-1, keepdims=True)
    inverse = lax.rsqrt(jnp.mean(center * center, axis=-1, keepdims=True) + norm_eps)
    normed = center * inverse
    return (normed * gain + shift, normed, inverse)


def norm_back(grad_out, normed, inverse, gain):
    scaled = grad_out * gain
    grad_in = inverse * (
        scaled
        - jnp.mean(scaled, axis=-1, keepdims=True)
        - normed * jnp.mean(scaled * normed, axis=-1, keepdims=True)
    )
    return (grad_in, jnp.sum(grad_out * normed, axis=0), jnp.sum(grad_out, axis=0))


def gelu_parts(pre_act):
    phi = 0.5 * (1.0 + lax.erf(pre_act * 0.7071067811865476))
    slope = phi + pre_act * jnp.exp(-0.5 * pre_act * pre_act) * 0.3989422804014327
    return pre_act * phi, slope


def split_low(values):
    high = lax.reduce_precision(values, 8, 7)
    return high.astype(bf16), (values - high).astype(bf16)


def swap(array, bit):
    n = lax.axis_size("dp")
    return lax.ppermute(array, "dp", [(i, i ^ bit) for i in range(n)])


def shift(array, step):
    n = lax.axis_size("blk")
    return lax.ppermute(array, "blk", [(i, (i + step) % n) for i in range(n)])


def dp_bits():
    return [1 << i for i in range(lax.axis_size("dp").bit_length() - 1)]


def after(array, *others):
    return lax.optimization_barrier((array, *others))[0]


def pick(array, axis, index):
    return lax.dynamic_index_in_dim(array, index, axis, False)


def halves(array, side):
    half = array.shape[-1] // 2
    left, right = array[..., :half], array[..., half:]
    return jnp.where(side == 0, left, right), jnp.where(side == 0, right, left)


def sum_small(values):
    n_dp, blocks = lax.axis_size("dp"), lax.axis_size("blk")
    me = lax.axis_index("blk") * n_dp + lax.axis_index("dp")
    width = -(-n_dp * blocks // 128) * 128
    array = jnp.where(jnp.arange(width)[None, :] == me, values[:, None], 0.0)
    array = sum([shift(array, k) for k in range(1, blocks)], array)
    array = sum([swap(array, 2 * mask) for mask in range(1, n_dp // 2)], array)
    return jnp.sum(array + swap(array, 1), axis=1)


def gather_blocks(array):
    n = lax.axis_size("blk")
    return jnp.stack([array] + [shift(array, k) for k in range(1, n)])


def place_kernel(ref, out):
    rows = ref.shape[3]
    for d in range(ref.shape[1]):
        for m in range(ref.shape[2]):
            if len(out.shape) == 2:
                out[d * rows : (d + 1) * rows, m * D : (m + 1) * D] = ref[0, d, m]
            else:
                out[m, d * rows : (d + 1) * rows, :] = ref[0, d, m]


def gather(pieces):
    blocks, n_dp = lax.axis_size("blk"), lax.axis_size("dp")
    return lax.all_gather(pieces, ("blk", "dp"), axis=0).reshape((blocks, n_dp) + pieces.shape)


def place(every, first, size, wide=False):
    blocks, n_dp, _, rows, _ = every.shape
    tall = D // blocks
    at = first // size
    if wide:
        spec, shape = pl.BlockSpec((tall, size * D), lambda z: (z, 0)), (D, size * D)
    else:
        spec, shape = pl.BlockSpec((size, tall, D), lambda z: (0, z, 0)), (size, D, D)
    return pl.pallas_call(
        place_kernel,
        grid=(blocks,),
        in_specs=[pl.BlockSpec((1, n_dp, size, rows, D), lambda z: (z, 0, at, 0, 0))],
        out_specs=spec,
        out_shape=jax.ShapeDtypeStruct(shape, bf16),
        compiler_params=limit(32),
        cost_estimate=cost(0, 4 * size * D * D),
        name="place",
    )(every)


class SplitSum:
    def __init__(self, cur, order, low=True):
        self.blocks = lax.axis_size("blk")
        self.left = list(reversed(dp_bits()[1:]))
        rows = cur.shape[1] // (self.blocks << len(self.left))
        self.cur = cur.reshape((cur.shape[0], self.blocks) + (2,) * len(self.left) + (rows,) + cur.shape[2:])
        self.order = list(order)
        self.type = bf16 if low else f32
        self.got = []

    @classmethod
    def joined(cls, jobs):
        job = cls.__new__(cls)
        for other in jobs:
            other.take()
        job.blocks, job.type, job.got = jobs[0].blocks, jobs[0].type, []
        job.cur = jnp.concatenate([other.cur for other in jobs], axis=0)
        return job

    def take(self):
        for got in self.got:
            self.cur = self.cur + got.astype(f32)
        self.got = []

    def send(self):
        self.take()
        bit = self.order.pop(0)
        axis = 2 + self.left.index(bit)
        mine = (lax.axis_index("dp") // bit) % 2
        sent = pick(self.cur, axis, 1 - mine).astype(self.type)
        self.cur = pick(self.cur, axis, mine)
        self.left.remove(bit)
        self.got = [swap(sent, bit)]
        return sent

    def send_all(self):
        self.take()
        order, n, at = self.order, 1 << len(self.left), 2
        own = lax.axis_index("dp") // 2
        cur = self.cur.reshape(self.cur.shape[:2] + (n,) + self.cur.shape[2 + len(self.left) :])
        sent = [pick(cur, at, own ^ mask).astype(self.type) for mask in range(1, n)]
        self.cur, self.order, self.left = pick(cur, at, own), [], []
        self.got = [swap(a, 2 * (i + 1)) for i, a in enumerate(sent)]
        return sent

    def send_blocks(self):
        self.take()
        blk = lax.axis_index("blk")
        sent = [pick(self.cur, 1, (blk + k) % self.blocks).astype(self.type) for k in range(1, self.blocks)]
        self.cur = pick(self.cur, 1, blk)
        self.got = [shift(a, k + 1) for k, a in enumerate(sent)]
        return sent

    def parts(self):
        return [self.cur, *self.got]

    def end(self):
        for got in self.got:
            self.cur = self.cur + got.astype(f32)
        self.got = []
        return self.cur


class SumRows:
    def __init__(self, mine, other):
        self.rows = mine.shape[0]
        self.side = lax.axis_index("dp") % 2
        self.job = SplitSum((mine + swap(other, 1).astype(f32))[None], dp_bits()[1:])
        self.steps = [self.job.send_all, self.job.send_blocks, self.widen_blocks, self.widen, self.close]

    def step(self):
        return self.steps.pop(0)()

    def widen_blocks(self):
        part = self.job.end()[0].astype(bf16)
        n, blk = lax.axis_size("blk"), lax.axis_index("blk")
        cur = gather_blocks(part)
        self.cur = jnp.stack([pick(cur, 0, (blk - z + n) % n) for z in range(n)])

    def widen(self):
        n, own = lax.axis_size("dp") // 2, lax.axis_index("dp") // 2
        every = jnp.stack([self.cur] + [swap(self.cur, 2 * mask) for mask in range(1, n)])
        self.cur = jnp.stack([pick(every, 0, own ^ i) for i in range(n)], axis=1).reshape(self.rows, -1)

    def close(self):
        cur, got = self.cur, swap(self.cur, 1)
        whole = jnp.where(self.side == 0, jnp.concatenate([cur, got], 1), jnp.concatenate([got, cur], 1))
        return whole.astype(f32)

    def end(self):
        while len(self.steps) > 1:
            self.step()
        return self.step()


def shards(fields, targets, lead_time, pixel_mask, group_id, slot_of, tiles, tiles_m, tiles_v, vectors, vec_m, vec_v):
    _, count, _ = fields.shape
    blocks, n_dp = lax.axis_size("blk"), lax.axis_size("dp")
    total = count * blocks
    folds = FF // D
    dp, blk = lax.axis_index("dp"), lax.axis_index("blk")
    side = dp % 2
    start = blk * count
    others = dp_bits()[1:]
    first_order, second_order = tuple(others), tuple(reversed(others))
    slots, tall, _ = tiles.shape
    n_tiles = slots * n_dp
    rows = 2 * tall // n_dp
    half = D // 2
    fine = tall // n_dp % 16 == 0

    mask_float = pixel_mask[0].astype(f32)
    var_local = jnp.sum(jnp.sum(mask_float, axis=0).reshape(VARS, PIX), axis=1)
    group_hot = (group_id[0] == jnp.arange(GROUPS)).astype(f32)
    counted = sum_small(jnp.pad(jnp.concatenate([var_local, group_hot]), (0, 64 - VARS - GROUPS)))
    field_t = fields[0].astype(bf16).reshape(count, VARS, PIX).transpose(2, 1, 0)
    field_all = gather_blocks(field_t)

    if fine:
        low_rows = tall // n_dp
        pieces = tiles.astype(bf16).reshape(slots, n_dp, low_rows, D)
        pieces = lax.all_to_all(pieces, "dp", 1, 0, tiled=True).reshape(n_tiles, low_rows, D)
        first = gather(choose(slot_of, pieces, 0, 8, slot_of))
        weight_out = place(first, 7, 1)[0]
    else:
        slots_low = lax.all_gather(tiles.astype(bf16), "blk", axis=1, tiled=True)
        slots_low = lax.all_gather(slots_low, "dp", axis=0, tiled=True)
        weights = [pick(slots_low, 0, slot_of[m]) for m in range(n_tiles)]
        first = jnp.stack(weights[:8])[None, None]
        weight_out = weights[7]
        weight_one = jnp.concatenate(weights[8:12], axis=1)
        weight_two = jnp.concatenate(weights[12:], axis=0)

    var_total, group_total = counted[:VARS], counted[VARS : VARS + GROUPS] / blocks
    sample_weight = jnp.sum(group_total) / (GROUPS * jnp.sum(group_hot * group_total))
    count_pixels = VARS * jnp.repeat(var_total, PIX)
    factor = sample_weight * mask_float * latitude_table(start, count) / count_pixels

    offset = VARS * PIX
    embed_weight = vectors[:offset].reshape(VARS, PIX, D).transpose(1, 0, 2).reshape(offset, D)
    embed_bias = vectors[offset : offset + VARS] + vectors[offset + VARS : offset + 2 * VARS]
    embed = jnp.concatenate([embed_weight, embed_bias], axis=0)
    head_low = vectors[offset + 2 * VARS : 2 * offset + 2 * VARS].astype(bf16)
    extras = vectors[2 * offset + 2 * VARS :]
    gram = lax.dot_general(embed, embed, NT, precision=HIGHEST, preferred_element_type=f32)
    embed_hi, embed_lo = split_low(embed)

    fold_vecs = jnp.concatenate([extras[0:1], extras[3:5], jnp.zeros((5, D), f32)], axis=0)
    fold_vecs = after(fold_vecs, counted, field_all[:, 0, :8, :128])
    coef, fold_low, fold_low_t, fold_key, query_f = fold(first, embed_hi, embed_lo, fold_vecs)
    if fine:
        second = gather(choose(slot_of, pieces, 8, 8, first))
        weight_one, weight_two = place(second, 0, 4, True), place(second, 4, 4).reshape(FF, D)
    mixed = mix(field_all, coef, fold_low_t)

    row_part, col_part = position_parts()
    row_part = row_part.reshape(blocks, PROWS // blocks, D)
    row_here = jnp.concatenate([pick(row_part, 0, (blk - k + blocks) % blocks) for k in range(blocks)], axis=0)
    lead_row = extras[5] + lead_time[0] * extras[1] + extras[2]
    vecs = jnp.concatenate([extras[6:10], jnp.zeros((4, D), f32)], axis=0)
    hidden0, normed1_low, query_blk, key_all, value_all = front(
        mixed, first, row_here + lead_row, col_part, vecs, blocks
    )
    own1_low = normed1_low[:count]
    attended_low, log_total = attend(query_blk, key_all, value_all)

    hidden1 = hidden0[:count] + nn(attended_low, weight_out)
    normed2_out, normed2, inverse2 = layer_norm(hidden1, extras[10], extras[11])
    normed2_low = normed2_out.astype(bf16)
    pre_act = nn(normed2_low, weight_one) + extras[15 : 15 + folds].reshape(FF)
    activ, slope = gelu_parts(pre_act)
    activ_low = activ.astype(bf16)
    hidden2 = hidden1 + nn(activ_low, weight_two) + extras[12]
    normed3_out, normed3, inverse3 = layer_norm(hidden2, extras[13], extras[14])
    normed3_low = normed3_out.astype(bf16)
    error = nt(normed3_low, head_low) - targets[0]
    loss_local = jnp.sum(factor * error * error)
    grad_pred_low = (2.0 * factor * error).astype(bf16)
    grad_head = tn(grad_pred_low, normed3_low)
    grad_h2, gain3, shift3 = norm_back(nn(grad_pred_low, head_low), normed3, inverse3, extras[13])
    grad_h2_low = grad_h2.astype(bf16)
    bias2 = jnp.sum(grad_h2, axis=0)
    grad_pre = nt(grad_h2_low, weight_two) * slope
    bias1 = jnp.sum(grad_pre, axis=0).reshape(folds, D)
    grad_pre_low = grad_pre.astype(bf16)

    def weight_grads(left, mine, other):
        sent = tn(left, other).astype(bf16)
        return tn(left, mine), swap(sent, 1), sent

    both = lambda parts: parts[0] + parts[1].astype(f32)
    if fine:
        two_parts = weight_grads(activ_low, *halves(grad_h2_low, side))
        left, right = [
            jnp.concatenate([grad_pre_low[:, f * D + s * half : f * D + (s + 1) * half] for f in range(folds)], axis=1)
            for s in range(2)
        ]
        one_parts = weight_grads(normed2_low, jnp.where(side == 0, left, right), jnp.where(side == 0, right, left))
        two_job = SplitSum(both(two_parts).reshape(folds, D, half), first_order)
        one_job = SplitSum(both(one_parts)[None], second_order)
    grad_n2 = nt(grad_pre_low, weight_one)
    grad_h1_norm, gain2, shift2 = norm_back(grad_n2, normed2, inverse2, extras[10])
    grad_h1 = grad_h2 + grad_h1_norm
    grad_h1_low = grad_h1.astype(bf16)
    early = jnp.concatenate(
        [jnp.stack([bias2, gain3, shift3, gain2, shift2, jnp.zeros_like(bias2)]), bias1, jnp.zeros((6, D), f32), grad_head],
        axis=0,
    )
    grad_attended = nt(grad_h1_low, weight_out).astype(bf16)
    if fine:
        grad_attended = after(grad_attended, two_job.send(), one_job.send(), early)
    grad_query, grad_keys, grad_values = attend_back(query_blk, key_all, value_all, attended_low, grad_attended, log_total)
    if fine:
        sent = [two_job.send(), one_job.send()]
        grad_query, grad_keys, grad_values, *_ = lax.optimization_barrier((grad_query, grad_keys, grad_values, *sent))
        query_parts = weight_grads(own1_low, *halves(grad_query, side))
        out_parts = weight_grads(attended_low, *halves(grad_h1_low, side))
        key_parts = weight_grads(normed1_low, *halves(grad_keys, side))
        value_parts = weight_grads(normed1_low, *halves(grad_values, side))
        pair_job = SplitSum(jnp.stack([both(key_parts), both(value_parts)]), second_order)
        end_job = SplitSum(jnp.stack([both(query_parts), both(out_parts)]), first_order)
        grad_query = after(grad_query, pair_job.send(), end_job.send())
    grad_h0_low, grad_mixed, sums = back(grad_query, grad_keys, grad_values, hidden0, grad_h1, first, vecs, blocks)
    sums = jnp.where(jnp.arange(8)[:, None] == 5, sums[0] * lead_time[0], sums)
    step = 16 * (n_dp // 2) * blocks
    below = sums.shape[0] + early.shape[0]
    rest = jnp.concatenate([sums, early, jnp.zeros((-(TABLE + HEADS + below) % step, D), f32)], axis=0)
    if fine:
        sent = [pair_job.send(), end_job.send(), *two_job.send_blocks(), *one_job.send_blocks(), rest]
        grad_h0_low, grad_mixed, *_, rest = lax.optimization_barrier((grad_h0_low, grad_mixed, *sent))
        agg_parts = weight_grads(mixed, *halves(grad_h0_low, side))
        agg_job = SplitSum(both(agg_parts)[None], first_order)
        grad_mixed = after(grad_mixed, agg_parts[2])
    late_mine, late_other = mix_back(side.reshape(1), field_all, coef, fold_low, grad_mixed, rest)
    if fine:
        late_mine, late_other, *_ = lax.optimization_barrier((late_mine, late_other, *agg_job.send_all()))
    late_job = SumRows(late_mine, late_other)
    if fine:
        edge_job = SplitSum.joined([end_job, pair_job])
        sent = [*edge_job.send_blocks(), two_job.end(), one_job.end()]
        late_job.job.cur = after(late_job.job.cur, *sent)
        late_job.step()
        agg_job.send_blocks()
        plan = (
            [(12 + f, f, 0) for f in range(folds)],
            [(8 + f, 0, f) for f in range(folds)],
            [(m, i, 0) for i, m in enumerate((4, 7, 5, 6))],
            [(3, 0, 0)],
        )
        by_slot, square = finish(slot_of, plan, [j.parts() for j in (two_job, one_job, edge_job, agg_job)])
        part_square = jnp.sum(square)
        while len(late_job.steps) > 1:
            late_job.step()
        by_slot, late_job.cur = lax.optimization_barrier((by_slot, late_job.cur))
        by_slot = lax.all_to_all(by_slot, "dp", 0, 0, tiled=True).astype(f32)
        slot_grads = by_slot.reshape(n_dp // 2, 2, slots, rows, half).transpose(2, 0, 3, 1, 4).reshape(slots, tall, D)
    else:
        rest = [tn(mixed, grad_h0_low), tn(own1_low, grad_query), tn(normed1_low, grad_keys),
                tn(normed1_low, grad_values), tn(attended_low, grad_h1_low)]
        rest += [tn(normed2_low, grad_pre_low[:, f * D : (f + 1) * D]) for f in range(folds)]
        rest += [tn(activ_low[:, f * D : (f + 1) * D], grad_h2_low) for f in range(folds)]
        by_slot = jnp.zeros((n_tiles, D, D), f32)
        for m, grad in enumerate(rest):
            by_slot = lax.dynamic_update_index_in_dim(by_slot, grad, slot_of[m + 3], 0)
        slot_grads = lax.psum_scatter(by_slot, "dp", scatter_dimension=0, tiled=True)
        slot_grads = lax.psum_scatter(slot_grads, "blk", scatter_dimension=1, tiled=True)
        part_square = jnp.sum(slot_grads * slot_grads)
    late = late_job.end()
    numbers = sum_small(jnp.pad(jnp.stack([part_square, loss_local]), (0, 6)))
    loss = numbers[1]
    clips, grad_key, grad_agg, vectors_new, vec_m_new, vec_v_new = tail(
        numbers[:1], first, embed_hi, embed_lo, gram, fold_key, query_f, fold_vecs, late, vectors, vec_m, vec_v
    )
    clip, grad_norm = clips[0, 0], clips[0, 1]

    at_rows = blk * tall
    var_query_f = extras[0].astype(bf16).astype(f32)
    own_first = lax.dynamic_slice_in_dim(var_query_f, at_rows, tall, 0)[:, None] * grad_agg[0][None, :]
    own_key = lax.dynamic_slice_in_dim(grad_key, at_rows, tall, 1)
    own_second = jnp.repeat(own_key.T, HD, axis=1) * query_f[0][None, :]
    own_third = lax.dot_general(
        lax.dynamic_slice_in_dim(embed, at_rows, tall, 1), late[:TABLE], (((0,), (0,)), ((), ())),
        precision=HIGHEST, preferred_element_type=f32,
    )
    my_tiles = [jnp.sum(jnp.where(slot_of == dp * slots + t, jnp.arange(n_tiles), 0)) for t in range(slots)]
    shard_grads = jnp.stack(
        [
            jnp.where(m == 0, own_first, jnp.where(m == 1, own_second, jnp.where(m == 2, own_third, slot_grads[t])))
            for t, m in enumerate(my_tiles)
        ]
    )
    tiles_new, tiles_m_new, tiles_v_new = adam_update(tiles, shard_grads * clip, tiles_m, tiles_v, rate_tiles)
    return (loss, grad_norm, tiles_new, tiles_m_new, tiles_v_new, vectors_new, vec_m_new, vec_v_new)


def solution(mesh):
    tile = P("dp", "blk", None)
    placed = (tile, tile, P("dp"), tile, P("dp"), P(), tile, tile, tile, P(), P(), P())
    return jax.shard_map(
        shards,
        mesh=mesh,
        in_specs=placed,
        out_specs=(P(), P(), tile, tile, tile, P(), P(), P()),
        check_vma=False,
    )
```

time: 3450 us -> 675 us (0.20)
  matrix products: 911 us -> 88.2 us
  waiting for transfers between devices: 925 us -> 182 us
  local copies, waits for them, and re-layouts: 758 us -> 50.2 us
  other arithmetic: 726 us -> 43.4 us
  Pallas kernels: 0 us -> 190 us
  starting transfers between devices: 0.37 us -> 68 us
  blocking collectives: 83.4 us -> 20.3 us
    dot_general x40 -> x25, matrix products: 911 us -> 88.2 us  [the longest x15 44.7 us: tn(): lax.dot_general(left, right, (((0,), (0,)), ((), ())), preferred_element_...]
    reshape x8 -> x5, local copies, waits for them, and re-layouts: 399 us -> 2.19 us  [the longest x1 1.31 us: shards(): own_second = jnp.repeat(own_key.T, HD, axis=1) * query_f[0][None, :]]
    all_gather x4 -> x2, waiting for transfers between devices: 508 us -> 116 us  [gather(): lax.all_gather(pieces, ('blk', 'dp'), axis=0)]
    reduce_scatter x4 -> x0, waiting for transfers between devices: 296 us -> none  [the longest x1 165 us: shards(): lax.psum_scatter(slot_grads.astype(jnp.bfloat16), 'blk', scatter_dimensio...]
    convert_element_type x12 -> x15, other arithmetic: 275 us -> 9.94 us  [the longest x2 2.56 us: send(): sent = pick(self.cur, axis, 1 - mine).astype(self.type)]
    pallas_call x0 -> x14, Pallas kernels: none -> 190 us  [the longest x1 45.2 us: attend_back(): pl.pallas_call(functools.partial(attend_back_kernel, qb), grid=(HEADS //...]
    convert_element_type x6 -> x14, local copies, waits for them, and re-layouts: 179 us -> 7.8 us  [the longest x6 3.39 us: send(): sent = pick(self.cur, axis, 1 - mine).astype(self.type)]
    dot_general x3 -> x0, other arithmetic: 148 us -> none  [the longest x1 63.8 us: shards(): jnp.einsum('rhv,rvhe->he', grad_score_agg, keys_agg, preferred_element_ty...]
  transfers between devices with their start and end apart: 9 -> 64, of which waited for: 8 -> 24; matrix products, arithmetic and copies ran while one was open for 24% -> 15% of each run, Pallas kernels for 0% -> 26%
where the time goes in v1:
time: 675 us; the launch traced here: 666 us
  Pallas kernels  190 us (28%)
  waiting for transfers between devices  182 us (27%)
  matrix products  88.2 us (13%)
  starting transfers between devices  68 us (10%)
  local copies, waits for them, and re-layouts  50.2 us (7%)
  other arithmetic  43.4 us (6%)
  between operations  23.6 us (3%)
  blocking collectives  20.3 us (3%)
    all_gather x2, waiting for transfers between devices, gather(): lax.all_gather(pieces, ('blk', 'dp'), axis=0)  116 us
    pallas_call x1, Pallas kernels, attend_back(): pl.pallas_call(functools.partial(attend_back_kernel, qb), grid=(HEADS //...  45.2 us
    dot_general x15, matrix products, tn(): lax.dot_general(left, right, (((0,), (0,)), ((), ())), preferred_element_...  44.7 us
    ppermute x27, waiting for transfers between devices, shift(): return lax.ppermute(array, 'blk', [(i, (i + step) % n) for i in range(n)])  42 us
    ppermute x27, starting transfers between devices, shift(): return lax.ppermute(array, 'blk', [(i, (i + step) % n) for i in range(n)])  35.4 us
    unnamed x232, local copies, waits for them, and re-layouts  34.9 us
    pallas_call x1, Pallas kernels, attend(): pl.pallas_call(functools.partial(attend_kernel, qb), grid=(HEADS // 2,),...  31.2 us
    pallas_call x1, Pallas kernels, back(): pl.pallas_call(back_kernel, grid=(blocks,), in_specs=[once((count, D)), b...  29 us
  transfers between devices with their start and end apart: 64, of which 24 were waited for; matrix products, arithmetic and copies ran while one was open for 15% of the time, Pallas kernels for 26%

profile of v1, /device:TPU:0, one launch (start us, length us, event | category | flops | bytes accessed | tf_op | source)
XLA Modules:
  0.0 665.8 jit_solution(4016356900780776261)
XLA Ops:
  9.1 20.3 %all_to_all.20 = bf16[2,8,32,1024]{3,2,0,1:T(8,128)(2,1)S(1)} all-to-all(bf16[2,8,32,1024]{3,2,0,1:T(8,128)(2,1)S(1)} %copy.69), channel_id=1, replica_groups=mesh['dp'=8,'blk'=4] {'dp'}, dimensions={1} | all-to-all | bytes 2097152 | tf_op jit(solution)/shard_map/all_to_all | solution.py:844
  30.9 114.3 %all-gather.5.cloned.1.call-done = bf16[256,32,1024]{2,1,0:T(8,128)(2,1)} async-done(((bf16[8,32,1024]{2,1,0:T(8,128)(2,1)}), bf16[256,32,1024]{2,1,0:T(8,128)(2,1)}) %all-gather.5.cloned.1.call-update) | async-done | bytes 16777232 | tf_op jit(solution)/shard_map/all_gather | solution.py:700
  145.2 5.8 copy-done
  159.1 3.3 collective-permute-start.2
  180.4 10.5 %collective-permute-done.1 = bf16[4,48,512]{2,1,0:T(8,128)(2,1)S(1)} collective-permute-done((bf16[4,48,512]{2,1,0:T(8,128)(2,1)}, bf16[4,48,512]{2,1,0:T(8,128)(2,1)S(1)}, u32[]{:S(2)}, u32[]{:S(2)}) %collective-permute-start.1) | collective-permute-done | bytes 196640 | tf_op jit(solution)/shard_map/ppermute | solution.py:652
  192.2 5.8 copy-done.1
  198.3 5.5 fold.1
  205.8 7.4 %mix.1.m_ref = bf16[2048,1024]{1,0:T(8,128)(2,1)S(1)} custom-call(bf16[4,4,48,512]{3,2,1,0:T(8,128)(2,1)S(1)} %pad_maximum_fusion.3.f_ref, f32[240,128]{1,0:T(8,128)S(1)} %get-tuple-element.52.coef_ref, bf16[1024,240]{1,0:T(8,128)(2,1)S(1)} %get-tuple-element.53.tt_ref), custom_call_target="tpu_custom_call" | custom-call | flops 4026531840 | bytes 8388608 | tf_op jit(solution)/shard_map/mix/pallas_call | solution.py:220
  215.9 23.1 %front.1 = (f32[2048,1024]{1,0:T(8,128)}, bf16[2048,1024]{1,0:T(8,128)(2,1)}, bf16[512,1024]{1,0:T(8,128)(2,1)S(1)}, bf16[2048,1024]{1,0:T(8,128)(2,1)}, bf16[2048,1024]{1,0:T(8,128)(2,1)}) custom-call(bf16[2048,1024]{1,0:T(8,128)(2,1)} %copy-done.3, bf16[4,8,8,32,1024]{4,3,2,1,0:T(8,128)(2,1)} %bitcast.298, bf16[4,8,8,32,1024]{4,3,2,1,0:T(8,128)(2,1)} %bitcast.299, ...), custom_call_target="tpu_custom_call" | custom-call | flops 12884901888 | bytes 33554432 | tf_op jit(solution)/shard_map/front/pallas_call | solution.py:321
  239.0 31.2 %attend.1 = (bf16[512,1024]{1,0:T(8,128)(2,1)S(1)}, f32[512,128]{1,0:T(8,128)S(1)}) custom-call(bf16[512,1024]{1,0:T(8,128)(2,1)S(1)} %get-tuple-element.55.q_ref, bf16[2048,1024]{1,0:T(8,128)(2,1)} %get-tuple-element.56.k_ref, bf16[2048,1024]{1,0:T(8,128)(2,1)} %get-tuple-element.57.v_ref), custom_call_target="tpu_custom_call" | custom-call | flops 17179869184 | bytes 16777216 | tf_op jit(solution)/shard_map/attend/pallas_call | solution.py:88
  270.3 3.4 fusion.198
  277.5 4.2 place.4
  281.8 7.6 %place.5 = bf16[4,1024,1024]{2,1,0:T(8,128)(2,1)S(1)} custom-call(bf16[4,8,8,32,1024]{4,3,2,1,0:T(8,128)(2,1)} %bitcast.316), custom_call_target="tpu_custom_call" | custom-call | bytes 16777216 | tf_op jit(solution)/shard_map/place/pallas_call | solution.py:711
  289.5 8.2 %multiply_convert_fusion = (bf16[512,4096]{1,0:T(8,128)(2,1)S(1)}, f32[512,4096]{1,0:T(8,128)}) fusion(f32[4096]{0:T(1024)S(1)} %bitcast.369, bf16[1024,4096]{1,0:T(8,128)(2,1)S(1)} %place.4, f32[512,1024]{1,0:T(8,128)S(1)} %copy-done.31, f32[1024]{0:T(1024)S(1)} %bitcast.376, f32[1024]{0:T(1024)S(1)} %bitcast.358, f32[512]{0:T(512)S(1)} %add_rsqrt_fusion.1, ...), kind=kOutput, calls=%fused_computation.8 | convolution fusion | flops 4310171648 | bytes 23097344 | tf_op jit(solution)/shard_map/dot_general | solution.py:30
  297.7 4.6 fusion.199
  308.7 10.2 %fusion.191 = (f32[4096]{0:T(1024)S(1)}, bf16[512,4096]{1,0:T(8,128)(2,1)S(1)}) fusion(f32[512,4096]{1,0:T(8,128)} %get-tuple-element.192, f32[4096]{0:T(1024)S(1)} %bitcast.370, bf16[512,1024]{1,0:T(8,128)(2,1)S(1)} %convert_element_type.551, bf16[4096,1024]{1,0:T(8,128)(2,1)S(1)} %bitcast.314), kind=kOutput, calls=%fused_computation.355 | convolution fusion | flops 4320129024 | bytes 22052864 | tf_op jit(solution)/shard_map/dot_general | solution.py:26
  322.0 6.0 convolution_convert_fusion.1
  328.4 2.5 fusion.87.gram_ref
  331.0 5.0 convolution_convert_fusion
  336.3 8.5 %multiply_reduce_fusion = (f32[1024]{0:T(1024)}, f32[512]{0:T(512)S(1)}, f32[512]{0:T(512)S(1)}, f32[1024]{0:T(1024)}, f32[512,1024]{1,0:T(8,128)S(1)}) fusion(f32[512,1024]{1,0:T(8,128)S(1)} %copy-done.33, f32[512]{0:T(512)S(1)} %copy-done.100, f32[512]{0:T(512)S(1)} %copy-done.91, f32[1024]{0:T(1024)S(1)} %bitcast.360, ...), kind=kOutput, calls=%fused_computation.63 | convolution fusion | flops 4299682816 | bytes 16797696 | tf_op jit(solution)/shard_map/dot_general | solution.py:26
  352.3 4.9 convert_add_fusion
  359.2 3.3 copy-done.43
  362.5 4.7 convert_add_fusion.1
  371.2 45.2 %attend_back.1 = (bf16[512,1024]{1,0:T(8,128)(2,1)S(1)}, bf16[2048,1024]{1,0:T(8,128)(2,1)}, bf16[2048,1024]{1,0:T(8,128)(2,1)}) custom-call(bf16[512,1024]{1,0:T(8,128)(2,1)S(1)} %copy-done.15, bf16[2048,1024]{1,0:T(8,128)(2,1)} %get-tuple-element.56.k_ref, bf16[2048,1024]{1,0:T(8,128)(2,1)} %get-tuple-element.57.v_ref, bf16[512,1024]{1,0:T(8,128)(2,1)S(1)} %copy-done.21, ...), custom_call_target="tpu_custom_call" | custom-call | flops 42949672960 | bytes 33554432 | tf_op jit(solution)/shard_map/attend_back/pallas_call | solution.py:141
  416.4 3.6 bitcast_add_fusion
  421.6 2.5 bitcast_add_fusion.1
  426.8 2.4 fusion.69
  433.8 2.4 fusion.66
  440.0 2.8 convert_add_fusion.4
  448.7 9.1 %collective-permute-done.18 = bf16[1,4,64,2048]{3,2,1,0:T(8,128)(2,1)S(1)} collective-permute-done((bf16[1,4,64,2048]{3,2,1,0:T(8,128)(2,1)S(1)}, bf16[1,4,64,2048]{3,2,1,0:T(8,128)(2,1)S(1)}, u32[]{:S(2)}, u32[]{:S(2)}) %collective-permute-start.18) | collective-permute-done | bytes 1048608 | tf_op jit(solution)/shard_map/ppermute | solution.py:647
  459.4 3.5 collective-permute-start.21
  462.9 29.0 %back.1 = (bf16[2048,1024]{1,0:T(8,128)(2,1)}, bf16[2048,1024]{1,0:T(8,128)(2,1)}, f32[8,1024]{1,0:T(8,128)S(1)}) custom-call(bf16[512,1024]{1,0:T(8,128)(2,1)S(1)} %get-tuple-element.68.dq_ref, bf16[2048,1024]{1,0:T(8,128)(2,1)} %get-tuple-element.66.dk_ref, bf16[2048,1024]{1,0:T(8,128)(2,1)} %get-tuple-element.67.dv_ref, ...), custom_call_target="tpu_custom_call" | custom-call | flops 15032385536 | bytes 33554432 | tf_op jit(solution)/shard_map/back/pallas_call | solution.py:386
  496.6 3.4 collective-permute-start.15
  500.0 11.1 %collective-permute-done.20 = bf16[1,64,2048]{2,1,0:T(8,128)(2,1)} collective-permute-done((bf16[1,64,2048]{2,1,0:T(8,128)(2,1)}, bf16[1,64,2048]{2,1,0:T(8,128)(2,1)}, u32[]{:S(2)}, u32[]{:S(2)}) %collective-permute-start.20) | collective-permute-done | bytes 262176 | tf_op jit(solution)/shard_map/ppermute | solution.py:652
  518.6 2.4 fusion.72
  521.1 4.7 collective-permute-done.14
  529.1 16.9 %mix_back.1 = (f32[512,512]{1,0:T(8,128)S(1)}, bf16[512,512]{1,0:T(8,128)(2,1)S(1)}) custom-call(s32[1]{0:T(128)} %bitcast.84.side_ref, bf16[4,4,48,512]{3,2,1,0:T(8,128)(2,1)S(1)} %copy-done.6, f32[240,128]{1,0:T(8,128)S(1)} %copy-done.19, bf16[240,1024]{1,0:T(8,128)(2,1)S(1)} %copy-done.17, bf16[2048,1024]{1,0:T(8,128)(2,1)S(1)} %copy-done.13, ...), custom_call_target="tpu_custom_call" | custom-call | flops 8053063680 | bytes 8388608 | tf_op jit(solution)/shard_map/mix_back/pallas_call | solution.py:279
  546.2 4.9 convert_add_fusion.2
  557.3 3.3 collective-permute-done.34
  560.6 5.1 collective-permute-done.35
  568.8 2.7 collective-permute-done.32.refs_5_
  574.3 5.9 collective-permute-done.31.refs_4_
  581.2 4.5 collective-permute-start.37
  597.9 2.6 collective-permute-done.52
  603.0 2.6 collective-permute-start.41
  619.5 3.8 all-to-all-start.1
  630.6 15.2 %tail.1 = (f32[8,128]{1,0:T(8,128)S(1)}, f32[16,1024]{1,0:T(8,128)S(1)}, f32[8,1024]{1,0:T(8,128)S(1)}, f32[499,1024]{1,0:T(8,128)}, f32[499,1024]{1,0:T(8,128)}, /*index=5*/f32[499,1024]{1,0:T(8,128)}) custom-call(f32[1]{0:T(128)} %get-tuple-element.187.square_ref, bf16[4,8,8,32,1024]{4,3,2,1,0:T(8,128)(2,1)} %bitcast.306, ...), custom_call_target="tpu_custom_call" | custom-call | flops 2013265920 | bytes 14307328 | tf_op jit(solution)/shard_map/tail/pallas_call | solution.py:566
  653.8 4.8 multiply_subtract_fusion
  (483 shorter events, 147.3 us)
Async XLA Ops:
  7.2 138.0 %all-gather.5.cloned.1.call-start = ((), (), s32[]{:S(2)}) async-start(), calls=%async_computation.2 | async-start | bytes 17301504 | tf_op jit(solution)/shard_map/all_gather | solution.py:700
  30.8 246.7 %all-gather.7.cloned.1.call-start = ((), (), s32[]{:S(2)}) async-start(), calls=%async_computation.3 | async-start | bytes 17301504 | tf_op jit(solution)/shard_map/all_gather | solution.py:700
  154.3 13.8 %collective-permute-start.4 = (f32[64,128]{1,0:T(8,128)}, f32[64,128]{1,0:T(8,128)}, u32[]{:S(2)}, u32[]{:S(2)}) collective-permute-start(f32[64,128]{1,0:T(8,128)} %broadcast_select_fusion.1), channel_id=1, source_target_pairs={{0,2},{1,3},{2,0},{3,1},{4,6},{5,7},{6,4},{7,5},{8,10},{9,11},{10,... | collective-permute-start | bytes 98312 | tf_op jit(solution)/shard_map/ppermute | solution.py:652
  155.8 12.3 %collective-permute-start.5 = (f32[64,128]{1,0:T(8,128)}, f32[64,128]{1,0:T(8,128)}, u32[]{:S(2)}, u32[]{:S(2)}) collective-permute-start(f32[64,128]{1,0:T(8,128)} %broadcast_select_fusion.1), channel_id=1, source_target_pairs={{0,3},{1,0},{2,1},{3,2},{4,7},{5,4},{6,5},{7,6},{8,11},{9,8},{10,9... | collective-permute-start | bytes 98312 | tf_op jit(solution)/shard_map/ppermute | solution.py:652
  157.1 11.0 %collective-permute-start.3 = (f32[64,128]{1,0:T(8,128)}, f32[64,128]{1,0:T(8,128)}, u32[]{:S(2)}, u32[]{:S(2)}) collective-permute-start(f32[64,128]{1,0:T(8,128)} %broadcast_select_fusion.1), channel_id=1, source_target_pairs={{0,1},{1,2},{2,3},{3,0},{4,5},{5,6},{6,7},{7,4},{8,9},{9,10},{10,1... | collective-permute-start | bytes 98312 | tf_op jit(solution)/shard_map/ppermute | solution.py:652
  158.6 21.7 %collective-permute-start = (bf16[4,48,512]{2,1,0:T(8,128)(2,1)}, bf16[4,48,512]{2,1,0:T(8,128)(2,1)}, u32[]{:S(2)}, u32[]{:S(2)}) collective-permute-start(bf16[4,48,512]{2,1,0:T(8,128)(2,1)} %bitcast.219.clone.2), channel_id=1, source_target_pairs={{0,1},{1,2},{2,3},{3,0},{4,5},{5,6},{6,7},{7,4},{8,9},{9,10},{10,1... | collective-permute-start | bytes 589832 | tf_op jit(solution)/shard_map/ppermute | solution.py:652
  159.1 21.2 %collective-permute-start.2 = (bf16[4,48,512]{2,1,0:T(8,128)(2,1)}, bf16[4,48,512]{2,1,0:T(8,128)(2,1)}, u32[]{:S(2)}, u32[]{:S(2)}) collective-permute-start(bf16[4,48,512]{2,1,0:T(8,128)(2,1)} %bitcast.219.clone.2), channel_id=1, source_target_pairs={{0,3},{1,0},{2,1},{3,2},{4,7},{5,4},{6,5},{7,6},{8,11},{9,8},{10,9... | collective-permute-start | bytes 589832 | tf_op jit(solution)/shard_map/ppermute | solution.py:652
  173.9 17.0 %collective-permute-start.1 = (bf16[4,48,512]{2,1,0:T(8,128)(2,1)}, bf16[4,48,512]{2,1,0:T(8,128)(2,1)S(1)}, u32[]{:S(2)}, u32[]{:S(2)}) collective-permute-start(bf16[4,48,512]{2,1,0:T(8,128)(2,1)} %bitcast.219.clone.2), channel_id=1, source_target_pairs={{0,2},{1,3},{2,0},{3,1},{4,6},{5,7},{6,4},{7,5},{8,10},{9,11},{10,... | collective-permute-start | bytes 589832 | tf_op jit(solution)/shard_map/ppermute | solution.py:652
  328.1 23.5 %collective-permute-start.16 = (bf16[1024,2048]{1,0:T(8,128)(2,1)}, bf16[1024,2048]{1,0:T(8,128)(2,1)}, u32[]{:S(2)}, u32[]{:S(2)}) collective-permute-start(bf16[1024,2048]{1,0:T(8,128)(2,1)} %convolution_convert_fusion.1), channel_id=1, source_target_pairs={{0,4},{4,0},{8,12},{12,8},{16,20},{20,16},{24,28},{28,24},{1,5},{5... | collective-permute-start | bytes 12582920 | tf_op jit(solution)/shard_map/ppermute | solution.py:647
  336.0 23.2 %collective-permute-start.10 = (bf16[4096,512]{1,0:T(8,128)(2,1)S(1)}, bf16[4096,512]{1,0:T(8,128)(2,1)}, u32[]{:S(2)}, u32[]{:S(2)}) collective-permute-start(bf16[4096,512]{1,0:T(8,128)(2,1)S(1)} %convolution_convert_fusion), channel_id=1, source_target_pairs={{0,4},{4,0},{8,12},{12,8},{16,20},{20,16},{24,28},{28,24},{1,5},{5... | collective-permute-start | bytes 12582920 | tf_op jit(solution)/shard_map/ppermute | solution.py:647
  348.6 80.9 %collective-permute-start.23 = (bf16[1024,512]{1,0:T(8,128)(2,1)}, bf16[1024,512]{1,0:T(8,128)(2,1)}, u32[]{:S(2)}, u32[]{:S(2)}) collective-permute-start(bf16[1024,512]{1,0:T(8,128)(2,1)} %convolution_convert_fusion.2), channel_id=1, source_target_pairs={{0,4},{4,0},{8,12},{12,8},{16,20},{20,16},{24,28},{28,24},{1,5},{5... | collective-permute-start | bytes 3145736 | tf_op jit(solution)/shard_map/ppermute | solution.py:647
  357.7 58.7 %collective-permute-start.17 = (bf16[1,4,2,64,2048]{4,3,1,2,0:T(8,128)(2,1)S(1)}, bf16[1,4,2,64,2048]{4,3,1,2,0:T(8,128)(2,1)}, u32[]{:S(2)}, u32[]{:S(2)}) collective-permute-start(bf16[1,4,2,64,2048]{4,3,1,2,0:T(8,128)(2,1)S(1)} %fusion.7), channel_id=1, source_target_pairs={{0,16},{4,20},{8,24},{12,28},{16,0},{20,4},{24,8},{28,12},{1,17},{... | collective-permute-start | bytes 6291464 | tf_op jit(solution)/shard_map/ppermute | solution.py:647
  368.9 51.0 %collective-permute-start.11 = (bf16[4,4,2,64,512]{4,3,0,1,2:T(8,128)(2,1)}, bf16[4,4,2,64,512]{4,3,0,1,2:T(8,128)(2,1)}, u32[]{:S(2)}, u32[]{:S(2)}) collective-permute-start(bf16[4,4,2,64,512]{4,3,0,1,2:T(8,128)(2,1)} %fusion.6), channel_id=1, source_target_pairs={{0,8},{4,12},{8,0},{12,4},{16,24},{20,28},{24,16},{28,20},{1,9},{5... | collective-permute-start | bytes 6291464 | tf_op jit(solution)/shard_map/ppermute | solution.py:647
  429.2 8.4 %collective-permute-start.27 = (bf16[1024,512]{1,0:T(8,128)(2,1)S(1)}, bf16[1024,512]{1,0:T(8,128)(2,1)S(1)}, u32[]{:S(2)}, u32[]{:S(2)}) collective-permute-start(bf16[1024,512]{1,0:T(8,128)(2,1)S(1)} %fusion.69), channel_id=1, source_target_pairs={{0,4},{4,0},{8,12},{12,8},{16,20},{20,16},{24,28},{28,24},{1,5},{5... | collective-permute-start | bytes 3145736 | tf_op jit(solution)/shard_map/ppermute | solution.py:647
  431.7 26.1 %collective-permute-start.18 = (bf16[1,4,64,2048]{3,2,1,0:T(8,128)(2,1)S(1)}, bf16[1,4,64,2048]{3,2,1,0:T(8,128)(2,1)S(1)}, u32[]{:S(2)}, u32[]{:S(2)}) collective-permute-start(bf16[1,4,64,2048]{3,2,1,0:T(8,128)(2,1)S(1)} %fusion.78), channel_id=1, source_target_pairs={{0,8},{4,12},{8,0},{12,4},{16,24},{20,28},{24,16},{28,20},{1,9},{5... | collective-permute-start | bytes 3145736 | tf_op jit(solution)/shard_map/ppermute | solution.py:647
  433.0 58.9 %collective-permute-start.12 = (bf16[4,4,64,512]{3,2,0,1:T(8,128)(2,1)}, bf16[4,4,64,512]{3,2,0,1:T(8,128)(2,1)S(1)}, u32[]{:S(2)}, u32[]{:S(2)}) collective-permute-start(bf16[4,4,64,512]{3,2,0,1:T(8,128)(2,1)} %fusion.77), channel_id=1, source_target_pairs={{0,16},{4,20},{8,24},{12,28},{16,0},{20,4},{24,8},{28,12},{1,17},{... | collective-permute-start | bytes 3145736 | tf_op jit(solution)/shard_map/ppermute | solution.py:647
  437.0 8.4 %collective-permute-start.22 = (bf16[1024,512]{1,0:T(8,128)(2,1)S(1)}, bf16[1024,512]{1,0:T(8,128)(2,1)S(1)}, u32[]{:S(2)}, u32[]{:S(2)}) collective-permute-start(bf16[1024,512]{1,0:T(8,128)(2,1)S(1)} %convolution_convert_fusion.3), channel_id=1, source_target_pairs={{0,4},{4,0},{8,12},{12,8},{16,20},{20,16},{24,28},{28,24},{1,5},{5... | collective-permute-start | bytes 3145736 | tf_op jit(solution)/shard_map/ppermute | solution.py:647
  444.2 68.4 %collective-permute-start.28 = (bf16[2,4,2,64,512]{4,3,0,1,2:T(8,128)(2,1)}, bf16[2,4,2,64,512]{4,3,0,1,2:T(8,128)(2,1)}, u32[]{:S(2)}, u32[]{:S(2)}) collective-permute-start(bf16[2,4,2,64,512]{4,3,0,1,2:T(8,128)(2,1)} %fusion.80), channel_id=1, source_target_pairs={{0,16},{4,20},{8,24},{12,28},{16,0},{20,4},{24,8},{28,12},{1,17},{... | collective-permute-start | bytes 3145736 | tf_op jit(solution)/shard_map/ppermute | solution.py:647
  447.9 66.8 %collective-permute-start.24 = (bf16[2,4,2,64,512]{4,3,0,1,2:T(8,128)(2,1)}, bf16[2,4,2,64,512]{4,3,0,1,2:T(8,128)(2,1)}, u32[]{:S(2)}, u32[]{:S(2)}) collective-permute-start(bf16[2,4,2,64,512]{4,3,0,1,2:T(8,128)(2,1)} %fusion.79), channel_id=1, source_target_pairs={{0,8},{4,12},{8,0},{12,4},{16,24},{20,28},{24,16},{28,20},{1,9},{5... | collective-permute-start | bytes 3145736 | tf_op jit(solution)/shard_map/ppermute | solution.py:647
  459.1 36.8 %collective-permute-start.19 = (bf16[1,64,2048]{2,1,0:T(8,128)(2,1)}, bf16[1,64,2048]{2,1,0:T(8,128)(2,1)}, u32[]{:S(2)}, u32[]{:S(2)}) collective-permute-start(bf16[1,64,2048]{2,1,0:T(8,128)(2,1)} %get-tuple-element.135), channel_id=1, source_target_pairs={{0,1},{1,2},{2,3},{3,0},{4,5},{5,6},{6,7},{7,4},{8,9},{9,10},{10,1... | collective-permute-start | bytes 786440 | tf_op jit(solution)/shard_map/ppermute | solution.py:652
  459.4 37.1 %collective-permute-start.21 = (bf16[1,64,2048]{2,1,0:T(8,128)(2,1)}, bf16[1,64,2048]{2,1,0:T(8,128)(2,1)}, u32[]{:S(2)}, u32[]{:S(2)}) collective-permute-start(bf16[1,64,2048]{2,1,0:T(8,128)(2,1)} %get-tuple-element.136), channel_id=1, source_target_pairs={{0,3},{1,0},{2,1},{3,2},{4,7},{5,4},{6,5},{7,6},{8,11},{9,8},{10,9... | collective-permute-start | bytes 786440 | tf_op jit(solution)/shard_map/ppermute | solution.py:652
  491.9 19.2 %collective-permute-start.20 = (bf16[1,64,2048]{2,1,0:T(8,128)(2,1)}, bf16[1,64,2048]{2,1,0:T(8,128)(2,1)}, u32[]{:S(2)}, u32[]{:S(2)}) collective-permute-start(bf16[1,64,2048]{2,1,0:T(8,128)(2,1)} %get-tuple-element.137), channel_id=1, source_target_pairs={{0,2},{1,3},{2,0},{3,1},{4,6},{5,7},{6,4},{7,5},{8,10},{9,11},{10,... | collective-permute-start | bytes 786440 | tf_op jit(solution)/shard_map/ppermute | solution.py:652
  495.9 25.1 %collective-permute-start.13 = (bf16[4,64,512]{2,1,0:T(8,128)(2,1)S(1)}, bf16[4,64,512]{2,1,0:T(8,128)(2,1)S(1)}, u32[]{:S(2)}, u32[]{:S(2)}) collective-permute-start(bf16[4,64,512]{2,1,0:T(8,128)(2,1)S(1)} %get-tuple-element.138), channel_id=1, source_target_pairs={{0,1},{1,2},{2,3},{3,0},{4,5},{5,6},{6,7},{7,4},{8,9},{9,10},{10,1... | collective-permute-start | bytes 786440 | tf_op jit(solution)/shard_map/ppermute | solution.py:652
  496.6 24.5 %collective-permute-start.15 = (bf16[4,64,512]{2,1,0:T(8,128)(2,1)S(1)}, bf16[4,64,512]{2,1,0:T(8,128)(2,1)S(1)}, u32[]{:S(2)}, u32[]{:S(2)}) collective-permute-start(bf16[4,64,512]{2,1,0:T(8,128)(2,1)S(1)} %get-tuple-element.139), channel_id=1, source_target_pairs={{0,3},{1,0},{2,1},{3,2},{4,7},{5,4},{6,5},{7,6},{8,11},{9,8},{10,9... | collective-permute-start | bytes 786440 | tf_op jit(solution)/shard_map/ppermute | solution.py:652
  511.1 14.7 %collective-permute-start.14 = (bf16[4,64,512]{2,1,0:T(8,128)(2,1)S(1)}, bf16[4,64,512]{2,1,0:T(8,128)(2,1)S(1)}, u32[]{:S(2)}, u32[]{:S(2)}) collective-permute-start(bf16[4,64,512]{2,1,0:T(8,128)(2,1)S(1)} %get-tuple-element.140), channel_id=1, source_target_pairs={{0,2},{1,3},{2,0},{3,1},{4,6},{5,7},{6,4},{7,5},{8,10},{9,11},{10,... | collective-permute-start | bytes 786440 | tf_op jit(solution)/shard_map/ppermute | solution.py:652
  521.0 25.2 %collective-permute-start.33 = (bf16[1024,512]{1,0:T(8,128)(2,1)S(1)}, bf16[1024,512]{1,0:T(8,128)(2,1)}, u32[]{:S(2)}, u32[]{:S(2)}) collective-permute-start(bf16[1024,512]{1,0:T(8,128)(2,1)S(1)} %fusion.72), channel_id=1, source_target_pairs={{0,4},{4,0},{8,12},{12,8},{16,20},{20,16},{24,28},{28,24},{1,5},{5... | collective-permute-start | bytes 3145736 | tf_op jit(solution)/shard_map/ppermute | solution.py:647
  527.0 19.0 %collective-permute-start.29 = (bf16[2,4,64,512]{3,2,0,1:T(8,128)(2,1)S(1)}, bf16[2,4,64,512]{3,2,0,1:T(8,128)(2,1)S(1)}, u32[]{:S(2)}, u32[]{:S(2)}) collective-permute-start(bf16[2,4,64,512]{3,2,0,1:T(8,128)(2,1)S(1)} %fusion.89), channel_id=1, source_target_pairs={{0,8},{4,12},{8,0},{12,4},{16,24},{20,28},{24,16},{28,20},{1,9},{5... | collective-permute-start | bytes 1572872 | tf_op jit(solution)/shard_map/ppermute | solution.py:647
  528.2 26.6 %collective-permute-start.25 = (bf16[2,4,64,512]{3,2,0,1:T(8,128)(2,1)S(1)}, bf16[2,4,64,512]{3,2,0,1:T(8,128)(2,1)S(1)}, u32[]{:S(2)}, u32[]{:S(2)}) collective-permute-start(bf16[2,4,64,512]{3,2,0,1:T(8,128)(2,1)S(1)} %fusion.88), channel_id=1, source_target_pairs={{0,16},{4,20},{8,24},{12,28},{16,0},{20,4},{24,8},{28,12},{1,17},{... | collective-permute-start | bytes 1572872 | tf_op jit(solution)/shard_map/ppermute | solution.py:647
  551.2 9.3 %collective-permute-start.34 = (bf16[1,4,64,512]{3,2,1,0:T(8,128)(2,1)S(1)}, bf16[1,4,64,512]{3,2,1,0:T(8,128)(2,1)S(1)}, u32[]{:S(2)}, u32[]{:S(2)}) collective-permute-start(bf16[1,4,64,512]{3,2,1,0:T(8,128)(2,1)S(1)} %get-tuple-element.129), channel_id=1, source_target_pairs={{0,8},{4,12},{8,0},{12,4},{16,24},{20,28},{24,16},{28,20},{1,9},{5... | collective-permute-start | bytes 786440 | tf_op jit(solution)/shard_map/ppermute | solution.py:647
  552.7 13.0 %collective-permute-start.35 = (bf16[1,4,64,512]{3,2,1,0:T(8,128)(2,1)S(1)}, bf16[1,4,64,512]{3,2,1,0:T(8,128)(2,1)S(1)}, u32[]{:S(2)}, u32[]{:S(2)}) collective-permute-start(bf16[1,4,64,512]{3,2,1,0:T(8,128)(2,1)S(1)} %get-tuple-element.130), channel_id=1, source_target_pairs={{0,16},{4,20},{8,24},{12,28},{16,0},{20,4},{24,8},{28,12},{1,17},{... | collective-permute-start | bytes 786440 | tf_op jit(solution)/shard_map/ppermute | solution.py:647
  553.3 12.4 %collective-permute-start.36 = (bf16[1,4,64,512]{3,2,1,0:T(8,128)(2,1)S(1)}, bf16[1,4,64,512]{3,2,1,0:T(8,128)(2,1)S(1)}, u32[]{:S(2)}, u32[]{:S(2)}) collective-permute-start(bf16[1,4,64,512]{3,2,1,0:T(8,128)(2,1)S(1)} %get-tuple-element.131), channel_id=1, source_target_pairs={{0,24},{4,28},{8,16},{12,20},{16,8},{20,12},{24,0},{28,4},{1,25},{... | collective-permute-start | bytes 786440 | tf_op jit(solution)/shard_map/ppermute | solution.py:647
  554.8 12.4 %collective-permute-start.47 = (bf16[512,512]{1,0:T(8,128)(2,1)S(1)}, bf16[512,512]{1,0:T(8,128)(2,1)S(1)}, u32[]{:S(2)}, u32[]{:S(2)}) collective-permute-start(bf16[512,512]{1,0:T(8,128)(2,1)S(1)} %get-tuple-element.84), channel_id=1, source_target_pairs={{0,4},{4,0},{8,12},{12,8},{16,20},{20,16},{24,28},{28,24},{1,5},{5... | collective-permute-start | bytes 1572872 | tf_op jit(solution)/shard_map/ppermute | solution.py:647
  555.1 16.4 %collective-permute-start.32 = (bf16[4,64,512]{2,1,0:T(8,128)(2,1)S(1)}, bf16[4,64,512]{2,1,0:T(8,128)(2,1)S(1)}, u32[]{:S(2)}, u32[]{:S(2)}) collective-permute-start(bf16[4,64,512]{2,1,0:T(8,128)(2,1)S(1)} %get-tuple-element.132), channel_id=1, source_target_pairs={{0,3},{1,0},{2,1},{3,2},{4,7},{5,4},{6,5},{7,6},{8,11},{9,8},{10,9... | collective-permute-start | bytes 786440 | tf_op jit(solution)/shard_map/ppermute | solution.py:652
  560.6 12.1 %collective-permute-start.30 = (bf16[4,64,512]{2,1,0:T(8,128)(2,1)S(1)}, bf16[4,64,512]{2,1,0:T(8,128)(2,1)S(1)}, u32[]{:S(2)}, u32[]{:S(2)}) collective-permute-start(bf16[4,64,512]{2,1,0:T(8,128)(2,1)S(1)} %get-tuple-element.133), channel_id=1, source_target_pairs={{0,1},{1,2},{2,3},{3,0},{4,5},{5,6},{6,7},{7,4},{8,9},{9,10},{10,1... | collective-permute-start | bytes 786440 | tf_op jit(solution)/shard_map/ppermute | solution.py:652
  565.7 14.5 %collective-permute-start.31 = (bf16[4,64,512]{2,1,0:T(8,128)(2,1)S(1)}, bf16[4,64,512]{2,1,0:T(8,128)(2,1)S(1)}, u32[]{:S(2)}, u32[]{:S(2)}) collective-permute-start(bf16[4,64,512]{2,1,0:T(8,128)(2,1)S(1)} %get-tuple-element.134), channel_id=1, source_target_pairs={{0,2},{1,3},{2,0},{3,1},{4,6},{5,7},{6,4},{7,5},{8,10},{9,11},{10,... | collective-permute-start | bytes 786440 | tf_op jit(solution)/shard_map/ppermute | solution.py:652
  565.9 15.4 %collective-permute-start.39 = (bf16[1,64,512]{2,1,0:T(8,128)(2,1)S(1)}, bf16[1,64,512]{2,1,0:T(8,128)(2,1)S(1)}, u32[]{:S(2)}, u32[]{:S(2)}) collective-permute-start(bf16[1,64,512]{2,1,0:T(8,128)(2,1)S(1)} %get-tuple-element.161), channel_id=1, source_target_pairs={{0,3},{1,0},{2,1},{3,2},{4,7},{5,4},{6,5},{7,6},{8,11},{9,8},{10,9... | collective-permute-start | bytes 196616 | tf_op jit(solution)/shard_map/ppermute | solution.py:652
  568.2 22.4 %collective-permute-start.48 = (bf16[1,4,32,512]{3,2,1,0:T(8,128)(2,1)}, bf16[1,4,32,512]{3,2,1,0:T(8,128)(2,1)}, u32[]{:S(2)}, u32[]{:S(2)}) collective-permute-start(bf16[1,4,32,512]{3,2,1,0:T(8,128)(2,1)} %get-tuple-element.152), channel_id=1, source_target_pairs={{0,8},{4,12},{8,0},{12,4},{16,24},{20,28},{24,16},{28,20},{1,9},{5... | collective-permute-start | bytes 393224 | tf_op jit(solution)/shard_map/ppermute | solution.py:647
  571.5 19.1 %collective-permute-start.49 = (bf16[1,4,32,512]{3,2,1,0:T(8,128)(2,1)}, bf16[1,4,32,512]{3,2,1,0:T(8,128)(2,1)}, u32[]{:S(2)}, u32[]{:S(2)}) collective-permute-start(bf16[1,4,32,512]{3,2,1,0:T(8,128)(2,1)} %get-tuple-element.153), channel_id=1, source_target_pairs={{0,16},{4,20},{8,24},{12,28},{16,0},{20,4},{24,8},{28,12},{1,17},{... | collective-permute-start | bytes 393224 | tf_op jit(solution)/shard_map/ppermute | solution.py:647
  572.6 17.9 %collective-permute-start.50 = (bf16[1,4,32,512]{3,2,1,0:T(8,128)(2,1)}, bf16[1,4,32,512]{3,2,1,0:T(8,128)(2,1)}, u32[]{:S(2)}, u32[]{:S(2)}) collective-permute-start(bf16[1,4,32,512]{3,2,1,0:T(8,128)(2,1)} %get-tuple-element.154), channel_id=1, source_target_pairs={{0,24},{4,28},{8,16},{12,20},{16,8},{20,12},{24,0},{28,4},{1,25},{... | collective-permute-start | bytes 393224 | tf_op jit(solution)/shard_map/ppermute | solution.py:647
  580.2 6.3 collective-permute-start.38
  581.2 6.9 %collective-permute-start.37 = (bf16[1,64,512]{2,1,0:T(8,128)(2,1)S(1)}, bf16[1,64,512]{2,1,0:T(8,128)(2,1)S(1)}, u32[]{:S(2)}, u32[]{:S(2)}) collective-permute-start(bf16[1,64,512]{2,1,0:T(8,128)(2,1)S(1)} %get-tuple-element.163), channel_id=1, source_target_pairs={{0,1},{1,2},{2,3},{3,0},{4,5},{5,6},{6,7},{7,4},{8,9},{9,10},{10,1... | collective-permute-start | bytes 196616 | tf_op jit(solution)/shard_map/ppermute | solution.py:652
  600.5 6.9 %collective-permute-start.56 = (bf16[32,512]{1,0:T(8,128)(2,1)S(1)}, bf16[32,512]{1,0:T(8,128)(2,1)S(1)}, u32[]{:S(2)}, u32[]{:S(2)}) collective-permute-start(bf16[32,512]{1,0:T(8,128)(2,1)S(1)} %bitcast.346), channel_id=1, source_target_pairs={{0,3},{1,0},{2,1},{3,2},{4,7},{5,4},{6,5},{7,6},{8,11},{9,8},{10,9... | collective-permute-start | bytes 98312 | tf_op jit(solution)/shard_map/ppermute | solution.py:652
  603.0 7.8 %collective-permute-start.41 = (f32[8,128]{1,0:T(8,128)S(1)}, f32[8,128]{1,0:T(8,128)S(1)}, u32[]{:S(2)}, u32[]{:S(2)}) collective-permute-start(f32[8,128]{1,0:T(8,128)S(1)} %broadcast_select_fusion.2), channel_id=1, source_target_pairs={{0,2},{1,3},{2,0},{3,1},{4,6},{5,7},{6,4},{7,5},{8,10},{9,11},{10,... | collective-permute-start | bytes 12296 | tf_op jit(solution)/shard_map/ppermute | solution.py:652
  607.9 8.0 %collective-permute-start.58 = (bf16[4,32,512]{2,1,0:T(8,128)(2,1)S(1)}, bf16[4,32,512]{2,1,0:T(8,128)(2,1)S(1)}, u32[]{:S(2)}, u32[]{:S(2)}) collective-permute-start(bf16[4,32,512]{2,1,0:T(8,128)(2,1)S(1)} %get-tuple-element.170), channel_id=1, source_target_pairs={{0,16},{4,20},{8,24},{12,28},{16,0},{20,4},{24,8},{28,12},{1,17},{... | collective-permute-start | bytes 393224 | tf_op jit(solution)/shard_map/ppermute | solution.py:647
  609.9 6.5 collective-permute-start.57
  616.8 11.7 %collective-permute-start.60 = (bf16[512,512]{1,0:T(8,128)(2,1)S(1)}, bf16[512,512]{1,0:T(8,128)(2,1)S(1)}, u32[]{:S(2)}, u32[]{:S(2)}) collective-permute-start(bf16[512,512]{1,0:T(8,128)(2,1)S(1)} %bitcast.341), channel_id=1, source_target_pairs={{0,4},{4,0},{8,12},{12,8},{16,20},{20,16},{24,28},{28,24},{1,5},{5... | collective-permute-start | bytes 1572872 | tf_op jit(solution)/shard_map/ppermute | solution.py:647
  619.5 8.3 %collective-permute-start.46 = (f32[8,128]{1,0:T(8,128)S(1)}, f32[8,128]{1,0:T(8,128)S(1)}, u32[]{:S(2)}, u32[]{:S(2)}) collective-permute-start(f32[8,128]{1,0:T(8,128)S(1)} %add_add_fusion.3), channel_id=1, source_target_pairs={{0,4},{4,0},{8,12},{12,8},{16,20},{20,16},{24,28},{28,24},{1,5},{5... | collective-permute-start | bytes 12296 | tf_op jit(solution)/shard_map/ppermute | solution.py:647
  619.5 28.3 %all-to-all-start.1 = ((bf16[16,64,512]{2,1,0:T(8,128)(2,1)}), bf16[16,64,512]{2,1,0:T(8,128)(2,1)S(1)}, u32[]{:S(2)}, u32[]{:S(2)}) async-start(bf16[16,64,512]{2,1,0:T(8,128)(2,1)} %get-tuple-element.90), calls=%async_computation.1 | async-start | bytes 2097152 | tf_op jit(solution)/shard_map/all_to_all | solution.py:977
  (131 other events, 839.9 us)
Sparse Core Ops, SparseCore 0:
  30.9 114.2 all-gather.4
  152.5 124.9 all-gather.6

commit v2 on v1

--- a/solution.py
+++ b/solution.py
@@ -187,7 +187,7 @@
             jax.ShapeDtypeStruct((HEADS, D), f32),
             jax.ShapeDtypeStruct((8, D), f32),
         ],
-        compiler_params=limit(40),
+        compiler_params=limit(60),
         cost_estimate=cost(6 * TABLE * D * D, 6 * D * D),
         name="fold",
     )(every, every, every, hi, lo, vecs)
@@ -342,6 +342,138 @@
     )(mixed, *[every] * 4, row.reshape(blocks, per, D), col, vecs)
 
 
+def norm_parts(values):
+    center = values - jnp.mean(values, axis=-1, keepdims=True)
+    inverse = lax.rsqrt(jnp.mean(center * center, axis=-1, keepdims=True) + norm_eps)
+    return center * inverse, inverse
+
+
+def norm_grad(grad, normed, inverse, gain):
+    scaled = grad * gain
+    return inverse * (
+        scaled
+        - jnp.mean(scaled, axis=-1, keepdims=True)
+        - normed * jnp.mean(scaled * normed, axis=-1, keepdims=True)
+    )
+
+
+def column_sum(array):
+    return jnp.sum(array, axis=0, keepdims=True)
+
+
+def mlp_kernel(h0_ref, att_ref, wo_ref, one_ref, two_ref, vec_ref, head_ref, target_ref, factor_ref,
+               act_ref, a2_ref, dh2_ref, du_ref, dh1_ref, dh1_low_ref, datt_ref, dhead_ref, sum_ref, loss_ref,
+               h1, acc, grad2, slope):
+    i = pl.program_id(0)
+    folds = slope.shape[0]
+    f = jnp.where(i < folds, i, 2 * folds - 1 - i)
+    gain2, shift2, bias2, gain3, shift3 = [vec_ref[r : r + 1, :] for r in range(5)]
+
+    @pl.when(i == 0)
+    def _():
+        h1[...] = h0_ref[...] + nn(att_ref[...], tile_of(wo_ref))
+        normed, _ = norm_parts(h1[...])
+        a2_ref[...] = (normed * gain2 + shift2).astype(bf16)
+        acc[...] = h1[...] + bias2
+        sum_ref[...] = jnp.zeros_like(sum_ref)
+
+    @pl.when(i < folds)
+    def _():
+        u = nn(a2_ref[...], tile_of(one_ref)) + vec_ref[pl.ds(8 + f, 1), :]
+        phi = 0.5 * (1.0 + lax.erf(u * 0.7071067811865476))
+        slope[f] = phi + u * jnp.exp(-0.5 * u * u) * 0.3989422804014327
+        act = (u * phi).astype(bf16)
+        act_ref[...] = act
+        acc[...] += nn(act, tile_of(two_ref))
+
+    @pl.when(i == folds - 1)
+    def _():
+        normed, inverse = norm_parts(acc[...])
+        z = (normed * gain3 + shift3).astype(bf16)
+        error = nt(z, head_ref[...]) - target_ref[...]
+        weighted = factor_ref[...] * error
+        loss_ref[...] = jnp.broadcast_to(jnp.sum(column_sum(weighted * error), axis=1, keepdims=True), loss_ref.shape)
+        dpred = (2.0 * weighted).astype(bf16)
+        dhead_ref[...] = lax.dot_general(dpred, z, (((0,), (0,)), ((), ())), preferred_element_type=f32)
+        dz = nn(dpred, head_ref[...])
+        sum_ref[1:2, :] = column_sum(dz * normed)
+        sum_ref[2:3, :] = column_sum(dz)
+        grad = norm_grad(dz, normed, inverse, gain3)
+        sum_ref[0:1, :] = column_sum(grad)
+        grad2[...] = grad
+        dh2_ref[...] = grad.astype(bf16)
+        acc[...] = jnp.zeros_like(acc)
+
+    @pl.when(i >= folds)
+    def _():
+        du = nt(dh2_ref[...], tile_of(two_ref)) * slope[f]
+        sum_ref[pl.ds(6 + f, 1), :] = column_sum(du)
+        low = du.astype(bf16)
+        du_ref[...] = low
+        acc[...] += nt(low, tile_of(one_ref))
+
+    @pl.when(i == 2 * folds - 1)
+    def _():
+        normed, inverse = norm_parts(h1[...])
+        grad = acc[...]
+        sum_ref[3:4, :] = column_sum(grad * normed)
+        sum_ref[4:5, :] = column_sum(grad)
+        grad = grad2[...] + norm_grad(grad, normed, inverse, gain2)
+        dh1_ref[...] = grad
+        low = grad.astype(bf16)
+        dh1_low_ref[...] = low
+        datt_ref[...] = nt(low, tile_of(wo_ref)).astype(bf16)
+
+
+def mlp(hidden0, attended, first, second, vecs, head, targets, factor):
+    count, width = targets.shape
+    folds = FF // D
+    fold = lambda i: jnp.where(i < folds, i, 2 * folds - 1 - i)
+    tile = lambda base: pl.BlockSpec(
+        second.shape[:2] + (1,) + second.shape[3:], lambda i: (0, 0, base + fold(i), 0, 0)
+    )
+    fixed = lambda s: pl.BlockSpec(s, lambda i: (0,) * len(s))
+    state = (count, D)
+    return pl.pallas_call(
+        mlp_kernel,
+        grid=(2 * folds,),
+        in_specs=[
+            once(state), once(state), tile_spec(first, 7), tile(0), tile(folds), once(vecs.shape), once(head.shape),
+            once(targets.shape), once(factor.shape),
+        ],
+        out_specs=[
+            pl.BlockSpec(state, lambda i: (0, jnp.minimum(i, folds - 1))),
+            fixed(state),
+            fixed(state),
+            pl.BlockSpec(state, lambda i: (0, jnp.minimum(2 * folds - 1 - i, folds - 1))),
+            fixed(state),
+            fixed(state),
+            fixed(state),
+            fixed(head.shape),
+            fixed((16, D)),
+            fixed((8, 128)),
+        ],
+        out_shape=[
+            jax.ShapeDtypeStruct((count, FF), bf16),
+            jax.ShapeDtypeStruct(state, bf16),
+            jax.ShapeDtypeStruct(state, bf16),
+            jax.ShapeDtypeStruct((count, FF), bf16),
+            jax.ShapeDtypeStruct(state, f32),
+            jax.ShapeDtypeStruct(state, bf16),
+            jax.ShapeDtypeStruct(state, bf16),
+            jax.ShapeDtypeStruct(head.shape, f32),
+            jax.ShapeDtypeStruct((16, D), f32),
+            jax.ShapeDtypeStruct((8, 128), f32),
+        ],
+        scratch_shapes=[
+            pltpu.VMEM(state, f32), pltpu.VMEM(state, f32), pltpu.VMEM(state, f32), pltpu.VMEM((folds,) + state, f32)
+        ],
+        compiler_params=limit(60),
+        cost_estimate=cost(8 * count * D * FF, 20 * D * FF, 2 * count * FF),
+        name="mlp",
+    )(hidden0, attended, first, second, second, vecs, head, targets, factor)
+
+
 def back_kernel(dq_ref, dk_ref, dv_ref, h_ref, dh_ref, w3_ref, w4_ref, w5_ref, w6_ref, vec_ref, g_ref, gm_ref, sum_ref, acc):
     first = pl.program_id(0) == 0
     acc[...] = nt(dk_ref[...], tile_of(w5_ref)) + nt(dv_ref[...], tile_of(w6_ref))
@@ -421,11 +553,11 @@
         grid_spec=pltpu.PrefetchScalarGridSpec(
             num_scalar_prefetch=1,
             grid=(1,),
-            in_specs=[whole(pieces.shape), pl.BlockSpec(memory_space=pl.ANY)],
+            in_specs=[whole(pieces.shape), pl.BlockSpec(memory_space=pltpu.HBM)],
             out_specs=whole(shape),
         ),
         out_shape=jax.ShapeDtypeStruct(shape, pieces.dtype),
-        compiler_params=limit(32),
+        compiler_params=limit(60),
         cost_estimate=cost(0, 4 * pieces.size),
         name="choose",
     )(slot_of, pieces, wait)
@@ -573,7 +705,7 @@
             jax.ShapeDtypeStruct(s, f32) for s in ((8, 128), (HEADS, D), (8, D), w.shape, w.shape, w.shape)
         ],
         scratch_shapes=[pltpu.VMEM((TABLE, D), f32), pltpu.VMEM((32 + PIX * VARS, D), f32)],
-        compiler_params=limit(52),
+        compiler_params=limit(36),
         cost_estimate=cost(8 * TABLE * D * D, 28 * w.size),
         name="tail",
     )(square, every, every, every, *arrays)
@@ -614,29 +746,6 @@
     return lax.dot_general(left, right, (((0,), (0,)), ((), ())), preferred_element_type=f32)
 
 
-def layer_norm(values, gain, shift):
-    center = values - jnp.mean(values, axis=-1, keepdims=True)
-    inverse = lax.rsqrt(jnp.mean(center * center, axis=-1, keepdims=True) + norm_eps)
-    normed = center * inverse
-    return (normed * gain + shift, normed, inverse)
-
-
-def norm_back(grad_out, normed, inverse, gain):
-    scaled = grad_out * gain
-    grad_in = inverse * (
-        scaled
-        - jnp.mean(scaled, axis=-1, keepdims=True)
-        - normed * jnp.mean(scaled * normed, axis=-1, keepdims=True)
-    )
-    return (grad_in, jnp.sum(grad_out * normed, axis=0), jnp.sum(grad_out, axis=0))
-
-
-def gelu_parts(pre_act):
-    phi = 0.5 * (1.0 + lax.erf(pre_act * 0.7071067811865476))
-    slope = phi + pre_act * jnp.exp(-0.5 * pre_act * pre_act) * 0.3989422804014327
-    return pre_act * phi, slope
-
-
 def split_low(values):
     high = lax.reduce_precision(values, 8, 7)
     return high.astype(bf16), (values - high).astype(bf16)
@@ -685,39 +794,9 @@
     return jnp.stack([array] + [shift(array, k) for k in range(1, n)])
 
 
-def place_kernel(ref, out):
-    rows = ref.shape[3]
-    for d in range(ref.shape[1]):
-        for m in range(ref.shape[2]):
-            if len(out.shape) == 2:
-                out[d * rows : (d + 1) * rows, m * D : (m + 1) * D] = ref[0, d, m]
-            else:
-                out[m, d * rows : (d + 1) * rows, :] = ref[0, d, m]
-
-
 def gather(pieces):
     blocks, n_dp = lax.axis_size("blk"), lax.axis_size("dp")
     return lax.all_gather(pieces, ("blk", "dp"), axis=0).reshape((blocks, n_dp) + pieces.shape)
-
-
-def place(every, first, size, wide=False):
-    blocks, n_dp, _, rows, _ = every.shape
-    tall = D // blocks
-    at = first // size
-    if wide:
-        spec, shape = pl.BlockSpec((tall, size * D), lambda z: (z, 0)), (D, size * D)
-    else:
-        spec, shape = pl.BlockSpec((size, tall, D), lambda z: (0, z, 0)), (size, D, D)
-    return pl.pallas_call(
-        place_kernel,
-        grid=(blocks,),
-        in_specs=[pl.BlockSpec((1, n_dp, size, rows, D), lambda z: (z, 0, at, 0, 0))],
-        out_specs=spec,
-        out_shape=jax.ShapeDtypeStruct(shape, bf16),
-        compiler_params=limit(32),
-        cost_estimate=cost(0, 4 * size * D * D),
-        name="place",
-    )(every)
 
 
 class SplitSum:
@@ -842,16 +921,13 @@
         low_rows = tall // n_dp
         pieces = tiles.astype(bf16).reshape(slots, n_dp, low_rows, D)
         pieces = lax.all_to_all(pieces, "dp", 1, 0, tiled=True).reshape(n_tiles, low_rows, D)
-        first = gather(choose(slot_of, pieces, 0, 8, slot_of))
-        weight_out = place(first, 7, 1)[0]
+        first = gather(choose(slot_of, pieces, 0, 8, field_all))
     else:
         slots_low = lax.all_gather(tiles.astype(bf16), "blk", axis=1, tiled=True)
         slots_low = lax.all_gather(slots_low, "dp", axis=0, tiled=True)
         weights = [pick(slots_low, 0, slot_of[m]) for m in range(n_tiles)]
         first = jnp.stack(weights[:8])[None, None]
-        weight_out = weights[7]
-        weight_one = jnp.concatenate(weights[8:12], axis=1)
-        weight_two = jnp.concatenate(weights[12:], axis=0)
+        second = jnp.stack(weights[8:])[None, None]
 
     var_total, group_total = counted[:VARS], counted[VARS : VARS + GROUPS] / blocks
     sample_weight = jnp.sum(group_total) / (GROUPS * jnp.sum(group_hot * group_total))
@@ -872,7 +948,6 @@
     coef, fold_low, fold_low_t, fold_key, query_f = fold(first, embed_hi, embed_lo, fold_vecs)
     if fine:
         second = gather(choose(slot_of, pieces, 8, 8, first))
-        weight_one, weight_two = place(second, 0, 4, True), place(second, 4, 4).reshape(FF, D)
     mixed = mix(field_all, coef, fold_low_t)
 
     row_part, col_part = position_parts()
@@ -886,25 +961,10 @@
     own1_low = normed1_low[:count]
     attended_low, log_total = attend(query_blk, key_all, value_all)
 
-    hidden1 = hidden0[:count] + nn(attended_low, weight_out)
-    normed2_out, normed2, inverse2 = layer_norm(hidden1, extras[10], extras[11])
-    normed2_low = normed2_out.astype(bf16)
-    pre_act = nn(normed2_low, weight_one) + extras[15 : 15 + folds].reshape(FF)
-    activ, slope = gelu_parts(pre_act)
-    activ_low = activ.astype(bf16)
-    hidden2 = hidden1 + nn(activ_low, weight_two) + extras[12]
-    normed3_out, normed3, inverse3 = layer_norm(hidden2, extras[13], extras[14])
-    normed3_low = normed3_out.astype(bf16)
-    error = nt(normed3_low, head_low) - targets[0]
-    loss_local = jnp.sum(factor * error * error)
-    grad_pred_low = (2.0 * factor * error).astype(bf16)
-    grad_head = tn(grad_pred_low, normed3_low)
-    grad_h2, gain3, shift3 = norm_back(nn(grad_pred_low, head_low), normed3, inverse3, extras[13])
-    grad_h2_low = grad_h2.astype(bf16)
-    bias2 = jnp.sum(grad_h2, axis=0)
-    grad_pre = nt(grad_h2_low, weight_two) * slope
-    bias1 = jnp.sum(grad_pre, axis=0).reshape(folds, D)
-    grad_pre_low = grad_pre.astype(bf16)
+    mlp_vecs = jnp.concatenate([extras[10:15], jnp.zeros((3, D), f32), extras[15 : 15 + folds], jnp.zeros((4, D), f32)], axis=0)
+    (activ_low, normed2_low, grad_h2_low, grad_pre_low, grad_h1, grad_h1_low, grad_attended, grad_head, mlp_sums,
+     loss_local) = mlp(hidden0, attended_low, first, second, mlp_vecs, head_low, targets[0], factor)
+    loss_local = loss_local[0, 0]
 
     def weight_grads(left, mine, other):
         sent = tn(left, other).astype(bf16)
@@ -920,15 +980,7 @@
         one_parts = weight_grads(normed2_low, jnp.where(side == 0, left, right), jnp.where(side == 0, right, left))
         two_job = SplitSum(both(two_parts).reshape(folds, D, half), first_order)
         one_job = SplitSum(both(one_parts)[None], second_order)
-    grad_n2 = nt(grad_pre_low, weight_one)
-    grad_h1_norm, gain2, shift2 = norm_back(grad_n2, normed2, inverse2, extras[10])
-    grad_h1 = grad_h2 + grad_h1_norm
-    grad_h1_low = grad_h1.astype(bf16)
-    early = jnp.concatenate(
-        [jnp.stack([bias2, gain3, shift3, gain2, shift2, jnp.zeros_like(bias2)]), bias1, jnp.zeros((6, D), f32), grad_head],
-        axis=0,
-    )
-    grad_attended = nt(grad_h1_low, weight_out).astype(bf16)
+    early = jnp.concatenate([mlp_sums, grad_head], axis=0)
     if fine:
         grad_attended = after(grad_attended, two_job.send(), one_job.send(), early)
     grad_query, grad_keys, grad_values = attend_back(query_blk, key_all, value_all, attended_low, grad_attended, log_total)
@@ -960,8 +1012,8 @@
     if fine:
         edge_job = SplitSum.joined([end_job, pair_job])
         sent = [*edge_job.send_blocks(), two_job.end(), one_job.end()]
+        late_job.step()
         late_job.job.cur = after(late_job.job.cur, *sent)
-        late_job.step()
         agg_job.send_blocks()
         plan = (
             [(12 + f, f, 0) for f in range(folds)],

time: 675 us -> 643 us (0.953)
  matrix products: 88.2 us -> 51.3 us
  Pallas kernels: 190 us -> 216 us
  blocking collectives: 20.3 us -> 0 us
  starting transfers between devices: 68 us -> 87.7 us
  waiting for transfers between devices: 182 us -> 170 us
    dot_general x8 -> x0, matrix products: 38.9 us -> none  [the longest x4 21.1 us: nt(): return lax.dot_general(a, b, NT, preferred_element_type=f32)]
    pallas_call x3 -> x1, Pallas kernels: 12.2 us -> 35.8 us  [mlp(): pl.pallas_call(mlp_kernel, grid=(2 * folds,), in_specs=[once(state), once...]
    all_to_all x1 -> x0, blocking collectives: 20.3 us -> none  [shards(): lax.all_to_all(pieces, 'dp', 1, 0, tiled=True).reshape(n_tiles, low_rows, D)]
    ppermute x27, starting transfers between devices: 35.4 us -> 48.8 us  [shift(): return lax.ppermute(array, 'blk', [(i, (i + step) % n) for i in range(n)])]
    unnamed x232 -> x166, local copies, waits for them, and re-layouts: 34.9 us -> 25.8 us
    ppermute x27, waiting for transfers between devices: 42 us -> 33.9 us  [shift(): return lax.ppermute(array, 'blk', [(i, (i + step) % n) for i in range(n)])]
    ppermute x34, waiting for transfers between devices: 23.4 us -> 16.3 us  [swap(): return lax.ppermute(array, 'dp', [(i, i ^ bit) for i in range(n)])]
    dot_general x15 -> x14, matrix products: 44.7 us -> 46.5 us  [tn(): lax.dot_general(left, right, (((0,), (0,)), ((), ())), preferred_element_...]
  transfers between devices with their start and end apart: 64 -> 65, of which waited for: 24 -> 20; matrix products, arithmetic and copies ran while one was open for 15% -> 15% of each run, Pallas kernels for 26% -> 27%
where the time goes in v2:
time: 643 us; the launch traced here: 639 us
  Pallas kernels  216 us (34%)
  waiting for transfers between devices  170 us (26%)
  starting transfers between devices  87.7 us (14%)
  matrix products  51.3 us (8%)
  local copies, waits for them, and re-layouts  47.1 us (7%)
  other arithmetic  43.8 us (7%)
  between operations  23 us (4%)
    all_gather x2, waiting for transfers between devices, gather(): lax.all_gather(pieces, ('blk', 'dp'), axis=0)  120 us
    ppermute x27, starting transfers between devices, shift(): return lax.ppermute(array, 'blk', [(i, (i + step) % n) for i in range(n)])  48.8 us
    dot_general x14, matrix products, tn(): lax.dot_general(left, right, (((0,), (0,)), ((), ())), preferred_element_...  46.5 us
    pallas_call x1, Pallas kernels, attend_back(): pl.pallas_call(functools.partial(attend_back_kernel, qb), grid=(HEADS //...  45.2 us
    pallas_call x1, Pallas kernels, mlp(): pl.pallas_call(mlp_kernel, grid=(2 * folds,), in_specs=[once(state), once...  35.8 us
    ppermute x27, waiting for transfers between devices, shift(): return lax.ppermute(array, 'blk', [(i, (i + step) % n) for i in range(n)])  33.9 us
    pallas_call x1, Pallas kernels, attend(): pl.pallas_call(functools.partial(attend_kernel, qb), grid=(HEADS // 2,),...  30.9 us
    ppermute x34, starting transfers between devices, swap(): return lax.ppermute(array, 'dp', [(i, i ^ bit) for i in range(n)])  29.2 us
  transfers between devices with their start and end apart: 65, of which 20 were waited for; matrix products, arithmetic and copies ran while one was open for 15% of the time, Pallas kernels for 27%

profile of v2, /device:TPU:0, one launch (start us, length us, event | category | flops | bytes accessed | tf_op | source)
XLA Modules:
  0.0 639.2 jit_solution(4523245404072309569)
XLA Ops:
  10.0 5.2 all-to-all-start
  15.4 3.7 collective-permute-start.2
  20.0 4.3 collective-permute-done.2
  24.3 12.0 %collective-permute-done.1 = bf16[4,48,512]{2,1,0:T(8,128)(2,1)S(1)} collective-permute-done((bf16[4,48,512]{2,1,0:T(8,128)(2,1)S(1)}, bf16[4,48,512]{2,1,0:T(8,128)(2,1)S(1)}, u32[]{:S(2)}, u32[]{:S(2)}) %collective-permute-start.1) | collective-permute-done | bytes 196640 | tf_op jit(solution)/shard_map/ppermute | solution.py:761
  38.3 2.7 choose.2
  41.1 115.5 %all-gather.5.cloned.1.call-done = bf16[256,32,1024]{2,1,0:T(8,128)(2,1)} async-done(((bf16[8,32,1024]{2,1,0:T(8,128)(2,1)}), bf16[256,32,1024]{2,1,0:T(8,128)(2,1)}) %all-gather.5.cloned.1.call-update) | async-done | bytes 16777232 | tf_op jit(solution)/shard_map/all_gather | solution.py:799
  156.6 2.8 choose.3
  194.7 6.6 %fold.1 = (f32[240,128]{1,0:T(8,128)}, bf16[240,1024]{1,0:T(8,128)(2,1)}, bf16[1024,240]{1,0:T(8,128)(2,1)}, f32[16,1024]{1,0:T(8,128)}, f32[8,1024]{1,0:T(8,128)}) custom-call(bf16[4,8,8,32,1024]{4,3,2,1,0:T(8,128)(2,1)} %bitcast.244, bf16[4,8,8,32,1024]{4,3,2,1,0:T(8,128)(2,1)} %bitcast.245, bf16[4,8,8,32,1024]{4,3,2,1,0:T(8,128)(2,1)} %bitcast.246, ...), custom_call_target="tpu_custom_call" | custom-call | flops 1509949440 | bytes 6291456 | tf_op jit(solution)/shard_map/fold/pallas_call | solution.py:178
  203.3 7.5 %mix.1.m_ref = bf16[2048,1024]{1,0:T(8,128)(2,1)S(1)} custom-call(bf16[4,4,48,512]{3,2,1,0:T(8,128)(2,1)S(1)} %copy-done.5, f32[240,128]{1,0:T(8,128)S(1)} %copy-done.17, bf16[1024,240]{1,0:T(8,128)(2,1)S(1)} %copy-done.15), custom_call_target="tpu_custom_call" | custom-call | flops 4026531840 | bytes 8388608 | tf_op jit(solution)/shard_map/mix/pallas_call | solution.py:220
  212.8 23.1 %front.1 = (f32[2048,1024]{1,0:T(8,128)}, bf16[2048,1024]{1,0:T(8,128)(2,1)}, bf16[512,1024]{1,0:T(8,128)(2,1)S(1)}, bf16[2048,1024]{1,0:T(8,128)(2,1)}, bf16[2048,1024]{1,0:T(8,128)(2,1)}) custom-call(bf16[2048,1024]{1,0:T(8,128)(2,1)} %copy-done.3, bf16[4,8,8,32,1024]{4,3,2,1,0:T(8,128)(2,1)} %bitcast.247, bf16[4,8,8,32,1024]{4,3,2,1,0:T(8,128)(2,1)} %bitcast.248, ...), custom_call_target="tpu_custom_call" | custom-call | flops 12884901888 | bytes 33554432 | tf_op jit(solution)/shard_map/front/pallas_call | solution.py:321
  235.9 30.9 %attend.1 = (bf16[512,1024]{1,0:T(8,128)(2,1)S(1)}, f32[512,128]{1,0:T(8,128)S(1)}) custom-call(bf16[512,1024]{1,0:T(8,128)(2,1)S(1)} %get-tuple-element.65.q_ref, bf16[2048,1024]{1,0:T(8,128)(2,1)} %get-tuple-element.66.k_ref, bf16[2048,1024]{1,0:T(8,128)(2,1)} %get-tuple-element.67.v_ref), custom_call_target="tpu_custom_call" | custom-call | flops 17179869184 | bytes 16777216 | tf_op jit(solution)/shard_map/attend/pallas_call | solution.py:88
  268.8 4.3 all-gather.7.cloned.1.call-done
  273.1 35.8 %mlp.1 = (bf16[512,4096]{1,0:T(8,128)(2,1)}, bf16[512,1024]{1,0:T(8,128)(2,1)}, bf16[512,1024]{1,0:T(8,128)(2,1)}, bf16[512,4096]{1,0:T(8,128)(2,1)}, f32[512,10...) custom-call(f32[2048,1024]{1,0:T(8,128)} %get-tuple-element.64.h0_re, ...), custom_call_target="tpu_custom_call" | custom-call | flops 17179869184 | bytes 83886080 | tf_op jit(solution)/shard_map/mlp/pallas_call | solution.py:437
  308.9 7.0 %convolution_convert_fusion = bf16[4096,512]{1,0:T(8,128)(2,1)} fusion(bf16[512,4096]{1,0:T(8,128)(2,1)} %get-tuple-element.69, pred[]{:T(512)S(6)} %eq.112, bf16[512,1024]{1,0:T(8,128)(2,1)} %get-tuple-element.70), kind=kOutput, calls=%fused_computation.2 | convolution fusion | flops 2149842944 | bytes 9437185 | tf_op jit(solution)/shard_map/dot_general | solution.py:746
  317.4 5.2 convolution_convert_fusion.1
  325.7 2.6 fusion.73.gram_ref
  331.7 2.6 convert_add_fusion.5
  334.3 4.8 convert_add_fusion.1
  339.1 3.3 copy-done.23
  344.6 5.7 convert_add_fusion
  354.8 45.2 %attend_back.1 = (bf16[512,1024]{1,0:T(8,128)(2,1)S(1)}, bf16[2048,1024]{1,0:T(8,128)(2,1)}, bf16[2048,1024]{1,0:T(8,128)(2,1)}) custom-call(bf16[512,1024]{1,0:T(8,128)(2,1)S(1)} %copy-done.14, bf16[2048,1024]{1,0:T(8,128)(2,1)} %get-tuple-element.66.k_ref, bf16[2048,1024]{1,0:T(8,128)(2,1)} %get-tuple-element.67.v_ref, bf16[512,1024]{1,0:T(8,128)(2,1)S(1)} %copy-done.21, ...), custom_call_target="tpu_custom_call" | custom-call | flops 42949672960 | bytes 33554432 | tf_op jit(solution)/shard_map/attend_back/pallas_call | solution.py:141
  400.1 3.9 bitcast_add_fusion.1
  405.7 2.6 bitcast_add_fusion
  411.6 2.4 fusion.52
  414.1 2.4 fusion.55
  420.7 2.4 convert_add_fusion.4
  423.1 2.8 convert_add_fusion.3
  428.7 5.9 collective-permute-done.18
  437.7 29.1 %back.1 = (bf16[2048,1024]{1,0:T(8,128)(2,1)}, bf16[2048,1024]{1,0:T(8,128)(2,1)}, f32[8,1024]{1,0:T(8,128)S(1)}) custom-call(bf16[512,1024]{1,0:T(8,128)(2,1)S(1)} %get-tuple-element.84.dq_ref, bf16[2048,1024]{1,0:T(8,128)(2,1)} %get-tuple-element.82.dk_ref, bf16[2048,1024]{1,0:T(8,128)(2,1)} %get-tuple-element.83.dv_ref, ...), custom_call_target="tpu_custom_call" | custom-call | flops 15032385536 | bytes 33554432 | tf_op jit(solution)/shard_map/back/pallas_call | solution.py:518
  470.5 2.2 collective-permute-start.15
  473.4 4.6 collective-permute-done.19
  478.0 9.3 %collective-permute-start.13 = (bf16[4,64,512]{2,1,0:T(8,128)(2,1)S(1)}, bf16[4,64,512]{2,1,0:T(8,128)(2,1)S(1)}, u32[]{:S(2)}, u32[]{:S(2)}) collective-permute-start(bf16[4,64,512]{2,1,0:T(8,128)(2,1)S(1)} %get-tuple-element.144), channel_id=1, source_target_pairs={{0,1},{1,2},{2,3},{3,0},{4,5},{5,6},{6,7},{7,4},{8,9},{9,10},{10,1... | collective-permute-start | bytes 786440 | tf_op jit(solution)/shard_map/ppermute | solution.py:761
  496.4 3.4 fusion.58
  501.9 17.9 %mix_back.1 = (f32[512,512]{1,0:T(8,128)S(1)}, bf16[512,512]{1,0:T(8,128)(2,1)S(1)}) custom-call(s32[1]{0:T(128)} %bitcast.72.side_ref, bf16[4,4,48,512]{3,2,1,0:T(8,128)(2,1)S(1)} %copy-done.5, f32[240,128]{1,0:T(8,128)S(1)} %copy-done.18, bf16[240,1024]{1,0:T(8,128)(2,1)S(1)} %copy-done.16, bf16[2048,1024]{1,0:T(8,128)(2,1)S(1)} %copy-done.12, ...), custom_call_target="tpu_custom_call" | custom-call | flops 8053063680 | bytes 8388608 | tf_op jit(solution)/shard_map/mix_back/pallas_call | solution.py:279
  520.0 4.6 convert_add_fusion.2
  528.6 2.7 collective-permute-start.30
  531.4 3.6 collective-permute-done.36
  537.0 2.5 collective-permute-done.35
  540.1 2.2 collective-permute-start.37
  545.1 2.8 collective-permute-start.39
  547.9 3.8 collective-permute-done.31.refs_4_
  553.3 2.8 collective-permute-done.32.refs_5_
  563.9 5.4 collective-permute-start.53
  571.2 2.8 collective-permute-done.52
  592.5 4.5 all-to-all-start.1
  602.2 2.7 fusion.170
  606.5 12.9 %tail.1 = (f32[8,128]{1,0:T(8,128)S(1)}, f32[16,1024]{1,0:T(8,128)S(1)}, f32[8,1024]{1,0:T(8,128)S(1)}, f32[499,1024]{1,0:T(8,128)}, f32[499,1024]{1,0:T(8,128)}, /*index=5*/f32[499,1024]{1,0:T(8,128)}) custom-call(f32[1]{0:T(128)} %get-tuple-element.186.square_ref, bf16[4,8,8,32,1024]{4,3,2,1,0:T(8,128)(2,1)} %bitcast.256, ...), custom_call_target="tpu_custom_call" | custom-call | flops 2013265920 | bytes 14307328 | tf_op jit(solution)/shard_map/tail/pallas_call | solution.py:698
  627.4 4.8 multiply_subtract_fusion
  (404 shorter events, 138.6 us)
Async XLA Ops:
  10.0 27.3 %all-to-all-start = ((bf16[2,8,32,1024]{3,2,0,1:T(8,128)(2,1)}), bf16[2,8,32,1024]{3,2,0,1:T(8,128)(2,1)S(1)}, u32[]{:S(2)}, u32[]{:S(2)}) async-start(bf16[2,8,32,1024]{3,2,0,1:T(8,128)(2,1)} %copy.74), calls=%async_computation | async-start | bytes 2097152 | tf_op jit(solution)/shard_map/all_to_all | solution.py:923
  15.2 141.4 %all-gather.5.cloned.1.call-start = ((), (), s32[]{:S(2)}) async-start(), calls=%async_computation.2 | async-start | bytes 17301504 | tf_op jit(solution)/shard_map/all_gather | solution.py:799
  15.4 9.0 %collective-permute-start.2 = (bf16[4,48,512]{2,1,0:T(8,128)(2,1)S(1)}, bf16[4,48,512]{2,1,0:T(8,128)(2,1)S(1)}, u32[]{:S(2)}, u32[]{:S(2)}) collective-permute-start(bf16[4,48,512]{2,1,0:T(8,128)(2,1)S(1)} %bitcast.288), channel_id=1, source_target_pairs={{0,3},{1,0},{2,1},{3,2},{4,7},{5,4},{6,5},{7,6},{8,11},{9,8},{10,9... | collective-permute-start | bytes 589832 | tf_op jit(solution)/shard_map/ppermute | solution.py:761
  19.0 17.3 %collective-permute-start.1 = (bf16[4,48,512]{2,1,0:T(8,128)(2,1)S(1)}, bf16[4,48,512]{2,1,0:T(8,128)(2,1)S(1)}, u32[]{:S(2)}, u32[]{:S(2)}) collective-permute-start(bf16[4,48,512]{2,1,0:T(8,128)(2,1)S(1)} %bitcast.289), channel_id=1, source_target_pairs={{0,2},{1,3},{2,0},{3,1},{4,6},{5,7},{6,4},{7,5},{8,10},{9,11},{10,... | collective-permute-start | bytes 589832 | tf_op jit(solution)/shard_map/ppermute | solution.py:761
  19.0 17.3 %collective-permute-start = (bf16[4,48,512]{2,1,0:T(8,128)(2,1)S(1)}, bf16[4,48,512]{2,1,0:T(8,128)(2,1)S(1)}, u32[]{:S(2)}, u32[]{:S(2)}) collective-permute-start(bf16[4,48,512]{2,1,0:T(8,128)(2,1)S(1)} %bitcast.290), channel_id=1, source_target_pairs={{0,1},{1,2},{2,3},{3,0},{4,5},{5,6},{6,7},{7,4},{8,9},{9,10},{10,1... | collective-permute-start | bytes 589832 | tf_op jit(solution)/shard_map/ppermute | solution.py:761
  41.0 232.1 %all-gather.7.cloned.1.call-start = ((), (), s32[]{:S(2)}) async-start(), calls=%async_computation.3 | async-start | bytes 17301504 | tf_op jit(solution)/shard_map/all_gather | solution.py:799
  161.4 9.7 %collective-permute-start.5 = (f32[64,128]{1,0:T(8,128)S(1)}, f32[64,128]{1,0:T(8,128)S(1)}, u32[]{:S(2)}, u32[]{:S(2)}) collective-permute-start(f32[64,128]{1,0:T(8,128)S(1)} %broadcast_select_fusion.1), channel_id=1, source_target_pairs={{0,3},{1,0},{2,1},{3,2},{4,7},{5,4},{6,5},{7,6},{8,11},{9,8},{10,9... | collective-permute-start | bytes 98312 | tf_op jit(solution)/shard_map/ppermute | solution.py:761
  162.9 8.3 %collective-permute-start.4 = (f32[64,128]{1,0:T(8,128)S(1)}, f32[64,128]{1,0:T(8,128)S(1)}, u32[]{:S(2)}, u32[]{:S(2)}) collective-permute-start(f32[64,128]{1,0:T(8,128)S(1)} %broadcast_select_fusion.1), channel_id=1, source_target_pairs={{0,2},{1,3},{2,0},{3,1},{4,6},{5,7},{6,4},{7,5},{8,10},{9,11},{10,... | collective-permute-start | bytes 98312 | tf_op jit(solution)/shard_map/ppermute | solution.py:761
  163.3 8.5 %collective-permute-start.3 = (f32[64,128]{1,0:T(8,128)S(1)}, f32[64,128]{1,0:T(8,128)}, u32[]{:S(2)}, u32[]{:S(2)}) collective-permute-start(f32[64,128]{1,0:T(8,128)S(1)} %broadcast_select_fusion.1), channel_id=1, source_target_pairs={{0,1},{1,2},{2,3},{3,0},{4,5},{5,6},{6,7},{7,4},{8,9},{9,10},{10,1... | collective-permute-start | bytes 98312 | tf_op jit(solution)/shard_map/ppermute | solution.py:761
  172.7 7.7 %collective-permute-start.8 = (f32[64,128]{1,0:T(8,128)S(1)}, f32[64,128]{1,0:T(8,128)S(1)}, u32[]{:S(2)}, u32[]{:S(2)}) collective-permute-start(f32[64,128]{1,0:T(8,128)S(1)} %add_add_fusion.1), channel_id=1, source_target_pairs={{0,24},{4,28},{8,16},{12,20},{16,8},{20,12},{24,0},{28,4},{1,25},{... | collective-permute-start | bytes 98312 | tf_op jit(solution)/shard_map/ppermute | solution.py:756
  181.9 8.6 %collective-permute-start.9 = (f32[64,128]{1,0:T(8,128)S(1)}, f32[64,128]{1,0:T(8,128)S(1)}, u32[]{:S(2)}, u32[]{:S(2)}) collective-permute-start(f32[64,128]{1,0:T(8,128)S(1)} %add_add_fusion), channel_id=1, source_target_pairs={{0,4},{4,0},{8,12},{12,8},{16,20},{20,16},{24,28},{28,24},{1,5},{5... | collective-permute-start | bytes 98312 | tf_op jit(solution)/shard_map/ppermute | solution.py:756
  315.9 18.4 %collective-permute-start.10 = (bf16[4096,512]{1,0:T(8,128)(2,1)}, bf16[4096,512]{1,0:T(8,128)(2,1)}, u32[]{:S(2)}, u32[]{:S(2)}) collective-permute-start(bf16[4096,512]{1,0:T(8,128)(2,1)} %convolution_convert_fusion), channel_id=1, source_target_pairs={{0,4},{4,0},{8,12},{12,8},{16,20},{20,16},{24,28},{28,24},{1,5},{5... | collective-permute-start | bytes 12582920 | tf_op jit(solution)/shard_map/ppermute | solution.py:756
  322.6 21.5 %collective-permute-start.16 = (bf16[1024,2048]{1,0:T(8,128)(2,1)}, bf16[1024,2048]{1,0:T(8,128)(2,1)}, u32[]{:S(2)}, u32[]{:S(2)}) collective-permute-start(bf16[1024,2048]{1,0:T(8,128)(2,1)} %convolution_convert_fusion.1), channel_id=1, source_target_pairs={{0,4},{4,0},{8,12},{12,8},{16,20},{20,16},{24,28},{28,24},{1,5},{5... | collective-permute-start | bytes 12582920 | tf_op jit(solution)/shard_map/ppermute | solution.py:756
  324.7 7.0 %collective-permute-start.23 = (bf16[1024,512]{1,0:T(8,128)(2,1)}, bf16[1024,512]{1,0:T(8,128)(2,1)}, u32[]{:S(2)}, u32[]{:S(2)}) collective-permute-start(bf16[1024,512]{1,0:T(8,128)(2,1)} %convolution_convert_fusion.2), channel_id=1, source_target_pairs={{0,4},{4,0},{8,12},{12,8},{16,20},{20,16},{24,28},{28,24},{1,5},{5... | collective-permute-start | bytes 3145736 | tf_op jit(solution)/shard_map/ppermute | solution.py:756
  342.8 57.3 %collective-permute-start.11 = (bf16[4,4,2,64,512]{4,3,0,1,2:T(8,128)(2,1)S(1)}, bf16[4,4,2,64,512]{4,3,0,1,2:T(8,128)(2,1)}, u32[]{:S(2)}, u32[]{:S(2)}) collective-permute-start(bf16[4,4,2,64,512]{4,3,0,1,2:T(8,128)(2,1)S(1)} %fusion.1), channel_id=1, source_target_pairs={{0,8},{4,12},{8,0},{12,4},{16,24},{20,28},{24,16},{28,20},{1,9},{5... | collective-permute-start | bytes 6291464 | tf_op jit(solution)/shard_map/ppermute | solution.py:756
  352.0 53.7 %collective-permute-start.17 = (bf16[1,4,2,64,2048]{4,3,1,2,0:T(8,128)(2,1)}, bf16[1,4,2,64,2048]{4,3,1,2,0:T(8,128)(2,1)}, u32[]{:S(2)}, u32[]{:S(2)}) collective-permute-start(bf16[1,4,2,64,2048]{4,3,1,2,0:T(8,128)(2,1)} %fusion.2), channel_id=1, source_target_pairs={{0,16},{4,20},{8,24},{12,28},{16,0},{20,4},{24,8},{28,12},{1,17},{... | collective-permute-start | bytes 6291464 | tf_op jit(solution)/shard_map/ppermute | solution.py:756
  404.2 62.6 %collective-permute-start.12 = (bf16[4,4,64,512]{3,2,0,1:T(8,128)(2,1)S(1)}, bf16[4,4,64,512]{3,2,0,1:T(8,128)(2,1)}, u32[]{:S(2)}, u32[]{:S(2)}) collective-permute-start(bf16[4,4,64,512]{3,2,0,1:T(8,128)(2,1)S(1)} %fusion.63), channel_id=1, source_target_pairs={{0,16},{4,20},{8,24},{12,28},{16,0},{20,4},{24,8},{28,12},{1,17},{... | collective-permute-start | bytes 3145736 | tf_op jit(solution)/shard_map/ppermute | solution.py:756
  408.5 26.1 %collective-permute-start.18 = (bf16[1,4,64,2048]{3,2,1,0:T(8,128)(2,1)S(1)}, bf16[1,4,64,2048]{3,2,1,0:T(8,128)(2,1)S(1)}, u32[]{:S(2)}, u32[]{:S(2)}) collective-permute-start(bf16[1,4,64,2048]{3,2,1,0:T(8,128)(2,1)S(1)} %fusion.64), channel_id=1, source_target_pairs={{0,8},{4,12},{8,0},{12,4},{16,24},{20,28},{24,16},{28,20},{1,9},{5... | collective-permute-start | bytes 3145736 | tf_op jit(solution)/shard_map/ppermute | solution.py:756
  410.2 6.8 %collective-permute-start.22 = (bf16[1024,512]{1,0:T(8,128)(2,1)S(1)}, bf16[1024,512]{1,0:T(8,128)(2,1)S(1)}, u32[]{:S(2)}, u32[]{:S(2)}) collective-permute-start(bf16[1024,512]{1,0:T(8,128)(2,1)S(1)} %convolution_convert_fusion.3), channel_id=1, source_target_pairs={{0,4},{4,0},{8,12},{12,8},{16,20},{20,16},{24,28},{28,24},{1,5},{5... | collective-permute-start | bytes 3145736 | tf_op jit(solution)/shard_map/ppermute | solution.py:756
  414.0 6.6 %collective-permute-start.26 = (bf16[1024,512]{1,0:T(8,128)(2,1)S(1)}, bf16[1024,512]{1,0:T(8,128)(2,1)S(1)}, u32[]{:S(2)}, u32[]{:S(2)}) collective-permute-start(bf16[1024,512]{1,0:T(8,128)(2,1)S(1)} %fusion.52), channel_id=1, source_target_pairs={{0,4},{4,0},{8,12},{12,8},{16,20},{20,16},{24,28},{28,24},{1,5},{5... | collective-permute-start | bytes 3145736 | tf_op jit(solution)/shard_map/ppermute | solution.py:756
  419.5 69.1 %collective-permute-start.24 = (bf16[2,4,2,64,512]{4,3,0,1,2:T(8,128)(2,1)}, bf16[2,4,2,64,512]{4,3,0,1,2:T(8,128)(2,1)}, u32[]{:S(2)}, u32[]{:S(2)}) collective-permute-start(bf16[2,4,2,64,512]{4,3,0,1,2:T(8,128)(2,1)} %fusion.65), channel_id=1, source_target_pairs={{0,8},{4,12},{8,0},{12,4},{16,24},{20,28},{24,16},{28,20},{1,9},{5... | collective-permute-start | bytes 3145736 | tf_op jit(solution)/shard_map/ppermute | solution.py:756
  427.6 65.0 %collective-permute-start.28 = (bf16[2,4,2,64,512]{4,3,0,1,2:T(8,128)(2,1)}, bf16[2,4,2,64,512]{4,3,0,1,2:T(8,128)(2,1)}, u32[]{:S(2)}, u32[]{:S(2)}) collective-permute-start(bf16[2,4,2,64,512]{4,3,0,1,2:T(8,128)(2,1)} %fusion.66), channel_id=1, source_target_pairs={{0,16},{4,20},{8,24},{12,28},{16,0},{20,4},{24,8},{28,12},{1,17},{... | collective-permute-start | bytes 3145736 | tf_op jit(solution)/shard_map/ppermute | solution.py:756
  435.8 34.7 %collective-permute-start.21 = (bf16[1,64,2048]{2,1,0:T(8,128)(2,1)}, bf16[1,64,2048]{2,1,0:T(8,128)(2,1)}, u32[]{:S(2)}, u32[]{:S(2)}) collective-permute-start(bf16[1,64,2048]{2,1,0:T(8,128)(2,1)} %get-tuple-element.142), channel_id=1, source_target_pairs={{0,3},{1,0},{2,1},{3,2},{4,7},{5,4},{6,5},{7,6},{8,11},{9,8},{10,9... | collective-permute-start | bytes 786440 | tf_op jit(solution)/shard_map/ppermute | solution.py:761
  437.3 35.4 %collective-permute-start.20 = (bf16[1,64,2048]{2,1,0:T(8,128)(2,1)S(1)}, bf16[1,64,2048]{2,1,0:T(8,128)(2,1)}, u32[]{:S(2)}, u32[]{:S(2)}) collective-permute-start(bf16[1,64,2048]{2,1,0:T(8,128)(2,1)S(1)} %get-tuple-element.143), channel_id=1, source_target_pairs={{0,2},{1,3},{2,0},{3,1},{4,6},{5,7},{6,4},{7,5},{8,10},{9,11},{10,... | collective-permute-start | bytes 786440 | tf_op jit(solution)/shard_map/ppermute | solution.py:761
  466.8 11.2 %collective-permute-start.19 = (bf16[1,64,2048]{2,1,0:T(8,128)(2,1)S(1)}, bf16[1,64,2048]{2,1,0:T(8,128)(2,1)S(1)}, u32[]{:S(2)}, u32[]{:S(2)}) collective-permute-start(bf16[1,64,2048]{2,1,0:T(8,128)(2,1)S(1)} %get-tuple-element.141), channel_id=1, source_target_pairs={{0,1},{1,2},{2,3},{3,0},{4,5},{5,6},{6,7},{7,4},{8,9},{9,10},{10,1... | collective-permute-start | bytes 786440 | tf_op jit(solution)/shard_map/ppermute | solution.py:761
  470.5 29.3 %collective-permute-start.15 = (bf16[4,64,512]{2,1,0:T(8,128)(2,1)S(1)}, bf16[4,64,512]{2,1,0:T(8,128)(2,1)S(1)}, u32[]{:S(2)}, u32[]{:S(2)}) collective-permute-start(bf16[4,64,512]{2,1,0:T(8,128)(2,1)S(1)} %get-tuple-element.145), channel_id=1, source_target_pairs={{0,3},{1,0},{2,1},{3,2},{4,7},{5,4},{6,5},{7,6},{8,11},{9,8},{10,9... | collective-permute-start | bytes 786440 | tf_op jit(solution)/shard_map/ppermute | solution.py:761
  472.7 27.1 %collective-permute-start.14 = (bf16[4,64,512]{2,1,0:T(8,128)(2,1)S(1)}, bf16[4,64,512]{2,1,0:T(8,128)(2,1)S(1)}, u32[]{:S(2)}, u32[]{:S(2)}) collective-permute-start(bf16[4,64,512]{2,1,0:T(8,128)(2,1)S(1)} %get-tuple-element.146), channel_id=1, source_target_pairs={{0,2},{1,3},{2,0},{3,1},{4,6},{5,7},{6,4},{7,5},{8,10},{9,11},{10,... | collective-permute-start | bytes 786440 | tf_op jit(solution)/shard_map/ppermute | solution.py:761
  478.0 21.8 %collective-permute-start.13 = (bf16[4,64,512]{2,1,0:T(8,128)(2,1)S(1)}, bf16[4,64,512]{2,1,0:T(8,128)(2,1)S(1)}, u32[]{:S(2)}, u32[]{:S(2)}) collective-permute-start(bf16[4,64,512]{2,1,0:T(8,128)(2,1)S(1)} %get-tuple-element.144), channel_id=1, source_target_pairs={{0,1},{1,2},{2,3},{3,0},{4,5},{5,6},{6,7},{7,4},{8,9},{9,10},{10,1... | collective-permute-start | bytes 786440 | tf_op jit(solution)/shard_map/ppermute | solution.py:761
  499.8 20.2 %collective-permute-start.33 = (bf16[1024,512]{1,0:T(8,128)(2,1)}, bf16[1024,512]{1,0:T(8,128)(2,1)S(1)}, u32[]{:S(2)}, u32[]{:S(2)}) collective-permute-start(bf16[1024,512]{1,0:T(8,128)(2,1)} %fusion.58), channel_id=1, source_target_pairs={{0,4},{4,0},{8,12},{12,8},{16,20},{20,16},{24,28},{28,24},{1,5},{5... | collective-permute-start | bytes 3145736 | tf_op jit(solution)/shard_map/ppermute | solution.py:756
  499.9 19.8 %collective-permute-start.25 = (bf16[2,4,64,512]{3,2,0,1:T(8,128)(2,1)}, bf16[2,4,64,512]{3,2,0,1:T(8,128)(2,1)S(1)}, u32[]{:S(2)}, u32[]{:S(2)}) collective-permute-start(bf16[2,4,64,512]{3,2,0,1:T(8,128)(2,1)} %fusion.74), channel_id=1, source_target_pairs={{0,16},{4,20},{8,24},{12,28},{16,0},{20,4},{24,8},{28,12},{1,17},{... | collective-permute-start | bytes 1572872 | tf_op jit(solution)/shard_map/ppermute | solution.py:756
  500.8 27.5 %collective-permute-start.29 = (bf16[2,4,64,512]{3,2,0,1:T(8,128)(2,1)S(1)}, bf16[2,4,64,512]{3,2,0,1:T(8,128)(2,1)S(1)}, u32[]{:S(2)}, u32[]{:S(2)}) collective-permute-start(bf16[2,4,64,512]{3,2,0,1:T(8,128)(2,1)S(1)} %fusion.75), channel_id=1, source_target_pairs={{0,8},{4,12},{8,0},{12,4},{16,24},{20,28},{24,16},{28,20},{1,9},{5... | collective-permute-start | bytes 1572872 | tf_op jit(solution)/shard_map/ppermute | solution.py:756
  524.7 10.2 %collective-permute-start.36 = (bf16[1,4,64,512]{3,2,1,0:T(8,128)(2,1)S(1)}, bf16[1,4,64,512]{3,2,1,0:T(8,128)(2,1)S(1)}, u32[]{:S(2)}, u32[]{:S(2)}) collective-permute-start(bf16[1,4,64,512]{3,2,1,0:T(8,128)(2,1)S(1)} %get-tuple-element.137), channel_id=1, source_target_pairs={{0,24},{4,28},{8,16},{12,20},{16,8},{20,12},{24,0},{28,4},{1,25},{... | collective-permute-start | bytes 786440 | tf_op jit(solution)/shard_map/ppermute | solution.py:756
  526.4 13.1 %collective-permute-start.35 = (bf16[1,4,64,512]{3,2,1,0:T(8,128)(2,1)S(1)}, bf16[1,4,64,512]{3,2,1,0:T(8,128)(2,1)S(1)}, u32[]{:S(2)}, u32[]{:S(2)}) collective-permute-start(bf16[1,4,64,512]{3,2,1,0:T(8,128)(2,1)S(1)} %get-tuple-element.136), channel_id=1, source_target_pairs={{0,16},{4,20},{8,24},{12,28},{16,0},{20,4},{24,8},{28,12},{1,17},{... | collective-permute-start | bytes 786440 | tf_op jit(solution)/shard_map/ppermute | solution.py:756
  527.2 12.7 %collective-permute-start.34 = (bf16[1,4,64,512]{3,2,1,0:T(8,128)(2,1)S(1)}, bf16[1,4,64,512]{3,2,1,0:T(8,128)(2,1)S(1)}, u32[]{:S(2)}, u32[]{:S(2)}) collective-permute-start(bf16[1,4,64,512]{3,2,1,0:T(8,128)(2,1)S(1)} %get-tuple-element.135), channel_id=1, source_target_pairs={{0,8},{4,12},{8,0},{12,4},{16,24},{20,28},{24,16},{28,20},{1,9},{5... | collective-permute-start | bytes 786440 | tf_op jit(solution)/shard_map/ppermute | solution.py:756
  528.5 13.9 %collective-permute-start.47 = (bf16[512,512]{1,0:T(8,128)(2,1)S(1)}, bf16[512,512]{1,0:T(8,128)(2,1)S(1)}, u32[]{:S(2)}, u32[]{:S(2)}) collective-permute-start(bf16[512,512]{1,0:T(8,128)(2,1)S(1)} %get-tuple-element.104), channel_id=1, source_target_pairs={{0,4},{4,0},{8,12},{12,8},{16,20},{20,16},{24,28},{28,24},{1,5},{5... | collective-permute-start | bytes 1572872 | tf_op jit(solution)/shard_map/ppermute | solution.py:756
  528.6 16.3 %collective-permute-start.30 = (bf16[4,64,512]{2,1,0:T(8,128)(2,1)S(1)}, bf16[4,64,512]{2,1,0:T(8,128)(2,1)S(1)}, u32[]{:S(2)}, u32[]{:S(2)}) collective-permute-start(bf16[4,64,512]{2,1,0:T(8,128)(2,1)S(1)} %get-tuple-element.139), channel_id=1, source_target_pairs={{0,1},{1,2},{2,3},{3,0},{4,5},{5,6},{6,7},{7,4},{8,9},{9,10},{10,1... | collective-permute-start | bytes 786440 | tf_op jit(solution)/shard_map/ppermute | solution.py:761
  534.9 16.9 %collective-permute-start.31 = (bf16[4,64,512]{2,1,0:T(8,128)(2,1)S(1)}, bf16[4,64,512]{2,1,0:T(8,128)(2,1)S(1)}, u32[]{:S(2)}, u32[]{:S(2)}) collective-permute-start(bf16[4,64,512]{2,1,0:T(8,128)(2,1)S(1)} %get-tuple-element.140), channel_id=1, source_target_pairs={{0,2},{1,3},{2,0},{3,1},{4,6},{5,7},{6,4},{7,5},{8,10},{9,11},{10,... | collective-permute-start | bytes 786440 | tf_op jit(solution)/shard_map/ppermute | solution.py:761
  539.5 16.7 %collective-permute-start.32 = (bf16[4,64,512]{2,1,0:T(8,128)(2,1)S(1)}, bf16[4,64,512]{2,1,0:T(8,128)(2,1)S(1)}, u32[]{:S(2)}, u32[]{:S(2)}) collective-permute-start(bf16[4,64,512]{2,1,0:T(8,128)(2,1)S(1)} %get-tuple-element.138), channel_id=1, source_target_pairs={{0,3},{1,0},{2,1},{3,2},{4,7},{5,4},{6,5},{7,6},{8,11},{9,8},{10,9... | collective-permute-start | bytes 786440 | tf_op jit(solution)/shard_map/ppermute | solution.py:761
  540.1 16.8 %collective-permute-start.37 = (bf16[1,64,512]{2,1,0:T(8,128)(2,1)S(1)}, bf16[1,64,512]{2,1,0:T(8,128)(2,1)S(1)}, u32[]{:S(2)}, u32[]{:S(2)}) collective-permute-start(bf16[1,64,512]{2,1,0:T(8,128)(2,1)S(1)} %get-tuple-element.162), channel_id=1, source_target_pairs={{0,1},{1,2},{2,3},{3,0},{4,5},{5,6},{6,7},{7,4},{8,9},{9,10},{10,1... | collective-permute-start | bytes 196616 | tf_op jit(solution)/shard_map/ppermute | solution.py:761
  542.3 18.1 %collective-permute-start.38 = (bf16[1,64,512]{2,1,0:T(8,128)(2,1)S(1)}, bf16[1,64,512]{2,1,0:T(8,128)(2,1)S(1)}, u32[]{:S(2)}, u32[]{:S(2)}) collective-permute-start(bf16[1,64,512]{2,1,0:T(8,128)(2,1)S(1)} %get-tuple-element.161), channel_id=1, source_target_pairs={{0,2},{1,3},{2,0},{3,1},{4,6},{5,7},{6,4},{7,5},{8,10},{9,11},{10,... | collective-permute-start | bytes 196616 | tf_op jit(solution)/shard_map/ppermute | solution.py:761
  545.1 15.3 %collective-permute-start.39 = (bf16[1,64,512]{2,1,0:T(8,128)(2,1)S(1)}, bf16[1,64,512]{2,1,0:T(8,128)(2,1)S(1)}, u32[]{:S(2)}, u32[]{:S(2)}) collective-permute-start(bf16[1,64,512]{2,1,0:T(8,128)(2,1)S(1)} %get-tuple-element.160), channel_id=1, source_target_pairs={{0,3},{1,0},{2,1},{3,2},{4,7},{5,4},{6,5},{7,6},{8,11},{9,8},{10,9... | collective-permute-start | bytes 196616 | tf_op jit(solution)/shard_map/ppermute | solution.py:761
  551.8 11.9 %collective-permute-start.50 = (bf16[1,4,32,512]{3,2,1,0:T(8,128)(2,1)}, bf16[1,4,32,512]{3,2,1,0:T(8,128)(2,1)S(1)}, u32[]{:S(2)}, u32[]{:S(2)}) collective-permute-start(bf16[1,4,32,512]{3,2,1,0:T(8,128)(2,1)} %get-tuple-element.152), channel_id=1, source_target_pairs={{0,24},{4,28},{8,16},{12,20},{16,8},{20,12},{24,0},{28,4},{1,25},{... | collective-permute-start | bytes 393224 | tf_op jit(solution)/shard_map/ppermute | solution.py:756
  556.1 7.6 %collective-permute-start.49 = (bf16[1,4,32,512]{3,2,1,0:T(8,128)(2,1)}, bf16[1,4,32,512]{3,2,1,0:T(8,128)(2,1)S(1)}, u32[]{:S(2)}, u32[]{:S(2)}) collective-permute-start(bf16[1,4,32,512]{3,2,1,0:T(8,128)(2,1)} %get-tuple-element.153), channel_id=1, source_target_pairs={{0,16},{4,20},{8,24},{12,28},{16,0},{20,4},{24,8},{28,12},{1,17},{... | collective-permute-start | bytes 393224 | tf_op jit(solution)/shard_map/ppermute | solution.py:756
  556.9 6.8 %collective-permute-start.48 = (bf16[1,4,32,512]{3,2,1,0:T(8,128)(2,1)S(1)}, bf16[1,4,32,512]{3,2,1,0:T(8,128)(2,1)S(1)}, u32[]{:S(2)}, u32[]{:S(2)}) collective-permute-start(bf16[1,4,32,512]{3,2,1,0:T(8,128)(2,1)S(1)} %get-tuple-element.151), channel_id=1, source_target_pairs={{0,8},{4,12},{8,0},{12,4},{16,24},{20,28},{24,16},{28,20},{1,9},{5... | collective-permute-start | bytes 393224 | tf_op jit(solution)/shard_map/ppermute | solution.py:756
  563.9 7.4 %collective-permute-start.53 = (bf16[1,32,512]{2,1,0:T(8,128)(2,1)S(1)}, bf16[1,32,512]{2,1,0:T(8,128)(2,1)S(1)}, u32[]{:S(2)}, u32[]{:S(2)}) collective-permute-start(bf16[1,32,512]{2,1,0:T(8,128)(2,1)S(1)} %get-tuple-element.164), channel_id=1, source_target_pairs={{0,3},{1,0},{2,1},{3,2},{4,7},{5,4},{6,5},{7,6},{8,11},{9,8},{10,9... | collective-permute-start | bytes 98312 | tf_op jit(solution)/shard_map/ppermute | solution.py:761
  590.4 11.8 %collective-permute-start.60 = (bf16[512,512]{1,0:T(8,128)(2,1)S(1)}, bf16[512,512]{1,0:T(8,128)(2,1)}, u32[]{:S(2)}, u32[]{:S(2)}) collective-permute-start(bf16[512,512]{1,0:T(8,128)(2,1)S(1)} %bitcast.284), channel_id=1, source_target_pairs={{0,4},{4,0},{8,12},{12,8},{16,20},{20,16},{24,28},{28,24},{1,5},{5... | collective-permute-start | bytes 1572872 | tf_op jit(solution)/shard_map/ppermute | solution.py:756
  592.5 9.0 %collective-permute-start.46 = (f32[8,128]{1,0:T(8,128)S(1)}, f32[8,128]{1,0:T(8,128)S(1)}, u32[]{:S(2)}, u32[]{:S(2)}) collective-permute-start(f32[8,128]{1,0:T(8,128)S(1)} %add_add_fusion.2), channel_id=1, source_target_pairs={{0,4},{4,0},{8,12},{12,8},{16,20},{20,16},{24,28},{28,24},{1,5},{5... | collective-permute-start | bytes 12296 | tf_op jit(solution)/shard_map/ppermute | solution.py:756
  592.5 28.0 %all-to-all-start.1 = ((bf16[16,64,512]{2,1,0:T(8,128)(2,1)}), bf16[16,64,512]{2,1,0:T(8,128)(2,1)}, u32[]{:S(2)}, u32[]{:S(2)}) async-start(bf16[16,64,512]{2,1,0:T(8,128)(2,1)} %get-tuple-element.110), calls=%async_computation.1 | async-start | bytes 2097152 | tf_op jit(solution)/shard_map/all_to_all | solution.py:1029
  (99 other events, 454.2 us)
Sparse Core Ops, SparseCore 0:
  41.1 115.4 all-gather.4
  160.0 113.0 all-gather.6

commit v3 on v2

--- a/solution.py
+++ b/solution.py
@@ -921,7 +921,8 @@
         low_rows = tall // n_dp
         pieces = tiles.astype(bf16).reshape(slots, n_dp, low_rows, D)
         pieces = lax.all_to_all(pieces, "dp", 1, 0, tiled=True).reshape(n_tiles, low_rows, D)
-        first = gather(choose(slot_of, pieces, 0, 8, field_all))
+        first = gather(choose(slot_of, pieces, 0, 8, slot_of))
+        first, field_all = lax.optimization_barrier((first, field_all))
     else:
         slots_low = lax.all_gather(tiles.astype(bf16), "blk", axis=1, tiled=True)
         slots_low = lax.all_gather(slots_low, "dp", axis=0, tiled=True)

time: 643 us -> 639 us (level)
  blocking collectives: 0 us -> 20.6 us
  waiting for transfers between devices: 170 us -> 155 us
    all_gather x2, waiting for transfers between devices: 120 us -> 96.2 us  [gather(): lax.all_gather(pieces, ('blk', 'dp'), axis=0)]
    all_to_all x0 -> x1, blocking collectives: none -> 20.6 us  [shards(): lax.all_to_all(pieces, 'dp', 1, 0, tiled=True).reshape(n_tiles, low_rows, D)]
    ppermute x27, waiting for transfers between devices: 33.9 us -> 42.4 us  [shift(): return lax.ppermute(array, 'blk', [(i, (i + step) % n) for i in range(n)])]
  transfers between devices with their start and end apart: 65 -> 64, of which waited for: 20 -> 19; matrix products, arithmetic and copies ran while one was open for 15% -> 15% of each run, Pallas kernels for 27% -> 28%
where the time goes in v3:
time: 639 us; the launch traced here: 635 us
  Pallas kernels  216 us (34%)
  waiting for transfers between devices  155 us (24%)
  starting transfers between devices  82.9 us (13%)
  matrix products  50.7 us (8%)
  other arithmetic  44.5 us (7%)
  local copies, waits for them, and re-layouts  42.2 us (7%)
  between operations  23 us (4%)
  blocking collectives  20.6 us (3%)
    all_gather x2, waiting for transfers between devices, gather(): lax.all_gather(pieces, ('blk', 'dp'), axis=0)  96.2 us
    ppermute x27, starting transfers between devices, shift(): return lax.ppermute(array, 'blk', [(i, (i + step) % n) for i in range(n)])  49.9 us
    dot_general x14, matrix products, tn(): lax.dot_general(left, right, (((0,), (0,)), ((), ())), preferred_element_...  46.5 us
    pallas_call x1, Pallas kernels, attend_back(): pl.pallas_call(functools.partial(attend_back_kernel, qb), grid=(HEADS //...  45.2 us
    ppermute x27, waiting for transfers between devices, shift(): return lax.ppermute(array, 'blk', [(i, (i + step) % n) for i in range(n)])  42.4 us
    pallas_call x1, Pallas kernels, mlp(): pl.pallas_call(mlp_kernel, grid=(2 * folds,), in_specs=[once(state), once...  35.8 us
    pallas_call x1, Pallas kernels, attend(): pl.pallas_call(functools.partial(attend_kernel, qb), grid=(HEADS // 2,),...  30.9 us
    ppermute x34, starting transfers between devices, swap(): return lax.ppermute(array, 'dp', [(i, i ^ bit) for i in range(n)])  29.2 us
  transfers between devices with their start and end apart: 64, of which 19 were waited for; matrix products, arithmetic and copies ran while one was open for 15% of the time, Pallas kernels for 28%

profile of v3, /device:TPU:0, one launch (start us, length us, event | category | flops | bytes accessed | tf_op | source)
XLA Modules:
  0.0 634.8 jit_solution(12946065130911179158)
XLA Ops:
  9.1 20.6 %all_to_all.20 = bf16[2,8,32,1024]{3,2,0,1:T(8,128)(2,1)} all-to-all(bf16[2,8,32,1024]{3,2,0,1:T(8,128)(2,1)S(1)} %copy.73), channel_id=1, replica_groups=mesh['dp'=8,'blk'=4] {'dp'}, dimensions={1} | all-to-all | bytes 2097152 | tf_op jit(solution)/shard_map/all_to_all | solution.py:923
  29.6 2.7 choose.2
  32.6 3.7 collective-permute-start.2
  37.2 4.4 collective-permute-done.2
  41.7 20.1 %collective-permute-done.1 = bf16[4,48,512]{2,1,0:T(8,128)(2,1)S(1)} collective-permute-done((bf16[4,48,512]{2,1,0:T(8,128)(2,1)S(1)}, bf16[4,48,512]{2,1,0:T(8,128)(2,1)S(1)}, u32[]{:S(2)}, u32[]{:S(2)}) %collective-permute-start.1) | collective-permute-done | bytes 196640 | tf_op jit(solution)/shard_map/ppermute | solution.py:761
  62.8 91.9 %all-gather.5.cloned.1.call-done = bf16[256,32,1024]{2,1,0:T(8,128)(2,1)} async-done(((bf16[8,32,1024]{2,1,0:T(8,128)(2,1)}), bf16[256,32,1024]{2,1,0:T(8,128)(2,1)}) %all-gather.5.cloned.1.call-update) | async-done | bytes 16777232 | tf_op jit(solution)/shard_map/all_gather | solution.py:799
  154.6 2.8 choose.3
  192.8 6.6 %fold.1 = (f32[240,128]{1,0:T(8,128)}, bf16[240,1024]{1,0:T(8,128)(2,1)}, bf16[1024,240]{1,0:T(8,128)(2,1)}, f32[16,1024]{1,0:T(8,128)}, f32[8,1024]{1,0:T(8,128)}) custom-call(bf16[4,8,8,32,1024]{4,3,2,1,0:T(8,128)(2,1)} %bitcast.244, bf16[4,8,8,32,1024]{4,3,2,1,0:T(8,128)(2,1)} %bitcast.245, bf16[4,8,8,32,1024]{4,3,2,1,0:T(8,128)(2,1)} %bitcast.246, ...), custom_call_target="tpu_custom_call" | custom-call | flops 1509949440 | bytes 6291456 | tf_op jit(solution)/shard_map/fold/pallas_call | solution.py:178
  201.3 7.5 %mix.1.m_ref = bf16[2048,1024]{1,0:T(8,128)(2,1)S(1)} custom-call(bf16[4,4,48,512]{3,2,1,0:T(8,128)(2,1)S(1)} %copy-done.7, f32[240,128]{1,0:T(8,128)S(1)} %copy-done.18, bf16[1024,240]{1,0:T(8,128)(2,1)S(1)} %copy-done.16), custom_call_target="tpu_custom_call" | custom-call | flops 4026531840 | bytes 8388608 | tf_op jit(solution)/shard_map/mix/pallas_call | solution.py:220
  210.9 23.0 %front.1 = (f32[2048,1024]{1,0:T(8,128)}, bf16[2048,1024]{1,0:T(8,128)(2,1)}, bf16[512,1024]{1,0:T(8,128)(2,1)S(1)}, bf16[2048,1024]{1,0:T(8,128)(2,1)}, bf16[2048,1024]{1,0:T(8,128)(2,1)}) custom-call(bf16[2048,1024]{1,0:T(8,128)(2,1)} %copy-done.3, bf16[4,8,8,32,1024]{4,3,2,1,0:T(8,128)(2,1)} %bitcast.247, bf16[4,8,8,32,1024]{4,3,2,1,0:T(8,128)(2,1)} %bitcast.248, ...), custom_call_target="tpu_custom_call" | custom-call | flops 12884901888 | bytes 33554432 | tf_op jit(solution)/shard_map/front/pallas_call | solution.py:321
  233.9 30.9 %attend.1 = (bf16[512,1024]{1,0:T(8,128)(2,1)S(1)}, f32[512,128]{1,0:T(8,128)S(1)}) custom-call(bf16[512,1024]{1,0:T(8,128)(2,1)S(1)} %get-tuple-element.69.q_ref, bf16[2048,1024]{1,0:T(8,128)(2,1)} %get-tuple-element.70.k_ref, bf16[2048,1024]{1,0:T(8,128)(2,1)} %get-tuple-element.71.v_ref), custom_call_target="tpu_custom_call" | custom-call | flops 17179869184 | bytes 16777216 | tf_op jit(solution)/shard_map/attend/pallas_call | solution.py:88
  266.8 4.3 all-gather.7.cloned.1.call-done
  271.1 35.8 %mlp.1 = (bf16[512,4096]{1,0:T(8,128)(2,1)}, bf16[512,1024]{1,0:T(8,128)(2,1)}, bf16[512,1024]{1,0:T(8,128)(2,1)}, bf16[512,4096]{1,0:T(8,128)(2,1)}, f32[512,10...) custom-call(f32[2048,1024]{1,0:T(8,128)} %get-tuple-element.68.h0_re, ...), custom_call_target="tpu_custom_call" | custom-call | flops 17179869184 | bytes 83886080 | tf_op jit(solution)/shard_map/mlp/pallas_call | solution.py:437
  306.9 6.9 %convolution_convert_fusion = bf16[4096,512]{1,0:T(8,128)(2,1)} fusion(bf16[512,4096]{1,0:T(8,128)(2,1)} %get-tuple-element.73, pred[]{:T(512)S(6)} %eq.112, bf16[512,1024]{1,0:T(8,128)(2,1)} %get-tuple-element.74), kind=kOutput, calls=%fused_computation.2 | convolution fusion | flops 2149842944 | bytes 9437185 | tf_op jit(solution)/shard_map/dot_general | solution.py:746
  315.3 5.1 convolution_convert_fusion.1
  327.0 2.6 collective-permute-done.23
  329.6 2.6 convert_add_fusion.5
  332.3 4.8 convert_add_fusion.1
  337.0 3.2 copy-done.24
  342.4 5.7 convert_add_fusion
  352.7 45.2 %attend_back.1 = (bf16[512,1024]{1,0:T(8,128)(2,1)S(1)}, bf16[2048,1024]{1,0:T(8,128)(2,1)}, bf16[2048,1024]{1,0:T(8,128)(2,1)}) custom-call(bf16[512,1024]{1,0:T(8,128)(2,1)S(1)} %copy-done.15, bf16[2048,1024]{1,0:T(8,128)(2,1)} %get-tuple-element.70.k_ref, bf16[2048,1024]{1,0:T(8,128)(2,1)} %get-tuple-element.71.v_ref, bf16[512,1024]{1,0:T(8,128)(2,1)S(1)} %copy-done.22, ...), custom_call_target="tpu_custom_call" | custom-call | flops 42949672960 | bytes 33554432 | tf_op jit(solution)/shard_map/attend_back/pallas_call | solution.py:141
  398.0 3.9 bitcast_add_fusion.1
  403.6 2.6 bitcast_add_fusion
  409.5 2.4 fusion.52
  412.0 2.4 fusion.55
  418.6 2.4 convert_add_fusion.4
  421.0 2.8 convert_add_fusion.3
  426.5 6.0 collective-permute-done.18
  434.8 29.0 %back.1 = (bf16[2048,1024]{1,0:T(8,128)(2,1)}, bf16[2048,1024]{1,0:T(8,128)(2,1)}, f32[8,1024]{1,0:T(8,128)S(1)}) custom-call(bf16[512,1024]{1,0:T(8,128)(2,1)S(1)} %get-tuple-element.88.dq_ref, bf16[2048,1024]{1,0:T(8,128)(2,1)} %get-tuple-element.86.dk_ref, bf16[2048,1024]{1,0:T(8,128)(2,1)} %get-tuple-element.87.dv_ref, ...), custom_call_target="tpu_custom_call" | custom-call | flops 15032385536 | bytes 33554432 | tf_op jit(solution)/shard_map/back/pallas_call | solution.py:518
  467.5 2.2 collective-permute-start.15
  470.4 4.6 collective-permute-done.19
  475.0 9.3 %collective-permute-start.13 = (bf16[4,64,512]{2,1,0:T(8,128)(2,1)S(1)}, bf16[4,64,512]{2,1,0:T(8,128)(2,1)S(1)}, u32[]{:S(2)}, u32[]{:S(2)}) collective-permute-start(bf16[4,64,512]{2,1,0:T(8,128)(2,1)S(1)} %get-tuple-element.148), channel_id=1, source_target_pairs={{0,1},{1,2},{2,3},{3,0},{4,5},{5,6},{6,7},{7,4},{8,9},{9,10},{10,1... | collective-permute-start | bytes 786440 | tf_op jit(solution)/shard_map/ppermute | solution.py:761
  492.6 3.4 fusion.58
  498.1 17.9 %mix_back.1 = (f32[512,512]{1,0:T(8,128)S(1)}, bf16[512,512]{1,0:T(8,128)(2,1)S(1)}) custom-call(s32[1]{0:T(128)} %bitcast.72.side_ref, bf16[4,4,48,512]{3,2,1,0:T(8,128)(2,1)S(1)} %copy-done.8, f32[240,128]{1,0:T(8,128)S(1)} %copy-done.19, bf16[240,1024]{1,0:T(8,128)(2,1)S(1)} %copy-done.17, bf16[2048,1024]{1,0:T(8,128)(2,1)S(1)} %copy-done.13, ...), custom_call_target="tpu_custom_call" | custom-call | flops 8053063680 | bytes 8388608 | tf_op jit(solution)/shard_map/mix_back/pallas_call | solution.py:279
  516.2 4.6 convert_add_fusion.2
  524.8 2.7 collective-permute-start.30
  527.5 3.6 collective-permute-done.36
  533.2 2.5 collective-permute-done.35
  536.3 2.2 collective-permute-start.37
  541.0 2.8 collective-permute-start.39
  543.8 4.1 collective-permute-done.31.refs_4_
  549.6 2.7 collective-permute-done.32.refs_5_
  560.0 6.4 %collective-permute-start.53 = (bf16[1,32,512]{2,1,0:T(8,128)(2,1)S(1)}, bf16[1,32,512]{2,1,0:T(8,128)(2,1)S(1)}, u32[]{:S(2)}, u32[]{:S(2)}) collective-permute-start(bf16[1,32,512]{2,1,0:T(8,128)(2,1)S(1)} %get-tuple-element.168), channel_id=1, source_target_pairs={{0,3},{1,0},{2,1},{3,2},{4,7},{5,4},{6,5},{7,6},{8,11},{9,8},{10,9... | collective-permute-start | bytes 98312 | tf_op jit(solution)/shard_map/ppermute | solution.py:761
  568.5 2.8 collective-permute-done.52
  589.8 3.8 all-to-all-start.1
  598.8 3.1 fusion.170
  603.5 12.9 %tail.1 = (f32[8,128]{1,0:T(8,128)S(1)}, f32[16,1024]{1,0:T(8,128)S(1)}, f32[8,1024]{1,0:T(8,128)S(1)}, f32[499,1024]{1,0:T(8,128)}, f32[499,1024]{1,0:T(8,128)}, /*index=5*/f32[499,1024]{1,0:T(8,128)}) custom-call(f32[1]{0:T(128)} %get-tuple-element.190.square_ref, bf16[4,8,8,32,1024]{4,3,2,1,0:T(8,128)(2,1)} %bitcast.256, ...), custom_call_target="tpu_custom_call" | custom-call | flops 2013265920 | bytes 14307328 | tf_op jit(solution)/shard_map/tail/pallas_call | solution.py:698
  623.1 4.7 multiply_subtract_fusion
  (403 shorter events, 133.5 us)
Async XLA Ops:
  7.2 147.5 %all-gather.5.cloned.1.call-start = ((), (), s32[]{:S(2)}) async-start(), calls=%async_computation.2 | async-start | bytes 17301504 | tf_op jit(solution)/shard_map/all_gather | solution.py:799
  32.4 238.8 %all-gather.7.cloned.1.call-start = ((), (), s32[]{:S(2)}) async-start(), calls=%async_computation.3 | async-start | bytes 17301504 | tf_op jit(solution)/shard_map/all_gather | solution.py:799
  32.6 9.1 %collective-permute-start.2 = (bf16[4,48,512]{2,1,0:T(8,128)(2,1)S(1)}, bf16[4,48,512]{2,1,0:T(8,128)(2,1)S(1)}, u32[]{:S(2)}, u32[]{:S(2)}) collective-permute-start(bf16[4,48,512]{2,1,0:T(8,128)(2,1)S(1)} %bitcast.287), channel_id=1, source_target_pairs={{0,3},{1,0},{2,1},{3,2},{4,7},{5,4},{6,5},{7,6},{8,11},{9,8},{10,9... | collective-permute-start | bytes 589832 | tf_op jit(solution)/shard_map/ppermute | solution.py:761
  36.2 25.6 %collective-permute-start.1 = (bf16[4,48,512]{2,1,0:T(8,128)(2,1)S(1)}, bf16[4,48,512]{2,1,0:T(8,128)(2,1)S(1)}, u32[]{:S(2)}, u32[]{:S(2)}) collective-permute-start(bf16[4,48,512]{2,1,0:T(8,128)(2,1)S(1)} %bitcast.288), channel_id=1, source_target_pairs={{0,2},{1,3},{2,0},{3,1},{4,6},{5,7},{6,4},{7,5},{8,10},{9,11},{10,... | collective-permute-start | bytes 589832 | tf_op jit(solution)/shard_map/ppermute | solution.py:761
  36.2 25.6 %collective-permute-start = (bf16[4,48,512]{2,1,0:T(8,128)(2,1)S(1)}, bf16[4,48,512]{2,1,0:T(8,128)(2,1)S(1)}, u32[]{:S(2)}, u32[]{:S(2)}) collective-permute-start(bf16[4,48,512]{2,1,0:T(8,128)(2,1)S(1)} %bitcast.289), channel_id=1, source_target_pairs={{0,1},{1,2},{2,3},{3,0},{4,5},{5,6},{6,7},{7,4},{8,9},{9,10},{10,1... | collective-permute-start | bytes 589832 | tf_op jit(solution)/shard_map/ppermute | solution.py:761
  159.5 9.7 %collective-permute-start.5 = (f32[64,128]{1,0:T(8,128)S(1)}, f32[64,128]{1,0:T(8,128)S(1)}, u32[]{:S(2)}, u32[]{:S(2)}) collective-permute-start(f32[64,128]{1,0:T(8,128)S(1)} %broadcast_select_fusion.1), channel_id=1, source_target_pairs={{0,3},{1,0},{2,1},{3,2},{4,7},{5,4},{6,5},{7,6},{8,11},{9,8},{10,9... | collective-permute-start | bytes 98312 | tf_op jit(solution)/shard_map/ppermute | solution.py:761
  160.9 8.3 %collective-permute-start.4 = (f32[64,128]{1,0:T(8,128)S(1)}, f32[64,128]{1,0:T(8,128)S(1)}, u32[]{:S(2)}, u32[]{:S(2)}) collective-permute-start(f32[64,128]{1,0:T(8,128)S(1)} %broadcast_select_fusion.1), channel_id=1, source_target_pairs={{0,2},{1,3},{2,0},{3,1},{4,6},{5,7},{6,4},{7,5},{8,10},{9,11},{10,... | collective-permute-start | bytes 98312 | tf_op jit(solution)/shard_map/ppermute | solution.py:761
  161.3 8.5 %collective-permute-start.3 = (f32[64,128]{1,0:T(8,128)S(1)}, f32[64,128]{1,0:T(8,128)}, u32[]{:S(2)}, u32[]{:S(2)}) collective-permute-start(f32[64,128]{1,0:T(8,128)S(1)} %broadcast_select_fusion.1), channel_id=1, source_target_pairs={{0,1},{1,2},{2,3},{3,0},{4,5},{5,6},{6,7},{7,4},{8,9},{9,10},{10,1... | collective-permute-start | bytes 98312 | tf_op jit(solution)/shard_map/ppermute | solution.py:761
  170.7 7.7 %collective-permute-start.8 = (f32[64,128]{1,0:T(8,128)S(1)}, f32[64,128]{1,0:T(8,128)S(1)}, u32[]{:S(2)}, u32[]{:S(2)}) collective-permute-start(f32[64,128]{1,0:T(8,128)S(1)} %add_add_fusion.1), channel_id=1, source_target_pairs={{0,24},{4,28},{8,16},{12,20},{16,8},{20,12},{24,0},{28,4},{1,25},{... | collective-permute-start | bytes 98312 | tf_op jit(solution)/shard_map/ppermute | solution.py:756
  179.9 8.6 %collective-permute-start.9 = (f32[64,128]{1,0:T(8,128)S(1)}, f32[64,128]{1,0:T(8,128)S(1)}, u32[]{:S(2)}, u32[]{:S(2)}) collective-permute-start(f32[64,128]{1,0:T(8,128)S(1)} %add_add_fusion), channel_id=1, source_target_pairs={{0,4},{4,0},{8,12},{12,8},{16,20},{20,16},{24,28},{28,24},{1,5},{5... | collective-permute-start | bytes 98312 | tf_op jit(solution)/shard_map/ppermute | solution.py:756
  313.9 18.4 %collective-permute-start.10 = (bf16[4096,512]{1,0:T(8,128)(2,1)}, bf16[4096,512]{1,0:T(8,128)(2,1)}, u32[]{:S(2)}, u32[]{:S(2)}) collective-permute-start(bf16[4096,512]{1,0:T(8,128)(2,1)} %convolution_convert_fusion), channel_id=1, source_target_pairs={{0,4},{4,0},{8,12},{12,8},{16,20},{20,16},{24,28},{28,24},{1,5},{5... | collective-permute-start | bytes 12582920 | tf_op jit(solution)/shard_map/ppermute | solution.py:756
  320.5 21.4 %collective-permute-start.16 = (bf16[1024,2048]{1,0:T(8,128)(2,1)}, bf16[1024,2048]{1,0:T(8,128)(2,1)}, u32[]{:S(2)}, u32[]{:S(2)}) collective-permute-start(bf16[1024,2048]{1,0:T(8,128)(2,1)} %convolution_convert_fusion.1), channel_id=1, source_target_pairs={{0,4},{4,0},{8,12},{12,8},{16,20},{20,16},{24,28},{28,24},{1,5},{5... | collective-permute-start | bytes 12582920 | tf_op jit(solution)/shard_map/ppermute | solution.py:756
  322.7 7.0 %collective-permute-start.23 = (bf16[1024,512]{1,0:T(8,128)(2,1)}, bf16[1024,512]{1,0:T(8,128)(2,1)}, u32[]{:S(2)}, u32[]{:S(2)}) collective-permute-start(bf16[1024,512]{1,0:T(8,128)(2,1)} %convolution_convert_fusion.2), channel_id=1, source_target_pairs={{0,4},{4,0},{8,12},{12,8},{16,20},{20,16},{24,28},{28,24},{1,5},{5... | collective-permute-start | bytes 3145736 | tf_op jit(solution)/shard_map/ppermute | solution.py:756
  340.6 57.3 %collective-permute-start.11 = (bf16[4,4,2,64,512]{4,3,0,1,2:T(8,128)(2,1)S(1)}, bf16[4,4,2,64,512]{4,3,0,1,2:T(8,128)(2,1)}, u32[]{:S(2)}, u32[]{:S(2)}) collective-permute-start(bf16[4,4,2,64,512]{4,3,0,1,2:T(8,128)(2,1)S(1)} %fusion.1), channel_id=1, source_target_pairs={{0,8},{4,12},{8,0},{12,4},{16,24},{20,28},{24,16},{28,20},{1,9},{5... | collective-permute-start | bytes 6291464 | tf_op jit(solution)/shard_map/ppermute | solution.py:756
  349.8 53.7 %collective-permute-start.17 = (bf16[1,4,2,64,2048]{4,3,1,2,0:T(8,128)(2,1)}, bf16[1,4,2,64,2048]{4,3,1,2,0:T(8,128)(2,1)}, u32[]{:S(2)}, u32[]{:S(2)}) collective-permute-start(bf16[1,4,2,64,2048]{4,3,1,2,0:T(8,128)(2,1)} %fusion.2), channel_id=1, source_target_pairs={{0,16},{4,20},{8,24},{12,28},{16,0},{20,4},{24,8},{28,12},{1,17},{... | collective-permute-start | bytes 6291464 | tf_op jit(solution)/shard_map/ppermute | solution.py:756
  402.0 61.8 %collective-permute-start.12 = (bf16[4,4,64,512]{3,2,0,1:T(8,128)(2,1)S(1)}, bf16[4,4,64,512]{3,2,0,1:T(8,128)(2,1)}, u32[]{:S(2)}, u32[]{:S(2)}) collective-permute-start(bf16[4,4,64,512]{3,2,0,1:T(8,128)(2,1)S(1)} %fusion.63), channel_id=1, source_target_pairs={{0,16},{4,20},{8,24},{12,28},{16,0},{20,4},{24,8},{28,12},{1,17},{... | collective-permute-start | bytes 3145736 | tf_op jit(solution)/shard_map/ppermute | solution.py:756
  406.4 26.1 %collective-permute-start.18 = (bf16[1,4,64,2048]{3,2,1,0:T(8,128)(2,1)S(1)}, bf16[1,4,64,2048]{3,2,1,0:T(8,128)(2,1)S(1)}, u32[]{:S(2)}, u32[]{:S(2)}) collective-permute-start(bf16[1,4,64,2048]{3,2,1,0:T(8,128)(2,1)S(1)} %fusion.64), channel_id=1, source_target_pairs={{0,8},{4,12},{8,0},{12,4},{16,24},{20,28},{24,16},{28,20},{1,9},{5... | collective-permute-start | bytes 3145736 | tf_op jit(solution)/shard_map/ppermute | solution.py:756
  408.1 6.8 %collective-permute-start.22 = (bf16[1024,512]{1,0:T(8,128)(2,1)S(1)}, bf16[1024,512]{1,0:T(8,128)(2,1)S(1)}, u32[]{:S(2)}, u32[]{:S(2)}) collective-permute-start(bf16[1024,512]{1,0:T(8,128)(2,1)S(1)} %convolution_convert_fusion.3), channel_id=1, source_target_pairs={{0,4},{4,0},{8,12},{12,8},{16,20},{20,16},{24,28},{28,24},{1,5},{5... | collective-permute-start | bytes 3145736 | tf_op jit(solution)/shard_map/ppermute | solution.py:756
  411.9 6.6 %collective-permute-start.26 = (bf16[1024,512]{1,0:T(8,128)(2,1)S(1)}, bf16[1024,512]{1,0:T(8,128)(2,1)S(1)}, u32[]{:S(2)}, u32[]{:S(2)}) collective-permute-start(bf16[1024,512]{1,0:T(8,128)(2,1)S(1)} %fusion.52), channel_id=1, source_target_pairs={{0,4},{4,0},{8,12},{12,8},{16,20},{20,16},{24,28},{28,24},{1,5},{5... | collective-permute-start | bytes 3145736 | tf_op jit(solution)/shard_map/ppermute | solution.py:756
  414.4 6.6 %collective-permute-start.27 = (bf16[1024,512]{1,0:T(8,128)(2,1)S(1)}, bf16[1024,512]{1,0:T(8,128)(2,1)S(1)}, u32[]{:S(2)}, u32[]{:S(2)}) collective-permute-start(bf16[1024,512]{1,0:T(8,128)(2,1)S(1)} %fusion.55), channel_id=1, source_target_pairs={{0,4},{4,0},{8,12},{12,8},{16,20},{20,16},{24,28},{28,24},{1,5},{5... | collective-permute-start | bytes 3145736 | tf_op jit(solution)/shard_map/ppermute | solution.py:756
  417.4 68.2 %collective-permute-start.24 = (bf16[2,4,2,64,512]{4,3,0,1,2:T(8,128)(2,1)}, bf16[2,4,2,64,512]{4,3,0,1,2:T(8,128)(2,1)}, u32[]{:S(2)}, u32[]{:S(2)}) collective-permute-start(bf16[2,4,2,64,512]{4,3,0,1,2:T(8,128)(2,1)} %fusion.65), channel_id=1, source_target_pairs={{0,8},{4,12},{8,0},{12,4},{16,24},{20,28},{24,16},{28,20},{1,9},{5... | collective-permute-start | bytes 3145736 | tf_op jit(solution)/shard_map/ppermute | solution.py:756
  425.5 63.4 %collective-permute-start.28 = (bf16[2,4,2,64,512]{4,3,0,1,2:T(8,128)(2,1)}, bf16[2,4,2,64,512]{4,3,0,1,2:T(8,128)(2,1)}, u32[]{:S(2)}, u32[]{:S(2)}) collective-permute-start(bf16[2,4,2,64,512]{4,3,0,1,2:T(8,128)(2,1)} %fusion.66), channel_id=1, source_target_pairs={{0,16},{4,20},{8,24},{12,28},{16,0},{20,4},{24,8},{28,12},{1,17},{... | collective-permute-start | bytes 3145736 | tf_op jit(solution)/shard_map/ppermute | solution.py:756
  432.9 34.6 %collective-permute-start.21 = (bf16[1,64,2048]{2,1,0:T(8,128)(2,1)S(1)}, bf16[1,64,2048]{2,1,0:T(8,128)(2,1)S(1)}, u32[]{:S(2)}, u32[]{:S(2)}) collective-permute-start(bf16[1,64,2048]{2,1,0:T(8,128)(2,1)S(1)} %get-tuple-element.146), channel_id=1, source_target_pairs={{0,3},{1,0},{2,1},{3,2},{4,7},{5,4},{6,5},{7,6},{8,11},{9,8},{10,9... | collective-permute-start | bytes 786440 | tf_op jit(solution)/shard_map/ppermute | solution.py:761
  434.4 35.4 %collective-permute-start.20 = (bf16[1,64,2048]{2,1,0:T(8,128)(2,1)S(1)}, bf16[1,64,2048]{2,1,0:T(8,128)(2,1)}, u32[]{:S(2)}, u32[]{:S(2)}) collective-permute-start(bf16[1,64,2048]{2,1,0:T(8,128)(2,1)S(1)} %get-tuple-element.147), channel_id=1, source_target_pairs={{0,2},{1,3},{2,0},{3,1},{4,6},{5,7},{6,4},{7,5},{8,10},{9,11},{10,... | collective-permute-start | bytes 786440 | tf_op jit(solution)/shard_map/ppermute | solution.py:761
  463.8 11.2 %collective-permute-start.19 = (bf16[1,64,2048]{2,1,0:T(8,128)(2,1)S(1)}, bf16[1,64,2048]{2,1,0:T(8,128)(2,1)S(1)}, u32[]{:S(2)}, u32[]{:S(2)}) collective-permute-start(bf16[1,64,2048]{2,1,0:T(8,128)(2,1)S(1)} %get-tuple-element.145), channel_id=1, source_target_pairs={{0,1},{1,2},{2,3},{3,0},{4,5},{5,6},{6,7},{7,4},{8,9},{9,10},{10,1... | collective-permute-start | bytes 786440 | tf_op jit(solution)/shard_map/ppermute | solution.py:761
  467.5 28.4 %collective-permute-start.15 = (bf16[4,64,512]{2,1,0:T(8,128)(2,1)S(1)}, bf16[4,64,512]{2,1,0:T(8,128)(2,1)S(1)}, u32[]{:S(2)}, u32[]{:S(2)}) collective-permute-start(bf16[4,64,512]{2,1,0:T(8,128)(2,1)S(1)} %get-tuple-element.149), channel_id=1, source_target_pairs={{0,3},{1,0},{2,1},{3,2},{4,7},{5,4},{6,5},{7,6},{8,11},{9,8},{10,9... | collective-permute-start | bytes 786440 | tf_op jit(solution)/shard_map/ppermute | solution.py:761
  469.7 26.3 %collective-permute-start.14 = (bf16[4,64,512]{2,1,0:T(8,128)(2,1)S(1)}, bf16[4,64,512]{2,1,0:T(8,128)(2,1)S(1)}, u32[]{:S(2)}, u32[]{:S(2)}) collective-permute-start(bf16[4,64,512]{2,1,0:T(8,128)(2,1)S(1)} %get-tuple-element.150), channel_id=1, source_target_pairs={{0,2},{1,3},{2,0},{3,1},{4,6},{5,7},{6,4},{7,5},{8,10},{9,11},{10,... | collective-permute-start | bytes 786440 | tf_op jit(solution)/shard_map/ppermute | solution.py:761
  475.0 21.0 %collective-permute-start.13 = (bf16[4,64,512]{2,1,0:T(8,128)(2,1)S(1)}, bf16[4,64,512]{2,1,0:T(8,128)(2,1)S(1)}, u32[]{:S(2)}, u32[]{:S(2)}) collective-permute-start(bf16[4,64,512]{2,1,0:T(8,128)(2,1)S(1)} %get-tuple-element.148), channel_id=1, source_target_pairs={{0,1},{1,2},{2,3},{3,0},{4,5},{5,6},{6,7},{7,4},{8,9},{9,10},{10,1... | collective-permute-start | bytes 786440 | tf_op jit(solution)/shard_map/ppermute | solution.py:761
  496.0 20.2 %collective-permute-start.33 = (bf16[1024,512]{1,0:T(8,128)(2,1)}, bf16[1024,512]{1,0:T(8,128)(2,1)S(1)}, u32[]{:S(2)}, u32[]{:S(2)}) collective-permute-start(bf16[1024,512]{1,0:T(8,128)(2,1)} %fusion.58), channel_id=1, source_target_pairs={{0,4},{4,0},{8,12},{12,8},{16,20},{20,16},{24,28},{28,24},{1,5},{5... | collective-permute-start | bytes 3145736 | tf_op jit(solution)/shard_map/ppermute | solution.py:756
  496.1 19.8 %collective-permute-start.25 = (bf16[2,4,64,512]{3,2,0,1:T(8,128)(2,1)S(1)}, bf16[2,4,64,512]{3,2,0,1:T(8,128)(2,1)S(1)}, u32[]{:S(2)}, u32[]{:S(2)}) collective-permute-start(bf16[2,4,64,512]{3,2,0,1:T(8,128)(2,1)S(1)} %fusion.74), channel_id=1, source_target_pairs={{0,16},{4,20},{8,24},{12,28},{16,0},{20,4},{24,8},{28,12},{1,17},{... | collective-permute-start | bytes 1572872 | tf_op jit(solution)/shard_map/ppermute | solution.py:756
  497.1 27.3 %collective-permute-start.29 = (bf16[2,4,64,512]{3,2,0,1:T(8,128)(2,1)S(1)}, bf16[2,4,64,512]{3,2,0,1:T(8,128)(2,1)S(1)}, u32[]{:S(2)}, u32[]{:S(2)}) collective-permute-start(bf16[2,4,64,512]{3,2,0,1:T(8,128)(2,1)S(1)} %fusion.75), channel_id=1, source_target_pairs={{0,8},{4,12},{8,0},{12,4},{16,24},{20,28},{24,16},{28,20},{1,9},{5... | collective-permute-start | bytes 1572872 | tf_op jit(solution)/shard_map/ppermute | solution.py:756
  520.9 10.2 %collective-permute-start.36 = (bf16[1,4,64,512]{3,2,1,0:T(8,128)(2,1)S(1)}, bf16[1,4,64,512]{3,2,1,0:T(8,128)(2,1)S(1)}, u32[]{:S(2)}, u32[]{:S(2)}) collective-permute-start(bf16[1,4,64,512]{3,2,1,0:T(8,128)(2,1)S(1)} %get-tuple-element.141), channel_id=1, source_target_pairs={{0,24},{4,28},{8,16},{12,20},{16,8},{20,12},{24,0},{28,4},{1,25},{... | collective-permute-start | bytes 786440 | tf_op jit(solution)/shard_map/ppermute | solution.py:756
  522.6 13.0 %collective-permute-start.35 = (bf16[1,4,64,512]{3,2,1,0:T(8,128)(2,1)S(1)}, bf16[1,4,64,512]{3,2,1,0:T(8,128)(2,1)S(1)}, u32[]{:S(2)}, u32[]{:S(2)}) collective-permute-start(bf16[1,4,64,512]{3,2,1,0:T(8,128)(2,1)S(1)} %get-tuple-element.140), channel_id=1, source_target_pairs={{0,16},{4,20},{8,24},{12,28},{16,0},{20,4},{24,8},{28,12},{1,17},{... | collective-permute-start | bytes 786440 | tf_op jit(solution)/shard_map/ppermute | solution.py:756
  523.6 12.5 %collective-permute-start.34 = (bf16[1,4,64,512]{3,2,1,0:T(8,128)(2,1)S(1)}, bf16[1,4,64,512]{3,2,1,0:T(8,128)(2,1)S(1)}, u32[]{:S(2)}, u32[]{:S(2)}) collective-permute-start(bf16[1,4,64,512]{3,2,1,0:T(8,128)(2,1)S(1)} %get-tuple-element.139), channel_id=1, source_target_pairs={{0,8},{4,12},{8,0},{12,4},{16,24},{20,28},{24,16},{28,20},{1,9},{5... | collective-permute-start | bytes 786440 | tf_op jit(solution)/shard_map/ppermute | solution.py:756
  524.6 13.9 %collective-permute-start.47 = (bf16[512,512]{1,0:T(8,128)(2,1)S(1)}, bf16[512,512]{1,0:T(8,128)(2,1)S(1)}, u32[]{:S(2)}, u32[]{:S(2)}) collective-permute-start(bf16[512,512]{1,0:T(8,128)(2,1)S(1)} %get-tuple-element.108), channel_id=1, source_target_pairs={{0,4},{4,0},{8,12},{12,8},{16,20},{20,16},{24,28},{28,24},{1,5},{5... | collective-permute-start | bytes 1572872 | tf_op jit(solution)/shard_map/ppermute | solution.py:756
  524.8 16.2 %collective-permute-start.30 = (bf16[4,64,512]{2,1,0:T(8,128)(2,1)S(1)}, bf16[4,64,512]{2,1,0:T(8,128)(2,1)S(1)}, u32[]{:S(2)}, u32[]{:S(2)}) collective-permute-start(bf16[4,64,512]{2,1,0:T(8,128)(2,1)S(1)} %get-tuple-element.143), channel_id=1, source_target_pairs={{0,1},{1,2},{2,3},{3,0},{4,5},{5,6},{6,7},{7,4},{8,9},{9,10},{10,1... | collective-permute-start | bytes 786440 | tf_op jit(solution)/shard_map/ppermute | solution.py:761
  531.1 16.9 %collective-permute-start.31 = (bf16[4,64,512]{2,1,0:T(8,128)(2,1)S(1)}, bf16[4,64,512]{2,1,0:T(8,128)(2,1)S(1)}, u32[]{:S(2)}, u32[]{:S(2)}) collective-permute-start(bf16[4,64,512]{2,1,0:T(8,128)(2,1)S(1)} %get-tuple-element.144), channel_id=1, source_target_pairs={{0,2},{1,3},{2,0},{3,1},{4,6},{5,7},{6,4},{7,5},{8,10},{9,11},{10,... | collective-permute-start | bytes 786440 | tf_op jit(solution)/shard_map/ppermute | solution.py:761
  535.6 16.6 %collective-permute-start.32 = (bf16[4,64,512]{2,1,0:T(8,128)(2,1)S(1)}, bf16[4,64,512]{2,1,0:T(8,128)(2,1)S(1)}, u32[]{:S(2)}, u32[]{:S(2)}) collective-permute-start(bf16[4,64,512]{2,1,0:T(8,128)(2,1)S(1)} %get-tuple-element.142), channel_id=1, source_target_pairs={{0,3},{1,0},{2,1},{3,2},{4,7},{5,4},{6,5},{7,6},{8,11},{9,8},{10,9... | collective-permute-start | bytes 786440 | tf_op jit(solution)/shard_map/ppermute | solution.py:761
  536.3 16.9 %collective-permute-start.37 = (bf16[1,64,512]{2,1,0:T(8,128)(2,1)S(1)}, bf16[1,64,512]{2,1,0:T(8,128)(2,1)S(1)}, u32[]{:S(2)}, u32[]{:S(2)}) collective-permute-start(bf16[1,64,512]{2,1,0:T(8,128)(2,1)S(1)} %get-tuple-element.166), channel_id=1, source_target_pairs={{0,1},{1,2},{2,3},{3,0},{4,5},{5,6},{6,7},{7,4},{8,9},{9,10},{10,1... | collective-permute-start | bytes 196616 | tf_op jit(solution)/shard_map/ppermute | solution.py:761
  538.5 18.1 %collective-permute-start.38 = (bf16[1,64,512]{2,1,0:T(8,128)(2,1)S(1)}, bf16[1,64,512]{2,1,0:T(8,128)(2,1)S(1)}, u32[]{:S(2)}, u32[]{:S(2)}) collective-permute-start(bf16[1,64,512]{2,1,0:T(8,128)(2,1)S(1)} %get-tuple-element.165), channel_id=1, source_target_pairs={{0,2},{1,3},{2,0},{3,1},{4,6},{5,7},{6,4},{7,5},{8,10},{9,11},{10,... | collective-permute-start | bytes 196616 | tf_op jit(solution)/shard_map/ppermute | solution.py:761
  541.0 15.6 %collective-permute-start.39 = (bf16[1,64,512]{2,1,0:T(8,128)(2,1)S(1)}, bf16[1,64,512]{2,1,0:T(8,128)(2,1)S(1)}, u32[]{:S(2)}, u32[]{:S(2)}) collective-permute-start(bf16[1,64,512]{2,1,0:T(8,128)(2,1)S(1)} %get-tuple-element.164), channel_id=1, source_target_pairs={{0,3},{1,0},{2,1},{3,2},{4,7},{5,4},{6,5},{7,6},{8,11},{9,8},{10,9... | collective-permute-start | bytes 196616 | tf_op jit(solution)/shard_map/ppermute | solution.py:761
  548.0 11.0 %collective-permute-start.50 = (bf16[1,4,32,512]{3,2,1,0:T(8,128)(2,1)}, bf16[1,4,32,512]{3,2,1,0:T(8,128)(2,1)S(1)}, u32[]{:S(2)}, u32[]{:S(2)}) collective-permute-start(bf16[1,4,32,512]{3,2,1,0:T(8,128)(2,1)} %get-tuple-element.156), channel_id=1, source_target_pairs={{0,24},{4,28},{8,16},{12,20},{16,8},{20,12},{24,0},{28,4},{1,25},{... | collective-permute-start | bytes 393224 | tf_op jit(solution)/shard_map/ppermute | solution.py:756
  552.3 6.7 %collective-permute-start.49 = (bf16[1,4,32,512]{3,2,1,0:T(8,128)(2,1)}, bf16[1,4,32,512]{3,2,1,0:T(8,128)(2,1)}, u32[]{:S(2)}, u32[]{:S(2)}) collective-permute-start(bf16[1,4,32,512]{3,2,1,0:T(8,128)(2,1)} %get-tuple-element.157), channel_id=1, source_target_pairs={{0,16},{4,20},{8,24},{12,28},{16,0},{20,4},{24,8},{28,12},{1,17},{... | collective-permute-start | bytes 393224 | tf_op jit(solution)/shard_map/ppermute | solution.py:756
  560.0 8.4 %collective-permute-start.53 = (bf16[1,32,512]{2,1,0:T(8,128)(2,1)S(1)}, bf16[1,32,512]{2,1,0:T(8,128)(2,1)S(1)}, u32[]{:S(2)}, u32[]{:S(2)}) collective-permute-start(bf16[1,32,512]{2,1,0:T(8,128)(2,1)S(1)} %get-tuple-element.168), channel_id=1, source_target_pairs={{0,3},{1,0},{2,1},{3,2},{4,7},{5,4},{6,5},{7,6},{8,11},{9,8},{10,9... | collective-permute-start | bytes 98312 | tf_op jit(solution)/shard_map/ppermute | solution.py:761
  572.8 6.6 %collective-permute-start.55 = (bf16[32,512]{1,0:T(8,128)(2,1)S(1)}, bf16[32,512]{1,0:T(8,128)(2,1)S(1)}, u32[]{:S(2)}, u32[]{:S(2)}) collective-permute-start(bf16[32,512]{1,0:T(8,128)(2,1)S(1)} %bitcast.296), channel_id=1, source_target_pairs={{0,2},{1,3},{2,0},{3,1},{4,6},{5,7},{6,4},{7,5},{8,10},{9,11},{10,... | collective-permute-start | bytes 98312 | tf_op jit(solution)/shard_map/ppermute | solution.py:761
  588.6 10.2 %collective-permute-start.60 = (bf16[512,512]{1,0:T(8,128)(2,1)}, bf16[512,512]{1,0:T(8,128)(2,1)}, u32[]{:S(2)}, u32[]{:S(2)}) collective-permute-start(bf16[512,512]{1,0:T(8,128)(2,1)} %bitcast.94), channel_id=1, source_target_pairs={{0,4},{4,0},{8,12},{12,8},{16,20},{20,16},{24,28},{28,24},{1,5},{5... | collective-permute-start | bytes 1572872 | tf_op jit(solution)/shard_map/ppermute | solution.py:756
  589.8 8.2 %collective-permute-start.46 = (f32[8,128]{1,0:T(8,128)S(1)}, f32[8,128]{1,0:T(8,128)S(1)}, u32[]{:S(2)}, u32[]{:S(2)}) collective-permute-start(f32[8,128]{1,0:T(8,128)S(1)} %add_add_fusion.2), channel_id=1, source_target_pairs={{0,4},{4,0},{8,12},{12,8},{16,20},{20,16},{24,28},{28,24},{1,5},{5... | collective-permute-start | bytes 12296 | tf_op jit(solution)/shard_map/ppermute | solution.py:756
  589.8 27.5 %all-to-all-start.1 = ((bf16[16,64,512]{2,1,0:T(8,128)(2,1)}), bf16[16,64,512]{2,1,0:T(8,128)(2,1)S(1)}, u32[]{:S(2)}, u32[]{:S(2)}) async-start(bf16[16,64,512]{2,1,0:T(8,128)(2,1)} %get-tuple-element.114), calls=%async_computation.1 | async-start | bytes 2097152 | tf_op jit(solution)/shard_map/all_to_all | solution.py:1030
  (98 other events, 470.7 us)
Sparse Core Ops, SparseCore 0:
  32.5 122.0 all-gather.4
  158.1 113.0 all-gather.6
